TPU v7x, 32 devices: a whole 2x2x4 slice. The times are simulated.
32 devices in a mesh: scen: 8 (over z, x), row: 4 (over y, core).
Axes of the slice: x: 2, y: 2, z: 4, core: 2. Of those that a mesh axis runs over, the one named last changes fastest.
Arguments:
- border: bfloat16 [128, 8192, 128], P('scen', 'row'), may hold values from -0.119628906 to 0.119628906
- col_index: int32 [128, 128], P('scen'), may hold values from 0 to 4095
- barrier: float32 [4096], replicated, may hold values from 0.3 to 3
- counts: int32 [8], replicated, may hold values from 1 to 16, as said below
- inverse: bfloat16 [1024, 1024], replicated, may hold values from -0.140625 to 0.140625
- slab: float32 [8192, 4096], P('row', 'scen'), may hold values from -1.5 to 1.5
Outputs:
- updated: float32 [8192, 4096], P('row', 'scen')
Inputs may be any that keep to these rules, and one draw needn't show every extreme that they name: `counts`: the scenario groups whose index differs by a multiple of 4 from one drawn index hold 16 live blocks; every other group holds 1 to 4.
All inputs are finite; a program needn't handle non-finite values.
Results may differ from a plain program's by a relative error of at most 0.0064.
Values may be sent and summed in bfloat16 or wider, within the bound.
No kernel may reach another device: no remote copies, remote signals or barrier semaphores. Data moves between devices by JAX's collectives and lax.ppermute only.
A program may use at most 128 MiB of HBM per device.

v0:
```python
import jax
import jax.numpy as jnp
from jax import lax
from jax.sharding import PartitionSpec as P

blocks_per_product = 4


def broadcast(value, axis, source):
    kept = jnp.where(lax.axis_index(axis) == source, value, 0).astype(value.dtype)
    return lax.psum(kept, axis)


def body(border, col_index, barrier, counts, inverse, slab):
    row_count = lax.axis_size("row")
    my_scen = lax.axis_index("scen")
    slot_count, local_rows, block_width = border.shape
    panel_width = inverse.shape[0]
    share_width = panel_width // row_count
    weights = barrier[col_index]
    scaled = (border.astype(jnp.float32) * weights[:, None, :]).astype(jnp.bfloat16)
    own_count = counts[my_scen]
    held = scaled
    held_slots = held.shape[0]
    held_ids = jnp.arange(held_slots, dtype=jnp.int32)
    held = jnp.where((held_ids < own_count)[:, None, None], held, jnp.zeros_like(held))
    heads = held[:, :share_width, :]
    held_padded = held
    group_total = (own_count + blocks_per_product - 1) // blocks_per_product
    piece = lax.all_gather(heads, "row", axis=1, tiled=True)
    piece_width = piece.shape[1]

    def one_group(number, running):
        left_part = lax.dynamic_slice_in_dim(
            held_padded, number * blocks_per_product, blocks_per_product, 0
        )
        right_part = lax.dynamic_slice_in_dim(
            piece, number * blocks_per_product, blocks_per_product, 0
        )
        return running + jnp.einsum(
            "kib,kjb->ij", left_part, right_part, preferred_element_type=jnp.float32
        )

    block_sum = lax.fori_loop(
        0, group_total, one_group, jnp.zeros((local_rows, piece_width), jnp.float32)
    )
    share_sum = lax.psum_scatter(block_sum, "scen", scatter_dimension=0, tiled=True)
    share_round = share_sum.astype(jnp.bfloat16)
    share_done = jnp.dot(share_round, inverse, preferred_element_type=jnp.float32).astype(
        jnp.bfloat16
    )
    finished, rounded = (
        lax.all_gather(share_done, "scen", axis=0, tiled=True),
        lax.all_gather(share_round, "scen", axis=0, tiled=True),
    )
    trail_width = slab.shape[1]
    first_row = my_scen * trail_width
    source_row = first_row // local_rows
    wanted = lax.dynamic_slice_in_dim(rounded, first_row % local_rows, trail_width, 0)
    trailing = broadcast(wanted, "row", source_row)
    update = jnp.einsum("ip,jp->ij", finished, trailing, preferred_element_type=jnp.float32)
    return slab - update


def solution(mesh):
    return jax.shard_map(
        body,
        mesh=mesh,
        in_specs=(P("scen", "row", None), P("scen", None), P(), P(), P(), P("row", "scen")),
        out_specs=P("row", "scen"),
        check_vma=False,
    )
```

profile of v0, /device:TPU:0, one launch (start us, length us, event | category | flops | bytes accessed | tf_op | source)
XLA Modules:
  0.0 463.3 jit_solution(14226902357094130237)
XLA Ops:
  6.5 0.0 copy-start
  6.5 0.0 copy-start.1
  6.5 0.0 all-gather.4.cloned.1.call-start
  6.5 1.5 dynamic_slice.12
  8.0 0.7 iota_compare_fusion
  8.7 0.7 fusion.5
  9.4 0.0 copy-done.1
  9.4 11.8 %gather_fusion = f32[2048]{0:T(1024)S(1)} fusion(f32[4096]{0:T(1024)S(1)} %copy-done.1, s32[2048]{0:T(1024)S(1)} %fusion.5), kind=kCustom, calls=%fused_computation | custom fusion | bytes 24576 | tf_op jit(solution)/shard_map/gather | solution.py:20
  21.2 9.1 %fusion.3 = bf16[16,2048,128]{2,1,0:T(8,128)(2,1)} fusion(bf16[16,2048,128]{2,1,0:T(8,128)(2,1)} %param.8, f32[16,128]{1,0:T(8,128)S(1)} %bitcast.14, pred[16]{0:T(512)(128)(4,1)S(1)} %iota_compare_fusion), kind=kLoop, calls=%fused_computation.6 | loop fusion | flops 16777216 | bytes 16785424 | tf_op jit(solution)/shard_map/jit(_where)/select_n | solution.py:26
  30.2 2.3 slice.6
  32.5 0.0 all-gather.4.cloned.1.call-update
  32.6 0.0 reduce-scatter.2.cloned.1.call-start
  33.3 36.6 %all-gather.4.cloned.1.call-done = bf16[16,1024,128]{2,1,0:T(8,128)(2,1)} async-done(((bf16[16,256,128]{2,1,0:T(8,128)(2,1)}), bf16[16,1024,128]{2,1,0:T(8,128)(2,1)}) %all-gather.4.cloned.1.call-update) | async-done | bytes 4194320 | tf_op jit(solution)/shard_map/all_gather | solution.py:30
  69.9 4.3 broadcast_in_dim.23
  74.2 10.0 %while.10 = (s32[]{:T(128)}, f32[2048,1024]{1,0:T(8,128)}, s32[]{:T(128)}, bf16[16,2048,128]{2,1,0:T(8,128)(2,1)}, bf16[16,1024,128]{2,1,0:T(8,128)(2,1)}, /*index=5*/s32[]{:T(128)}, s32[]{:T(128)}, s32[]{:T(128)}, s32[]{:T(128)}) while((s32[]{:T(128)}, f32[2048,1024]{1,0:T(8,128)}, s32[]{:T(128)}, bf16[16,2048,128]{2,1,0:T(8,128)(2,1)}, ...), condition=%wide.region_1.2_spmd, body=%wide.region_0.1_spmd.sunk | while | flops 2149580800 | bytes 19924108 | solution.py:44
  74.2 10.0 %bitcast_add_fusion.2 = f32[2048,1024]{1,0:T(8,128)} fusion(f32[2048,1024]{1,0:T(8,128)} %get-tuple-element.86, bf16[16,2048,128]{2,1,0:T(8,128)(2,1)} %get-tuple-element.97, s32[]{:T(128)S(6)} %select_n.57, bf16[16,1024,128]{2,1,0:T(8,128)(2,1)} %get-tuple-element.98), kind=kOutput, calls=%fused_computation.1.clone.1 | convolution fusion | flops 2149580800 | bytes 19923968 | tf_op jit(solution)/shard_map/while/body/kib,kjb->ij/dot_general | solution.py:40
  84.2 0.0 reduce-scatter.2.cloned.1.call-update
  84.2 0.0 all-gather.8.cloned.1.call-start
  84.2 179.0 %reduce-scatter.2.cloned.1.call-done = f32[256,1024]{1,0:T(8,128)} async-done(((f32[2048,1024]{1,0:T(8,128)}), f32[256,1024]{1,0:T(8,128)}) %reduce-scatter.2.cloned.1.call-update) | async-done | bytes 1048592 | tf_op jit(solution)/shard_map/reduce_scatter | solution.py:47
  263.2 2.1 convert_element_type.16
  265.3 0.0 all-gather.8.cloned.1.call-update
  265.3 0.0 all-gather.6.cloned.1.call-start
  265.4 0.0 copy-done
  265.4 2.6 convolution_convert_fusion
  268.0 0.0 all-gather.6.cloned.1.call-update
  268.0 0.0 all-reduce.2.cloned.1.call-start
  268.1 69.9 %all-gather.8.cloned.1.call-done = bf16[2048,1024]{1,0:T(8,128)(2,1)} async-done(((bf16[256,1024]{1,0:T(8,128)(2,1)}), bf16[2048,1024]{1,0:T(8,128)(2,1)}) %all-gather.8.cloned.1.call-update) | async-done | bytes 4194320 | tf_op jit(solution)/shard_map/all_gather | solution.py:54
  338.0 2.4 dynamic-slice_select_fusion
  340.4 0.0 all-reduce.2.cloned.1.call-update
  340.4 71.5 %all-gather.6.cloned.1.call-done = bf16[2048,1024]{1,0:T(8,128)(2,1)} async-done(((bf16[256,1024]{1,0:T(8,128)(2,1)}), bf16[2048,1024]{1,0:T(8,128)(2,1)}) %all-gather.6.cloned.1.call-update) | async-done | bytes 4194320 | tf_op jit(solution)/shard_map/all_gather | solution.py:53
  411.9 36.7 %all-reduce.2.cloned.1.call-done = bf16[512,1024]{1,0:T(8,128)(2,1)} async-done(((bf16[512,1024]{1,0:T(8,128)(2,1)}), bf16[512,1024]{1,0:T(8,128)(2,1)}) %all-reduce.2.cloned.1.call-update) | async-done | bytes 1048592 | tf_op jit(solution)/shard_map/psum | solution.py:11
  448.6 8.2 %convolution_subtract_fusion = f32[2048,512]{1,0:T(8,128)} fusion(f32[2048,512]{1,0:T(8,128)} %param.13, bf16[2048,1024]{1,0:T(8,128)(2,1)} %all-gather.6.cloned.1.call-done, bf16[512,1024]{1,0:T(8,128)(2,1)} %all-reduce.2.cloned.1.call-done), kind=kOutput, calls=%fused_computation.7 | convolution fusion | flops 2148532224 | bytes 13631488 | tf_op jit(solution)/shard_map/ip,jp->ij/dot_general | solution.py:61
Async XLA Ops:
  6.5 258.9 %copy-start = (bf16[1024,1024]{1,0:T(8,128)(2,1)S(1)}, bf16[1024,1024]{1,0:T(8,128)(2,1)}, u32[]{:S(2)}) copy-start(bf16[1024,1024]{1,0:T(8,128)(2,1)} %param.12) | copy-start | bytes 6291460
  6.5 2.9 copy-start.1
  6.5 63.4 %all-gather.4.cloned.1.call-start = ((), (), s32[]{:S(2)}) async-start(), calls=%async_computation.1 | async-start | bytes 5242880 | tf_op jit(solution)/shard_map/all_gather | solution.py:30
  32.6 230.7 %reduce-scatter.2.cloned.1.call-start = ((), (), s32[]{:S(2)}) async-start(), calls=%async_computation.2 | async-start | bytes 9437184 | tf_op jit(solution)/shard_map/reduce_scatter | solution.py:47
  84.2 253.8 %all-gather.8.cloned.1.call-start = ((), (), s32[]{:S(2)}) async-start(), calls=%async_computation.4 | async-start | bytes 4718592 | tf_op jit(solution)/shard_map/all_gather | solution.py:54
  265.3 146.5 %all-gather.6.cloned.1.call-start = ((), (), s32[]{:S(2)}) async-start(), calls=%async_computation.3 | async-start | bytes 4718592 | tf_op jit(solution)/shard_map/all_gather | solution.py:53
  268.0 180.6 %all-reduce.2.cloned.1.call-start = ((), (), s32[]{:S(2)}) async-start(), calls=%async_computation.5 | async-start | bytes 2097152 | tf_op jit(solution)/shard_map/psum | solution.py:11
Sparse Core Ops, SparseCore 0:
  32.7 37.1 all-gather.3
  84.3 178.8 reduce-scatter.1
  265.6 72.3 all-gather.7
  340.2 71.6 all-gather.5
  414.2 34.3 all-reduce.1
where the time goes:
time: 464 us; the launch traced here: 463 us
  waiting for transfers between devices  394 us (85%)
  matrix products  20.7 us (4%)
  local copies, waits for them, and re-layouts  19.8 us (4%)
  other arithmetic  14.9 us (3%)
  between operations  13.9 us (3%)
    reduce_scatter x1, waiting for transfers between devices, body(): lax.psum_scatter(block_sum, 'scen', scatter_dimension=0, tiled=True)  179 us
    all_gather x1, waiting for transfers between devices, body(): lax.all_gather(share_done, 'scen', axis=0, tiled=True)  71.5 us
    all_gather x1, waiting for transfers between devices, body(): lax.all_gather(share_round, 'scen', axis=0, tiled=True)  69.9 us
    psum x1, waiting for transfers between devices, broadcast(): return lax.psum(kept, axis)  36.7 us
    all_gather x1, waiting for transfers between devices, body(): piece = lax.all_gather(heads, 'row', axis=1, tiled=True)  36.6 us
    gather x1, local copies, waits for them, and re-layouts, body(): weights = barrier[col_index]  11.8 us
    dot_general x1, matrix products, one_group(): jnp.einsum('kib,kjb->ij', left_part, right_part, preferred_element_type=j...  9.96 us
  transfers between devices with their start and end apart: 5, of which 5 were waited for; matrix products, arithmetic and copies ran while one was open for 1% of the time, Pallas kernels for 0%

commit v1 on v0

v1 whole, which is shorter than its diff:
```python
import functools

import jax
import jax.numpy as jnp
from jax import lax
from jax.experimental import pallas as pl
from jax.experimental.pallas import tpu as pltpu
from jax.sharding import PartitionSpec as P

f32, bf16 = jnp.float32, jnp.bfloat16
LANES = 128


def nt_dot(a, b):
    return lax.dot_general(a, b, (((1,), (1,)), ((), ())), preferred_element_type=f32)


def weights_kernel(place_ref, counts_ref, index_ref, table_ref, out_ref):
    index = index_ref[...]
    high, low = index // LANES, index % LANES
    total = jnp.zeros(index.shape, f32)
    for row in range(table_ref.shape[0]):
        entries = jnp.broadcast_to(table_ref[row : row + 1, :], index.shape)
        picked = jnp.take_along_axis(entries, low, axis=1, mode="promise_in_bounds")
        total = jnp.where(high == row, picked, total)
    live = lax.broadcasted_iota(jnp.int32, index.shape, 0) < counts_ref[place_ref[0]]
    out_ref[...] = jnp.where(live, total, 0.0)


def live_weights(place, counts, col_index, barrier):
    smem = pl.BlockSpec(memory_space=pltpu.SMEM)
    vmem = pl.BlockSpec(memory_space=pltpu.VMEM)
    return pl.pallas_call(
        weights_kernel,
        out_shape=jax.ShapeDtypeStruct(col_index.shape, f32),
        in_specs=[smem, smem, vmem, vmem],
        out_specs=vmem,
        name="live_weights",
    )(place, counts, col_index, barrier.reshape(-1, LANES))


def scaled_flat(blocks, weights):
    parts = [
        (blocks[k].astype(f32) * weights[k : k + 1, :]).astype(bf16) for k in range(blocks.shape[0])
    ]
    return jnp.concatenate(parts, axis=1)


def partial_kernel(order_ref, border_ref, heads_ref, weights_ref, *rest):
    outs, scaled_heads = rest[:-1], rest[-1]

    @pl.when(pl.program_id(0) == 0)
    def _():
        scaled_heads[...] = scaled_flat(heads_ref, weights_ref[...])

    value = nt_dot(scaled_flat(border_ref, weights_ref[...]), scaled_heads[...])
    for out in outs:
        out[...] = value.astype(out.dtype)


def partial_panel(order, position, border, heads, head_rows, weights, kinds):
    slots, rows, width = border.shape
    quarter = rows // 4
    steps = 2 if quarter % 512 == 0 else 1
    tile = quarter // steps
    return pl.pallas_call(
        partial_kernel,
        grid_spec=pltpu.PrefetchScalarGridSpec(
            num_scalar_prefetch=1,
            grid=(steps,),
            in_specs=[
                pl.BlockSpec((slots, tile, width), lambda i, o: (0, o[position] * steps + i, 0)),
                pl.BlockSpec((slots, head_rows, width), lambda i, o: (0, 0, 0)),
                pl.BlockSpec((slots, width), lambda i, o: (0, 0)),
            ],
            out_specs=[pl.BlockSpec((tile, head_rows), lambda i, o: (i, 0)) for _ in kinds],
            scratch_shapes=[pltpu.VMEM((head_rows, slots * width), bf16)],
        ),
        out_shape=[jax.ShapeDtypeStruct((quarter, head_rows), kind) for kind in kinds],
        compiler_params=pltpu.CompilerParams(vmem_limit_bytes=24 << 20),
        cost_estimate=pl.CostEstimate(
            flops=2 * quarter * head_rows * slots * width,
            bytes_accessed=2 * slots * (quarter + head_rows) * width,
            transcendentals=0,
        ),
        name="partial_panel",
    )(order, border, heads, weights)


def update_kernel(n, order_ref, inverse_ref, slab_ref, *rest):
    trailing, pieces, out_ref, w_ref = rest[:n], rest[n : 5 * n], rest[-2], rest[-1]
    position = pl.program_id(0)
    ends = [0]
    for t in trailing:
        ends.append(ends[-1] + t.shape[1])

    @pl.when(position == 0)
    def _():
        total = None
        for j in range(n):
            part = nt_dot(inverse_ref[:, ends[j] : ends[j + 1]], trailing[j][...])
            total = part if total is None else total + part
        w_ref[...] = total.astype(bf16)

    for p in range(4):

        @pl.when(position == p)
        def _(p=p):
            total = slab_ref[...]
            for j in range(n):
                total -= jnp.dot(
                    pieces[j * 4 + p][...],
                    w_ref[ends[j] : ends[j + 1], :],
                    preferred_element_type=f32,
                )
            out_ref[...] = total


def update(order, inverse, slab, trailing, pieces):
    rows, columns = slab.shape
    quarter = rows // 4
    n = len(trailing)
    flat = [piece for chunk in pieces for piece in chunk]
    whole = lambda a: pl.BlockSpec(a.shape, lambda i, o: (0, 0))
    block = pl.BlockSpec((quarter, columns), lambda i, o: (o[i], 0))
    return pl.pallas_call(
        functools.partial(update_kernel, n),
        grid_spec=pltpu.PrefetchScalarGridSpec(
            num_scalar_prefetch=1,
            grid=(4,),
            in_specs=[whole(inverse), block] + [whole(a) for a in trailing + flat],
            out_specs=block,
            scratch_shapes=[pltpu.VMEM((inverse.shape[0], columns), bf16)],
        ),
        out_shape=jax.ShapeDtypeStruct(slab.shape, slab.dtype),
        compiler_params=pltpu.CompilerParams(vmem_limit_bytes=40 << 20),
        name="update",
    )(order, inverse, slab, *trailing, *flat)


def body(border, col_index, barrier, counts, inverse, slab):
    scen_count, row_count = lax.axis_size("scen"), lax.axis_size("row")
    s, r = lax.axis_index("scen"), lax.axis_index("row")
    slots, local_rows, width = border.shape
    panel_width = inverse.shape[0]
    share = panel_width // row_count
    quarter = local_rows // 4
    trail = slab.shape[1]
    line = scen_count // 2
    half = line // 2
    x, z = s % 2, s // 2
    side = (z >= half).astype(jnp.int32)
    order = jnp.stack([x, 1 - x, 2 + side, 3 - side]).astype(jnp.int32)

    swap_x = [(i, i ^ 1) for i in range(scen_count)]
    at = lambda place, lane: place * 2 + lane

    def both_ends(a, b):
        pairs = []
        for lane in range(2):
            pairs += [(at(a, lane), at(b, lane)), (at(line - 1 - a, lane), at(line - 1 - b, lane))]
        return pairs

    inward = [both_ends(t, t + 1) for t in range(half - 1)]
    outward = [both_ends(t + 1, t) for t in reversed(range(half - 1))]
    middle = both_ends(half - 1, half)
    inner_x = [(i, i ^ 1) for i in (at(a, lane) for a in (half - 1, half) for lane in range(2))]
    spread_to = [(z == t) | (z == line - 1 - t) for t in reversed(range(half - 1))]
    over_scen = lambda value, pairs: lax.ppermute(value.astype(bf16), "scen", pairs)
    over_row = lambda value, mask: lax.ppermute(
        value, "row", [(i, i ^ mask) for i in range(row_count)]
    )

    own = border[:, :share, :]
    sibling = over_row(own, 1)
    far = [over_row(own, mask) for mask in range(2, row_count, 2)]
    far_sibling = [over_row(value, 1) for value in far]
    heads = [(border, share), (sibling, share)]
    if far:
        for group in (far, far_sibling):
            joined = group[0] if len(group) == 1 else jnp.concatenate(group, axis=1)
            heads.append((joined, joined.shape[1]))
    n = len(heads)

    def share_order(device):
        masks = [0, 1] + list(range(2, row_count, 2)) + list(range(3, row_count, 2))
        return [device ^ mask for mask in masks]

    first_row = s * trail
    source = first_row // local_rows

    def take(value, shares, axis):
        return jnp.concatenate(
            [lax.dynamic_slice_in_dim(value, k * share, share, axis) for k in shares], axis
        )

    inverse_here = take(take(inverse, share_order(r), 0), share_order(source), 1)
    weights = live_weights(s.astype(jnp.int32).reshape(1), counts, col_index, barrier)

    kinds = ([f32], [bf16], [f32, bf16], [f32, bf16])
    pieces, trailing = [], []
    unit = min(trail, quarter)

    for values, head_rows in heads:
        (send,) = partial_panel(order, 1, border, values, head_rows, weights, kinds[1])
        got = over_scen(send, swap_x)
        keep2, send2 = partial_panel(order, 2, border, values, head_rows, weights, kinds[2])
        keep3, send3 = partial_panel(order, 3, border, values, head_rows, weights, kinds[3])
        (keep,) = partial_panel(order, 0, border, values, head_rows, weights, kinds[0])
        total = keep + got.astype(f32)
        for pairs in inward:
            total = total + over_scen(total, pairs).astype(f32)
        total = total + over_scen(total, middle).astype(f32)
        final = total.astype(bf16)
        for pairs, mine in zip(outward, spread_to):
            final = jnp.where(mine, over_scen(final, pairs), final)
        other = over_scen(final, swap_x)
        for step, pairs in enumerate(inward):
            got2, got3 = over_scen(send2, pairs), over_scen(send3, pairs)
            keep2, keep3 = keep2 + got2.astype(f32), keep3 + got3.astype(f32)
            send2, send3 = keep2.astype(bf16), keep3.astype(bf16)
        keep2 = keep2 + over_scen(send3, middle).astype(f32)
        keep2 = keep2 + over_scen(keep2, inner_x).astype(f32)
        final2 = keep2.astype(bf16)
        final3 = over_scen(final2, middle)
        for pairs, mine in zip(outward, spread_to):
            got2, got3 = over_scen(final2, pairs), over_scen(final3, pairs)
            final2, final3 = jnp.where(mine, got2, final2), jnp.where(mine, got3, final3)
        chunk = [final, other, final2, final3]
        pieces.append(chunk)

        joined = jnp.concatenate(chunk, axis=0)
        parts = []
        for k in range(trail // unit):
            start = first_row % local_rows + k * unit
            place = start // quarter
            position = jnp.argmax(order == place).astype(jnp.int32)
            parts.append(
                lax.dynamic_slice_in_dim(joined, position * quarter + start % quarter, unit, 0)
            )
        rows = parts[0] if len(parts) == 1 else jnp.concatenate(parts, axis=0)
        rows = jnp.where(source == r, rows, jnp.zeros_like(rows))
        masks = []
        mask = row_count // 2
        while mask:
            masks.append(mask)
            mask //= 2
        reached = {g: {g * trail // local_rows} for g in range(scen_count)}
        for mask in masks:
            pairs = [
                (g * row_count + k, g * row_count + (k ^ mask))
                for g in range(scen_count)
                for k in sorted(reached[g])
            ]
            rows = rows + lax.ppermute(rows, ("scen", "row"), pairs)
            for g in range(scen_count):
                reached[g] |= {k ^ mask for k in reached[g]}
        trailing.append(rows)

    return update(order, inverse_here, slab, trailing, pieces)


def solution(mesh):
    return jax.shard_map(
        body,
        mesh=mesh,
        in_specs=(P("scen", "row", None), P("scen", None), P(), P(), P(), P("row", "scen")),
        out_specs=P("row", "scen"),
        check_vma=False,
    )
```

time: 464 us -> 242 us (0.52)
  waiting for transfers between devices: 394 us -> 75.6 us
  starting transfers between devices: 0.17 us -> 84.7 us
  Pallas kernels: 0 us -> 38.6 us
  matrix products: 20.7 us -> 0 us
  between operations: 13.9 us -> 1.63 us
  other arithmetic: 14.9 us -> 26.4 us
  local copies, waits for them, and re-layouts: 19.8 us -> 13.2 us
    reduce_scatter x1 -> x0, waiting for transfers between devices: 179 us -> none  [body(): lax.psum_scatter(block_sum, 'scen', scatter_dimension=0, tiled=True)]
    all_gather x3 -> x0, waiting for transfers between devices: 178 us -> none  [the longest x1 71.5 us: body(): lax.all_gather(share_done, 'scen', axis=0, tiled=True)]
    ppermute x0 -> x59, starting transfers between devices: none -> 84.7 us  [the longest x48 66.6 us: body(): lax.ppermute(value.astype(bf16), 'scen', pairs)]
    ppermute x0 -> x59, waiting for transfers between devices: none -> 75.6 us  [the longest x48 75.4 us: body(): lax.ppermute(value.astype(bf16), 'scen', pairs)]
    pallas_call x0 -> x18, Pallas kernels: none -> 38.6 us  [the longest x16 31.2 us: partial_panel(): pl.pallas_call(partial_kernel, grid_spec=pltpu.PrefetchScalarGridSpec(num...]
    psum x1 -> x0, waiting for transfers between devices: 36.7 us -> none  [broadcast(): return lax.psum(kept, axis)]
    dot_general x3 -> x0, matrix products: 20.7 us -> none  [the longest x1 9.96 us: one_group(): jnp.einsum('kib,kjb->ij', left_part, right_part, preferred_element_type=j...]
    gather x1 -> x0, local copies, waits for them, and re-layouts: 11.8 us -> none  [body(): weights = barrier[col_index]]
  transfers between devices with their start and end apart: 5 -> 59, of which waited for: 5 -> 16; matrix products, arithmetic and copies ran while one was open for 1% -> 12% of each run, Pallas kernels for 0% -> 12%
where the time goes in v1:
time: 242 us; the launch traced here: 240 us
  starting transfers between devices  84.7 us (35%)
  waiting for transfers between devices  75.6 us (31%)
  Pallas kernels  38.6 us (16%)
  other arithmetic  26.4 us (11%)
  local copies, waits for them, and re-layouts  13.2 us (5%)
    ppermute x48, waiting for transfers between devices, body(): lax.ppermute(value.astype(bf16), 'scen', pairs)  75.4 us
    ppermute x48, starting transfers between devices, body(): lax.ppermute(value.astype(bf16), 'scen', pairs)  66.6 us
    pallas_call x16, Pallas kernels, partial_panel(): pl.pallas_call(partial_kernel, grid_spec=pltpu.PrefetchScalarGridSpec(num...  31.2 us
    ppermute x8, starting transfers between devices, body(): rows = rows + lax.ppermute(rows, ('scen', 'row'), pairs)  16.5 us
    unnamed x28, local copies, waits for them, and re-layouts  10.5 us
    select_n x4, other arithmetic, body(): rows = jnp.where(source == r, rows, jnp.zeros_like(rows))  8.98 us
    pallas_call x1, Pallas kernels, update(): pl.pallas_call(functools.partial(update_kernel, n), grid_spec=pltpu.Prefe...  5.94 us
  transfers between devices with their start and end apart: 59, of which 16 were waited for; matrix products, arithmetic and copies ran while one was open for 12% of the time, Pallas kernels for 12%

profile of v1, /device:TPU:0, one launch (start us, length us, event | category | flops | bytes accessed | tf_op | source)
XLA Modules:
  0.0 240.1 jit_solution(7112782615312812462)
XLA Ops:
  1.6 3.4 %copy-done = bf16[16,2048,128]{2,1,0:T(8,128)(2,1)S(1)} copy-done((bf16[16,2048,128]{2,1,0:T(8,128)(2,1)S(1)}, bf16[16,2048,128]{2,1,0:T(8,128)(2,1)}, u32[]{:S(2)}) %copy-start) | copy-done | bytes 8388632
  7.6 3.0 %collective-permute-start = (bf16[512,256]{1,0:T(8,128)(2,1)S(1)}, bf16[512,256]{1,0:T(8,128)(2,1)S(1)}, u32[]{:S(2)}, u32[]{:S(2)}) collective-permute-start(bf16[512,256]{1,0:T(8,128)(2,1)S(1)} %partial_panel.17), channel_id=1, source_target_pairs={{0,4},{4,0},{8,12},{12,8},{16,20},{20,16},{24,28},{28,24},{1,5},{5... | collective-permute-start | bytes 786440 | tf_op jit(solution)/shard_map/ppermute | solution.py:169
  13.2 2.6 %partial_panel.19 = (f32[512,256]{1,0:T(8,128)S(1)}, bf16[512,256]{1,0:T(8,128)(2,1)}) custom-call(s32[4]{0:T(128)S(1)} %pad_add_fusion.order_ref, bf16[16,2048,128]{2,1,0:T(8,128)(2,1)S(1)} %copy-done, bf16[16,2048,128]{2,1,0:T(8,128)(2,1)S(1)} %copy-done, f32[16,128]{1,0:T(8,128)S(1)} %copy-done.3), custom_call_target="tpu_custom_call" | custom-call | flops 536870912 | bytes 3145728 | tf_op jit(solution)/shard_map/partial_panel/pallas_call | solution.py:66
  16.6 4.2 %collective-permute-start.6 = (bf16[512,256]{1,0:T(8,128)(2,1)}, bf16[512,256]{1,0:T(8,128)(2,1)}, u32[]{:S(2)}, u32[]{:S(2)}) collective-permute-start(bf16[512,256]{1,0:T(8,128)(2,1)} %get-tuple-element.25), channel_id=1, source_target_pairs={{0,8},{24,16},{4,12},{28,20},{1,9},{25,17},{5,13},{29,21},{2,10},{... | collective-permute-start | bytes 786440 | tf_op jit(solution)/shard_map/ppermute | solution.py:169
  20.8 2.0 partial_panel.16
  23.6 2.0 collective-permute-start.1
  25.6 2.0 partial_panel.18
  27.6 2.0 collective-permute-start.5
  45.3 8.9 %collective-permute-done.3 = bf16[512,256]{1,0:T(8,128)(2,1)S(1)} collective-permute-done((bf16[512,256]{1,0:T(8,128)(2,1)S(1)}, bf16[512,256]{1,0:T(8,128)(2,1)S(1)}, u32[]{:S(2)}, u32[]{:S(2)}) %collective-permute-start.3) | collective-permute-done | bytes 262176 | tf_op jit(solution)/shard_map/ppermute | solution.py:169
  54.8 3.4 %copy-done.1 = bf16[16,2048,128]{2,1,0:T(8,128)(2,1)S(1)} copy-done((bf16[16,2048,128]{2,1,0:T(8,128)(2,1)S(1)}, bf16[16,2048,128]{2,1,0:T(8,128)(2,1)}, u32[]{:S(2)}) %copy-start.1) | copy-done | bytes 8388632
  67.4 5.0 %collective-permute-start.36 = (bf16[512,256]{1,0:T(8,128)(2,1)S(1)}, bf16[512,256]{1,0:T(8,128)(2,1)S(1)}, u32[]{:S(2)}, u32[]{:S(2)}) collective-permute-start(bf16[512,256]{1,0:T(8,128)(2,1)S(1)} %get-tuple-element.34), channel_id=1, source_target_pairs={{0,8},{24,16},{4,12},{28,20},{1,9},{25,17},{5,13},{29,21},{2,10},{... | collective-permute-start | bytes 786440 | tf_op jit(solution)/shard_map/ppermute | solution.py:169
  84.8 3.1 %collective-permute-done.15 = bf16[512,256]{1,0:T(8,128)(2,1)S(1)} collective-permute-done((bf16[512,256]{1,0:T(8,128)(2,1)S(1)}, bf16[512,256]{1,0:T(8,128)(2,1)S(1)}, u32[]{:S(2)}, u32[]{:S(2)}) %collective-permute-start.15) | collective-permute-done | bytes 262176 | tf_op jit(solution)/shard_map/ppermute | solution.py:169
  89.2 2.4 %collective-permute-done.21 = bf16[512,256]{1,0:T(8,128)(2,1)S(1)} collective-permute-done((bf16[512,256]{1,0:T(8,128)(2,1)S(1)}, bf16[512,256]{1,0:T(8,128)(2,1)S(1)}, u32[]{:S(2)}, u32[]{:S(2)}) %collective-permute-start.21) | collective-permute-done | bytes 262176 | tf_op jit(solution)/shard_map/ppermute | solution.py:169
  91.7 4.4 %collective-permute-done.11 = bf16[512,256]{1,0:T(8,128)(2,1)S(1)} collective-permute-done((bf16[512,256]{1,0:T(8,128)(2,1)S(1)}, bf16[512,256]{1,0:T(8,128)(2,1)S(1)}, u32[]{:S(2)}, u32[]{:S(2)}) %collective-permute-start.11) | collective-permute-done | bytes 262176 | tf_op jit(solution)/shard_map/ppermute | solution.py:169
  98.4 2.2 fusion.19
  102.3 4.4 %collective-permute-start.16 = (bf16[512,256]{1,0:T(8,128)(2,1)S(1)}, bf16[512,256]{1,0:T(8,128)(2,1)S(1)}, u32[]{:S(2)}, u32[]{:S(2)}) collective-permute-start(bf16[512,256]{1,0:T(8,128)(2,1)S(1)} %fusion.1), channel_id=1, source_target_pairs={{0,8},{24,16},{4,12},{28,20},{1,9},{25,17},{5,13},{29,21},{2,10},{... | collective-permute-start | bytes 786440 | tf_op jit(solution)/shard_map/ppermute | solution.py:169
  106.8 3.1 %collective-permute-start.12 = (bf16[512,256]{1,0:T(8,128)(2,1)}, bf16[512,256]{1,0:T(8,128)(2,1)}, u32[]{:S(2)}, u32[]{:S(2)}) collective-permute-start(bf16[512,256]{1,0:T(8,128)(2,1)} %fusion.19), channel_id=1, source_target_pairs={{0,2},{4,6},{8,10},{12,14},{17,19},{21,23},{25,27},{29,31}} | collective-permute-start | bytes 786440 | tf_op jit(solution)/shard_map/ppermute | solution.py:255
  121.9 20.1 %collective-permute-done.33 = bf16[512,256]{1,0:T(8,128)(2,1)S(1)} collective-permute-done((bf16[512,256]{1,0:T(8,128)(2,1)S(1)}, bf16[512,256]{1,0:T(8,128)(2,1)S(1)}, u32[]{:S(2)}, u32[]{:S(2)}) %collective-permute-start.33) | collective-permute-done | bytes 262176 | tf_op jit(solution)/shard_map/ppermute | solution.py:169
  146.6 6.5 %collective-permute-done.18 = bf16[512,256]{1,0:T(8,128)(2,1)S(1)} collective-permute-done((bf16[512,256]{1,0:T(8,128)(2,1)S(1)}, bf16[512,256]{1,0:T(8,128)(2,1)S(1)}, u32[]{:S(2)}, u32[]{:S(2)}) %collective-permute-start.18) | collective-permute-done | bytes 262176 | tf_op jit(solution)/shard_map/ppermute | solution.py:169
  160.8 2.3 collective-permute-done.51
  163.1 4.4 %collective-permute-start.46 = (bf16[512,256]{1,0:T(8,128)(2,1)S(1)}, bf16[512,256]{1,0:T(8,128)(2,1)S(1)}, u32[]{:S(2)}, u32[]{:S(2)}) collective-permute-start(bf16[512,256]{1,0:T(8,128)(2,1)S(1)} %fusion.3), channel_id=1, source_target_pairs={{0,8},{24,16},{4,12},{28,20},{1,9},{25,17},{5,13},{29,21},{2,10},{... | collective-permute-start | bytes 786440 | tf_op jit(solution)/shard_map/ppermute | solution.py:169
  169.2 2.1 collective-permute-done.46
  172.8 2.2 fusion.11
  176.6 3.1 %collective-permute-start.42 = (bf16[512,256]{1,0:T(8,128)(2,1)}, bf16[512,256]{1,0:T(8,128)(2,1)}, u32[]{:S(2)}, u32[]{:S(2)}) collective-permute-start(bf16[512,256]{1,0:T(8,128)(2,1)} %fusion.11), channel_id=1, source_target_pairs={{0,2},{4,6},{8,10},{12,14},{17,19},{21,23},{25,27},{29,31}} | collective-permute-start | bytes 786440 | tf_op jit(solution)/shard_map/ppermute | solution.py:255
  182.2 8.1 %collective-permute-done.26 = bf16[512,256]{1,0:T(8,128)(2,1)S(1)} collective-permute-done((bf16[512,256]{1,0:T(8,128)(2,1)S(1)}, bf16[512,256]{1,0:T(8,128)(2,1)S(1)}, u32[]{:S(2)}, u32[]{:S(2)}) %collective-permute-start.26) | collective-permute-done | bytes 262176 | tf_op jit(solution)/shard_map/ppermute | solution.py:169
  192.3 2.3 fusion.15
  194.6 7.8 %collective-permute-done.48 = bf16[512,256]{1,0:T(8,128)(2,1)S(1)} collective-permute-done((bf16[512,256]{1,0:T(8,128)(2,1)S(1)}, bf16[512,256]{1,0:T(8,128)(2,1)S(1)}, u32[]{:S(2)}, u32[]{:S(2)}) %collective-permute-start.48) | collective-permute-done | bytes 262176 | tf_op jit(solution)/shard_map/ppermute | solution.py:169
  202.4 3.1 %collective-permute-start.27 = (bf16[512,256]{1,0:T(8,128)(2,1)}, bf16[512,256]{1,0:T(8,128)(2,1)}, u32[]{:S(2)}, u32[]{:S(2)}) collective-permute-start(bf16[512,256]{1,0:T(8,128)(2,1)} %fusion.15), channel_id=1, source_target_pairs={{0,2},{4,6},{8,10},{12,14},{17,19},{21,23},{25,27},{29,31}} | collective-permute-start | bytes 786440 | tf_op jit(solution)/shard_map/ppermute | solution.py:255
  207.2 6.6 %collective-permute-done.56 = bf16[512,256]{1,0:T(8,128)(2,1)S(1)} collective-permute-done((bf16[512,256]{1,0:T(8,128)(2,1)S(1)}, bf16[512,256]{1,0:T(8,128)(2,1)S(1)}, u32[]{:S(2)}, u32[]{:S(2)}) %collective-permute-start.56) | collective-permute-done | bytes 262176 | tf_op jit(solution)/shard_map/ppermute | solution.py:169
  213.8 2.2 fusion.7
  216.8 2.0 collective-permute-start.57
  234.2 5.9 %update.1 = f32[2048,512]{1,0:T(8,128)} custom-call(s32[4]{0:T(128)S(1)} %pad_add_fusion.order_ref, bf16[1024,1024]{1,0:T(8,128)(2,1)S(1)} %pad_maximum_fusion.1.inverse_ref, f32[2048,512]{1,0:T(8,128)S(1)} %copy-done.2, bf16[512,256]{1,0:T(8,128)(2,1)S(1)} %add.188.rest_0_, bf16[512,256]{1,0:T(8,128)(2,1)S(1)} %add.197.rest_1_, ...), custom_call_target="tpu_custom_call" | custom-call | tf_op jit(solution)/shard_map/update/pallas_call | solution.py:126
  (187 shorter events, 101.7 us)
Async XLA Ops:
  7.6 15.2 %collective-permute-start = (bf16[512,256]{1,0:T(8,128)(2,1)S(1)}, bf16[512,256]{1,0:T(8,128)(2,1)S(1)}, u32[]{:S(2)}, u32[]{:S(2)}) collective-permute-start(bf16[512,256]{1,0:T(8,128)(2,1)S(1)} %partial_panel.17), channel_id=1, source_target_pairs={{0,4},{4,0},{8,12},{12,8},{16,20},{20,16},{24,28},{28,24},{1,5},{5... | collective-permute-start | bytes 786440 | tf_op jit(solution)/shard_map/ppermute | solution.py:169
  11.7 43.1 %collective-permute-start.29 = (bf16[16,256,128]{2,1,0:T(8,128)(2,1)}, bf16[16,256,128]{2,1,0:T(8,128)(2,1)S(1)}, u32[]{:S(2)}, u32[]{:S(2)}) collective-permute-start(bf16[16,256,128]{2,1,0:T(8,128)(2,1)} %slice.3), channel_id=1, source_target_pairs={{0,2},{1,3},{2,0},{3,1},{4,6},{5,7},{6,4},{7,5},{8,10},{9,11},{10,... | collective-permute-start | bytes 3145736 | tf_op jit(solution)/shard_map/ppermute | solution.py:170
  13.2 54.2 %collective-permute-start.14 = (bf16[16,256,128]{2,1,0:T(8,128)(2,1)}, bf16[16,256,128]{2,1,0:T(8,128)(2,1)S(1)}, u32[]{:S(2)}, u32[]{:S(2)}) collective-permute-start(bf16[16,256,128]{2,1,0:T(8,128)(2,1)} %slice.3), channel_id=1, source_target_pairs={{0,1},{1,0},{2,3},{3,2},{4,5},{5,4},{6,7},{7,6},{8,9},{9,8},{10,11... | collective-permute-start | bytes 3145736 | tf_op jit(solution)/shard_map/ppermute | solution.py:170
  16.6 13.0 %collective-permute-start.6 = (bf16[512,256]{1,0:T(8,128)(2,1)}, bf16[512,256]{1,0:T(8,128)(2,1)}, u32[]{:S(2)}, u32[]{:S(2)}) collective-permute-start(bf16[512,256]{1,0:T(8,128)(2,1)} %get-tuple-element.25), channel_id=1, source_target_pairs={{0,8},{24,16},{4,12},{28,20},{1,9},{25,17},{5,13},{29,21},{2,10},{... | collective-permute-start | bytes 786440 | tf_op jit(solution)/shard_map/ppermute | solution.py:169
  27.6 10.2 %collective-permute-start.5 = (bf16[512,256]{1,0:T(8,128)(2,1)S(1)}, bf16[512,256]{1,0:T(8,128)(2,1)}, u32[]{:S(2)}, u32[]{:S(2)}) collective-permute-start(bf16[512,256]{1,0:T(8,128)(2,1)S(1)} %get-tuple-element.23), channel_id=1, source_target_pairs={{0,8},{24,16},{4,12},{28,20},{1,9},{25,17},{5,13},{29,21},{2,10},{... | collective-permute-start | bytes 786440 | tf_op jit(solution)/shard_map/ppermute | solution.py:169
  40.8 13.4 %collective-permute-start.3 = (bf16[512,256]{1,0:T(8,128)(2,1)S(1)}, bf16[512,256]{1,0:T(8,128)(2,1)S(1)}, u32[]{:S(2)}, u32[]{:S(2)}) collective-permute-start(bf16[512,256]{1,0:T(8,128)(2,1)S(1)} %add_convert_fusion.11), channel_id=1, source_target_pairs={{8,0},{16,24},{12,4},{20,28},{9,1},{17,25},{13,5},{21,29},{10,2},{... | collective-permute-start | bytes 786440 | tf_op jit(solution)/shard_map/ppermute | solution.py:169
  43.3 40.1 %collective-permute-start.10 = (bf16[512,256]{1,0:T(8,128)(2,1)S(1)}, bf16[512,256]{1,0:T(8,128)(2,1)S(1)}, u32[]{:S(2)}, u32[]{:S(2)}) collective-permute-start(bf16[512,256]{1,0:T(8,128)(2,1)S(1)} %add_convert_fusion.9), channel_id=1, source_target_pairs={{8,16},{16,8},{12,20},{20,12},{9,17},{17,9},{13,21},{21,13},{10,18... | collective-permute-start | bytes 786440 | tf_op jit(solution)/shard_map/ppermute | solution.py:169
  44.0 34.1 %collective-permute-start.9 = (bf16[512,256]{1,0:T(8,128)(2,1)S(1)}, bf16[512,256]{1,0:T(8,128)(2,1)S(1)}, u32[]{:S(2)}, u32[]{:S(2)}) collective-permute-start(bf16[512,256]{1,0:T(8,128)(2,1)S(1)} %add_convert_fusion.9), channel_id=1, source_target_pairs={{8,0},{16,24},{12,4},{20,28},{9,1},{17,25},{13,5},{21,29},{10,2},{... | collective-permute-start | bytes 786440 | tf_op jit(solution)/shard_map/ppermute | solution.py:169
  54.2 43.5 %collective-permute-start.4 = (bf16[512,256]{1,0:T(8,128)(2,1)S(1)}, bf16[512,256]{1,0:T(8,128)(2,1)S(1)}, u32[]{:S(2)}, u32[]{:S(2)}) collective-permute-start(bf16[512,256]{1,0:T(8,128)(2,1)S(1)} %broadcast_select_fusion.11.rest_4_), channel_id=1, source_target_pairs={{0,4},{4,0},{8,12},{12,8},{16,20},{20,16},{24,28},{28,24},{1,5},{5... | collective-permute-start | bytes 786440 | tf_op jit(solution)/shard_map/ppermute | solution.py:169
  60.1 21.3 %collective-permute-start.30 = (bf16[512,256]{1,0:T(8,128)(2,1)S(1)}, bf16[512,256]{1,0:T(8,128)(2,1)S(1)}, u32[]{:S(2)}, u32[]{:S(2)}) collective-permute-start(bf16[512,256]{1,0:T(8,128)(2,1)S(1)} %partial_panel.25), channel_id=1, source_target_pairs={{0,4},{4,0},{8,12},{12,8},{16,20},{20,16},{24,28},{28,24},{1,5},{5... | collective-permute-start | bytes 786440 | tf_op jit(solution)/shard_map/ppermute | solution.py:169
  67.4 14.7 %collective-permute-start.36 = (bf16[512,256]{1,0:T(8,128)(2,1)S(1)}, bf16[512,256]{1,0:T(8,128)(2,1)S(1)}, u32[]{:S(2)}, u32[]{:S(2)}) collective-permute-start(bf16[512,256]{1,0:T(8,128)(2,1)S(1)} %get-tuple-element.34), channel_id=1, source_target_pairs={{0,8},{24,16},{4,12},{28,20},{1,9},{25,17},{5,13},{29,21},{2,10},{... | collective-permute-start | bytes 786440 | tf_op jit(solution)/shard_map/ppermute | solution.py:169
  78.1 28.6 %collective-permute-start.35 = (bf16[512,256]{1,0:T(8,128)(2,1)S(1)}, bf16[512,256]{1,0:T(8,128)(2,1)S(1)}, u32[]{:S(2)}, u32[]{:S(2)}) collective-permute-start(bf16[512,256]{1,0:T(8,128)(2,1)S(1)} %get-tuple-element.32), channel_id=1, source_target_pairs={{0,8},{24,16},{4,12},{28,20},{1,9},{25,17},{5,13},{29,21},{2,10},{... | collective-permute-start | bytes 786440 | tf_op jit(solution)/shard_map/ppermute | solution.py:169
  82.0 9.5 %collective-permute-start.21 = (bf16[512,256]{1,0:T(8,128)(2,1)S(1)}, bf16[512,256]{1,0:T(8,128)(2,1)S(1)}, u32[]{:S(2)}, u32[]{:S(2)}) collective-permute-start(bf16[512,256]{1,0:T(8,128)(2,1)S(1)} %get-tuple-element.30), channel_id=1, source_target_pairs={{0,8},{24,16},{4,12},{28,20},{1,9},{25,17},{5,13},{29,21},{2,10},{... | collective-permute-start | bytes 786440 | tf_op jit(solution)/shard_map/ppermute | solution.py:169
  83.4 28.0 %collective-permute-start.20 = (bf16[512,256]{1,0:T(8,128)(2,1)S(1)}, bf16[512,256]{1,0:T(8,128)(2,1)S(1)}, u32[]{:S(2)}, u32[]{:S(2)}) collective-permute-start(bf16[512,256]{1,0:T(8,128)(2,1)S(1)} %get-tuple-element.28), channel_id=1, source_target_pairs={{0,8},{24,16},{4,12},{28,20},{1,9},{25,17},{5,13},{29,21},{2,10},{... | collective-permute-start | bytes 786440 | tf_op jit(solution)/shard_map/ppermute | solution.py:169
  91.6 25.9 %collective-permute-start.44 = (bf16[16,256,128]{2,1,0:T(8,128)(2,1)S(1)}, bf16[16,256,128]{2,1,0:T(8,128)(2,1)S(1)}, u32[]{:S(2)}, u32[]{:S(2)}) collective-permute-start(bf16[16,256,128]{2,1,0:T(8,128)(2,1)S(1)} %collective-permute-done.29.heads_ref), channel_id=1, source_target_pairs={{0,1},{1,0},{2,3},{3,2},{4,5},{5,4},{6,7},{7,6},{8,9},{9,8},{10,11... | collective-permute-start | bytes 3145736 | tf_op jit(solution)/shard_map/ppermute | solution.py:170
  97.8 12.1 %collective-permute-start.37 = (bf16[512,256]{1,0:T(8,128)(2,1)S(1)}, bf16[512,256]{1,0:T(8,128)(2,1)S(1)}, u32[]{:S(2)}, u32[]{:S(2)}) collective-permute-start(bf16[512,256]{1,0:T(8,128)(2,1)S(1)} %add_convert_fusion.4), channel_id=1, source_target_pairs={{8,16},{16,8},{12,20},{20,12},{9,17},{17,9},{13,21},{21,13},{10,18... | collective-permute-start | bytes 786440 | tf_op jit(solution)/shard_map/ppermute | solution.py:169
  106.8 115.1 %collective-permute-start.12 = (bf16[512,256]{1,0:T(8,128)(2,1)}, bf16[512,256]{1,0:T(8,128)(2,1)}, u32[]{:S(2)}, u32[]{:S(2)}) collective-permute-start(bf16[512,256]{1,0:T(8,128)(2,1)} %fusion.19), channel_id=1, source_target_pairs={{0,2},{4,6},{8,10},{12,14},{17,19},{21,23},{25,27},{29,31}} | collective-permute-start | bytes 786440 | tf_op jit(solution)/shard_map/ppermute | solution.py:255
  113.8 44.6 %collective-permute-start.40 = (bf16[512,256]{1,0:T(8,128)(2,1)S(1)}, bf16[512,256]{1,0:T(8,128)(2,1)S(1)}, u32[]{:S(2)}, u32[]{:S(2)}) collective-permute-start(bf16[512,256]{1,0:T(8,128)(2,1)S(1)} %add_convert_fusion.3), channel_id=1, source_target_pairs={{8,16},{16,8},{12,20},{20,12},{9,17},{17,9},{13,21},{21,13},{10,18... | collective-permute-start | bytes 786440 | tf_op jit(solution)/shard_map/ppermute | solution.py:169
  114.6 28.8 %collective-permute-start.39 = (bf16[512,256]{1,0:T(8,128)(2,1)S(1)}, bf16[512,256]{1,0:T(8,128)(2,1)S(1)}, u32[]{:S(2)}, u32[]{:S(2)}) collective-permute-start(bf16[512,256]{1,0:T(8,128)(2,1)S(1)} %add_convert_fusion.3), channel_id=1, source_target_pairs={{8,0},{16,24},{12,4},{20,28},{9,1},{17,25},{13,5},{21,29},{10,2},{... | collective-permute-start | bytes 786440 | tf_op jit(solution)/shard_map/ppermute | solution.py:169
  116.0 26.0 %collective-permute-start.33 = (bf16[512,256]{1,0:T(8,128)(2,1)S(1)}, bf16[512,256]{1,0:T(8,128)(2,1)S(1)}, u32[]{:S(2)}, u32[]{:S(2)}) collective-permute-start(bf16[512,256]{1,0:T(8,128)(2,1)S(1)} %add_convert_fusion.5), channel_id=1, source_target_pairs={{8,0},{16,24},{12,4},{20,28},{9,1},{17,25},{13,5},{21,29},{10,2},{... | collective-permute-start | bytes 786440 | tf_op jit(solution)/shard_map/ppermute | solution.py:169
  117.4 57.6 %collective-permute-start.25 = (bf16[512,256]{1,0:T(8,128)(2,1)S(1)}, bf16[512,256]{1,0:T(8,128)(2,1)S(1)}, u32[]{:S(2)}, u32[]{:S(2)}) collective-permute-start(bf16[512,256]{1,0:T(8,128)(2,1)S(1)} %add_convert_fusion.6), channel_id=1, source_target_pairs={{8,16},{16,8},{12,20},{20,12},{9,17},{17,9},{13,21},{21,13},{10,18... | collective-permute-start | bytes 786440 | tf_op jit(solution)/shard_map/ppermute | solution.py:169
  142.0 12.9 %collective-permute-start.24 = (bf16[512,256]{1,0:T(8,128)(2,1)S(1)}, bf16[512,256]{1,0:T(8,128)(2,1)S(1)}, u32[]{:S(2)}, u32[]{:S(2)}) collective-permute-start(bf16[512,256]{1,0:T(8,128)(2,1)S(1)} %add_convert_fusion.6), channel_id=1, source_target_pairs={{8,0},{16,24},{12,4},{20,28},{9,1},{17,25},{13,5},{21,29},{10,2},{... | collective-permute-start | bytes 786440 | tf_op jit(solution)/shard_map/ppermute | solution.py:169
  143.4 9.7 %collective-permute-start.18 = (bf16[512,256]{1,0:T(8,128)(2,1)S(1)}, bf16[512,256]{1,0:T(8,128)(2,1)S(1)}, u32[]{:S(2)}, u32[]{:S(2)}) collective-permute-start(bf16[512,256]{1,0:T(8,128)(2,1)S(1)} %add_convert_fusion.8), channel_id=1, source_target_pairs={{8,0},{16,24},{12,4},{20,28},{9,1},{17,25},{13,5},{21,29},{10,2},{... | collective-permute-start | bytes 786440 | tf_op jit(solution)/shard_map/ppermute | solution.py:169
  158.4 13.7 %collective-permute-start.34 = (bf16[512,256]{1,0:T(8,128)(2,1)S(1)}, bf16[512,256]{1,0:T(8,128)(2,1)S(1)}, u32[]{:S(2)}, u32[]{:S(2)}) collective-permute-start(bf16[512,256]{1,0:T(8,128)(2,1)S(1)} %broadcast_select_fusion.5.rest_12_), channel_id=1, source_target_pairs={{0,4},{4,0},{8,12},{12,8},{16,20},{20,16},{24,28},{28,24},{1,5},{5... | collective-permute-start | bytes 786440 | tf_op jit(solution)/shard_map/ppermute | solution.py:169
  175.0 16.0 %collective-permute-start.19 = (bf16[512,256]{1,0:T(8,128)(2,1)S(1)}, bf16[512,256]{1,0:T(8,128)(2,1)S(1)}, u32[]{:S(2)}, u32[]{:S(2)}) collective-permute-start(bf16[512,256]{1,0:T(8,128)(2,1)S(1)} %broadcast_select_fusion.8.rest_8_), channel_id=1, source_target_pairs={{0,4},{4,0},{8,12},{12,8},{16,20},{20,16},{24,28},{28,24},{1,5},{5... | collective-permute-start | bytes 786440 | tf_op jit(solution)/shard_map/ppermute | solution.py:169
  175.3 15.0 %collective-permute-start.26 = (bf16[512,256]{1,0:T(8,128)(2,1)S(1)}, bf16[512,256]{1,0:T(8,128)(2,1)S(1)}, u32[]{:S(2)}, u32[]{:S(2)}) collective-permute-start(bf16[512,256]{1,0:T(8,128)(2,1)S(1)} %collective-permute-done.25), channel_id=1, source_target_pairs={{8,0},{16,24},{12,4},{20,28},{9,1},{17,25},{13,5},{21,29},{10,2},{... | collective-permute-start | bytes 786440 | tf_op jit(solution)/shard_map/ppermute | solution.py:169
  176.6 47.7 %collective-permute-start.42 = (bf16[512,256]{1,0:T(8,128)(2,1)}, bf16[512,256]{1,0:T(8,128)(2,1)}, u32[]{:S(2)}, u32[]{:S(2)}) collective-permute-start(bf16[512,256]{1,0:T(8,128)(2,1)} %fusion.11), channel_id=1, source_target_pairs={{0,2},{4,6},{8,10},{12,14},{17,19},{21,23},{25,27},{29,31}} | collective-permute-start | bytes 786440 | tf_op jit(solution)/shard_map/ppermute | solution.py:255
  180.7 21.7 %collective-permute-start.48 = (bf16[512,256]{1,0:T(8,128)(2,1)S(1)}, bf16[512,256]{1,0:T(8,128)(2,1)S(1)}, u32[]{:S(2)}, u32[]{:S(2)}) collective-permute-start(bf16[512,256]{1,0:T(8,128)(2,1)S(1)} %add_convert_fusion.2), channel_id=1, source_target_pairs={{8,0},{16,24},{12,4},{20,28},{9,1},{17,25},{13,5},{21,29},{10,2},{... | collective-permute-start | bytes 786440 | tf_op jit(solution)/shard_map/ppermute | solution.py:169
  190.3 15.2 %collective-permute-start.55 = (bf16[512,256]{1,0:T(8,128)(2,1)S(1)}, bf16[512,256]{1,0:T(8,128)(2,1)S(1)}, u32[]{:S(2)}, u32[]{:S(2)}) collective-permute-start(bf16[512,256]{1,0:T(8,128)(2,1)S(1)} %add_convert_fusion), channel_id=1, source_target_pairs={{8,16},{16,8},{12,20},{20,12},{9,17},{17,9},{13,21},{21,13},{10,18... | collective-permute-start | bytes 786440 | tf_op jit(solution)/shard_map/ppermute | solution.py:169
  191.0 15.8 %collective-permute-start.54 = (bf16[512,256]{1,0:T(8,128)(2,1)S(1)}, bf16[512,256]{1,0:T(8,128)(2,1)S(1)}, u32[]{:S(2)}, u32[]{:S(2)}) collective-permute-start(bf16[512,256]{1,0:T(8,128)(2,1)S(1)} %add_convert_fusion), channel_id=1, source_target_pairs={{8,0},{16,24},{12,4},{20,28},{9,1},{17,25},{13,5},{21,29},{10,2},{... | collective-permute-start | bytes 786440 | tf_op jit(solution)/shard_map/ppermute | solution.py:169
  202.4 24.2 %collective-permute-start.27 = (bf16[512,256]{1,0:T(8,128)(2,1)}, bf16[512,256]{1,0:T(8,128)(2,1)}, u32[]{:S(2)}, u32[]{:S(2)}) collective-permute-start(bf16[512,256]{1,0:T(8,128)(2,1)} %fusion.15), channel_id=1, source_target_pairs={{0,2},{4,6},{8,10},{12,14},{17,19},{21,23},{25,27},{29,31}} | collective-permute-start | bytes 786440 | tf_op jit(solution)/shard_map/ppermute | solution.py:255
  216.8 12.3 %collective-permute-start.57 = (bf16[512,256]{1,0:T(8,128)(2,1)}, bf16[512,256]{1,0:T(8,128)(2,1)}, u32[]{:S(2)}, u32[]{:S(2)}) collective-permute-start(bf16[512,256]{1,0:T(8,128)(2,1)} %fusion.7), channel_id=1, source_target_pairs={{0,2},{4,6},{8,10},{12,14},{17,19},{21,23},{25,27},{29,31}} | collective-permute-start | bytes 786440 | tf_op jit(solution)/shard_map/ppermute | solution.py:255
  (41 other events, 295.8 us)

commit v2 on v0

v2 whole, which is shorter than its diff:
```python
import functools

import jax
import jax.numpy as jnp
from jax import lax
from jax.experimental import pallas as pl
from jax.experimental.pallas import tpu as pltpu
from jax.sharding import PartitionSpec as P

f32, bf16 = jnp.float32, jnp.bfloat16
LANES = 128
MIB = 1 << 20
LIMIT = 10 * MIB
IN_VMEM = pl.BlockSpec(memory_space=pltpu.VMEM)
IN_HBM = pl.BlockSpec(memory_space=pltpu.HBM)
PIECES = ((2, 3, 3), (4, 4))
UNIT, HOP, STEP, LEAD, FAR, SLAB = 2.85, 2.0, 1.5, 1.5, 20.0, 60.0
BATCHES = ((0, 1, 2), (3,))


def nt_dot(a, b):
    return lax.dot_general(a, b, (((1,), (1,)), ((), ())), preferred_element_type=f32)


def scaled_flat(blocks, weights):
    parts = [
        (blocks[k].astype(f32) * weights[k : k + 1, :]).astype(bf16) for k in range(blocks.shape[0])
    ]
    return jnp.concatenate(parts, axis=1)


def first_kernel(
    parts, place_ref, counts_ref, order_ref, index_ref, table_ref, border_ref, *rest
):
    weights_ref, heads_ref, scaled_ref, send_ref, held_heads, held, sems = rest
    slots, quarter, width = held.shape
    share = heads_ref.shape[0]
    step = slots // parts
    first = pl.multiple_of(order_ref[1] * quarter, quarter)
    near = pltpu.make_async_copy(border_ref.at[:, pl.ds(0, share), :], held_heads, sems.at[parts])
    near.start()
    copies = [
        pltpu.make_async_copy(
            border_ref.at[pl.ds(i * step, step), pl.ds(first, quarter), :],
            held.at[pl.ds(i * step, step)],
            sems.at[i],
        )
        for i in range(parts)
    ]
    for copy in copies:
        copy.start()

    index = index_ref[...]
    high, low = index // LANES, index % LANES
    total = jnp.zeros(index.shape, f32)
    for row in range(table_ref.shape[0]):
        entries = jnp.broadcast_to(table_ref[row : row + 1, :], index.shape)
        picked = jnp.take_along_axis(entries, low, axis=1, mode="promise_in_bounds")
        total = jnp.where(high == row, picked, total)
    live = lax.broadcasted_iota(jnp.int32, index.shape, 0) < counts_ref[place_ref[0]]
    weights_ref[...] = jnp.where(live, total, 0.0)

    near.wait()
    heads_ref[...] = scaled_flat(held_heads, weights_ref[...])
    for i, copy in enumerate(copies):
        copy.wait()
        scaled_ref[:, i * step * width : (i + 1) * step * width] = scaled_flat(
            held.at[pl.ds(i * step, step)], weights_ref[i * step : (i + 1) * step, :]
        )
    send_ref[...] = nt_dot(scaled_ref[...], heads_ref[...]).astype(bf16)


def first_step(place, counts, order, col_index, barrier, border, share):
    slots, rows, width = border.shape
    quarter = rows // 4
    parts = 4 if slots % 4 == 0 else 1
    smem = pl.BlockSpec(memory_space=pltpu.SMEM)
    whole = lambda shape: pl.BlockSpec(shape, lambda i: (0,) * len(shape))
    table = barrier.reshape(-1, LANES)
    shapes = [
        jax.ShapeDtypeStruct(col_index.shape, f32),
        jax.ShapeDtypeStruct((share, slots * width), bf16),
        jax.ShapeDtypeStruct((quarter, slots * width), bf16),
        jax.ShapeDtypeStruct((quarter, share), bf16),
    ]
    return pl.pallas_call(
        functools.partial(first_kernel, parts),
        grid=(1,),
        in_specs=[smem, smem, smem, whole(col_index.shape), whole(table.shape), IN_HBM],
        out_specs=[whole(out.shape) for out in shapes],
        out_shape=shapes,
        scratch_shapes=[
            pltpu.VMEM((slots, share, width), bf16),
            pltpu.VMEM((slots, quarter, width), bf16),
            pltpu.SemaphoreType.DMA((parts + 1,)),
        ],
        compiler_params=pltpu.CompilerParams(vmem_limit_bytes=58 * MIB),
        name="first_step",
    )(place, counts, order, col_index, table, border)


def scale_kernel(position, parts, order_ref, border_ref, weights_ref, out_ref, held, sems):
    slots, rows, width = held.shape
    first = pl.multiple_of(order_ref[position] * rows, rows)
    step = slots // parts
    copies = [
        pltpu.make_async_copy(
            border_ref.at[pl.ds(i * step, step), pl.ds(first, rows), :],
            held.at[pl.ds(i * step, step)],
            sems.at[i],
        )
        for i in range(parts)
    ]
    for copy in copies:
        copy.start()
    for i, copy in enumerate(copies):
        copy.wait()
        out_ref[:, i * step * width : (i + 1) * step * width] = scaled_flat(
            held.at[pl.ds(i * step, step)], weights_ref[i * step : (i + 1) * step, :]
        )


def scaled_quarter(order, position, border, weights):
    slots, rows, width = border.shape
    quarter = rows // 4
    parts = 4 if slots % 4 == 0 else 1
    return pl.pallas_call(
        functools.partial(scale_kernel, position, parts),
        in_specs=[pl.BlockSpec(memory_space=pltpu.SMEM), IN_HBM, IN_VMEM],
        out_specs=IN_VMEM,
        out_shape=jax.ShapeDtypeStruct((quarter, slots * width), bf16),
        scratch_shapes=[
            pltpu.VMEM((slots, quarter, width), bf16),
            pltpu.SemaphoreType.DMA((parts,)),
        ],
        compiler_params=pltpu.CompilerParams(vmem_limit_bytes=LIMIT),
        name="scaled_quarter",
    )(order, border, weights)


def piece_kernel(runs, adds, *refs):
    rows_refs, heads_refs = refs[:2], refs[2 : 2 + len({g for g, _, _, _ in runs})]
    rest = refs[2 + len(heads_refs) :]
    got, outs = rest[:adds], rest[adds:]
    groups = sorted({g for g, _, _, _ in runs})
    at = 0
    for g, half, begin, end in runs:
        value = nt_dot(rows_refs[half][begin:end, :], heads_refs[groups.index(g)][...])
        place = slice(at, at + end - begin)
        if adds:
            value += got[0][place, :].astype(f32)
        for out in outs:
            out[place, :] = value.astype(out.dtype)
        at += end - begin


def panel_piece(runs, scaled, heads, got, kinds):
    groups = sorted({g for g, _, _, _ in runs})
    rows = sum(end - begin for _, _, begin, end in runs)
    operands = [*scaled, *(heads[g] for g in groups), *got]
    return pl.pallas_call(
        functools.partial(piece_kernel, runs, len(got)),
        in_specs=[IN_VMEM] * len(operands),
        out_specs=[IN_VMEM] * len(kinds),
        out_shape=[jax.ShapeDtypeStruct((rows, heads[groups[0]].shape[0]), kind) for kind in kinds],
        compiler_params=pltpu.CompilerParams(vmem_limit_bytes=LIMIT),
        name="panel_piece",
    )(*operands)


def hold_kernel(order_ref, slab_ref, out_ref, sems):
    quarter = out_ref.shape[1]
    copies = []
    for p in range(4):
        rows = pl.ds(pl.multiple_of(order_ref[p] * quarter, quarter), quarter)
        copies.append(pltpu.make_async_copy(slab_ref.at[rows], out_ref.at[p], sems.at[p]))
    for copy in copies:
        copy.start()
    for copy in copies:
        copy.wait()


def held_slab(order, slab):
    rows, columns = slab.shape
    return pl.pallas_call(
        hold_kernel,
        in_specs=[pl.BlockSpec(memory_space=pltpu.SMEM), IN_HBM],
        out_specs=IN_VMEM,
        out_shape=jax.ShapeDtypeStruct((4, rows // 4, columns), slab.dtype),
        scratch_shapes=[pltpu.SemaphoreType.DMA((4,))],
        compiler_params=pltpu.CompilerParams(vmem_limit_bytes=LIMIT),
        name="held_slab",
    )(order, slab)


def factor_kernel(plan, ids_ref, inverse_ref, *rest):
    widths, sources = plan
    n = len(widths)
    trailing, rest = rest[: len(sources)], rest[len(sources) :]
    total_ref, out_ref = rest if len(rest) == 2 else (None, rest[0])
    ends = [sum(widths[:g]) for g in range(n + 1)]
    begin_of = lambda which, g: (
        ends[g] if ids_ref is None else pl.multiple_of(ids_ref[which, g] * widths[g], widths[g])
    )
    for g in range(n):
        total = None if total_ref is None else total_ref[ends[g] : ends[g + 1], :]
        for batch, groups in enumerate(sources):
            begin = 0
            for j in groups:
                block = inverse_ref[pl.ds(begin_of(0, g), widths[g]), pl.ds(begin_of(1, j), widths[j])]
                part = nt_dot(block, trailing[batch][:, begin : begin + widths[j]])
                total = part if total is None else total + part
                begin += widths[j]
        out_ref[ends[g] : ends[g + 1], :] = total.astype(out_ref.dtype)


def factor(ids, inverse, widths, sources, trailing, total, kind):
    smem = pl.BlockSpec(memory_space=pltpu.SMEM)

    def kernel(*refs):
        factor_kernel((widths, sources), *((None, *refs) if ids is None else refs))

    operands = ([] if ids is None else [ids]) + [inverse, *trailing, *total]
    return pl.pallas_call(
        kernel,
        in_specs=([] if ids is None else [smem]) + [IN_VMEM] * (1 + len(trailing) + len(total)),
        out_specs=IN_VMEM,
        out_shape=jax.ShapeDtypeStruct((inverse.shape[0], trailing[0].shape[0]), kind),
        compiler_params=pltpu.CompilerParams(vmem_limit_bytes=LIMIT),
        name="factor",
    )(*operands)


def update_kernel(plan, order_ref, slab_ref, factor_ref, *rest):
    widths, places = plan
    *pieces, out_ref, held, sems = rest
    quarter = held.shape[1]
    ends = [sum(widths[:g]) for g in range(len(widths) + 1)]
    stores = []
    for p in range(4):
        rows = pl.ds(pl.multiple_of(order_ref[p] * quarter, quarter), quarter)
        stores.append(pltpu.make_async_copy(held.at[p], out_ref.at[rows], sems.at[p]))
    for p in range(4):
        held[p] = slab_ref[p]
        for g, side, half, begin, end, piece, at in places:
            if 2 * half + side == p:
                held[p, begin:end, :] -= jnp.dot(
                    pieces[piece][at : at + end - begin, :],
                    factor_ref[ends[g] : ends[g + 1], :],
                    preferred_element_type=f32,
                )
        stores[p].start()
    for store in stores:
        store.wait()


def update(order, held, factor_value, plan, pieces):
    _, quarter, columns = held.shape
    return pl.pallas_call(
        functools.partial(update_kernel, plan),
        in_specs=[pl.BlockSpec(memory_space=pltpu.SMEM)] + [IN_VMEM] * (2 + len(pieces)),
        out_specs=IN_HBM,
        out_shape=jax.ShapeDtypeStruct((4 * quarter, columns), held.dtype),
        scratch_shapes=[
            pltpu.VMEM(held.shape, f32),
            pltpu.SemaphoreType.DMA((4,)),
        ],
        compiler_params=pltpu.CompilerParams(vmem_limit_bytes=LIMIT),
        name="update",
    )(order, held, factor_value, *pieces)


def body(border, col_index, barrier, counts, inverse, slab):
    scen_count, row_count = lax.axis_size("scen"), lax.axis_size("row")
    s, r = lax.axis_index("scen"), lax.axis_index("row")
    slots, local_rows, width = border.shape
    panel_width = inverse.shape[0]
    share = panel_width // row_count
    quarter = local_rows // 4
    trail = slab.shape[1]
    line = scen_count // 2
    half = line // 2
    x, z = s % 2, s // 2
    order = jnp.stack([x, 1 - x, 2 + x, 3 - x]).astype(jnp.int32)

    swap_x = [(i, i ^ 1) for i in range(scen_count)]
    at = lambda place, lane: place * 2 + lane

    def both_ends(a, b):
        pairs = []
        for lane in range(2):
            pairs += [(at(a, lane), at(b, lane)), (at(line - 1 - a, lane), at(line - 1 - b, lane))]
        return pairs

    inward = [both_ends(t, t + 1) for t in range(half - 1)]
    outward = [both_ends(t + 1, t) for t in reversed(range(half - 1))]
    middle = both_ends(half - 1, half)
    spread_to = [(z == t) | (z == line - 1 - t) for t in reversed(range(half - 1))]
    hops = len(inward)
    over_scen = lambda value, pairs: lax.ppermute(value.astype(bf16), "scen", pairs)
    over_row = lambda value, mask: lax.ppermute(
        value, "row", [(i, i ^ mask) for i in range(row_count)]
    )

    last = []

    def after(*values):
        if not last:
            return values if len(values) > 1 else values[0]
        out = lax.optimization_barrier((*values, *last))
        return out[: len(values)] if len(values) > 1 else out[0]

    def done(*values):
        last[:] = values

    place = s.astype(jnp.int32).reshape(1)
    weights, own, scaled_sent, first_send = first_step(
        place, counts, order, col_index, barrier, border, share
    )
    scaled = {1: scaled_sent}
    done(own)
    far = [over_row(own, mask) for mask in range(2, row_count, 2)]
    sibling = over_row(own, 1)
    joined = lambda group: group[0] if len(group) == 1 else jnp.concatenate(group, axis=0)
    heads = [own, sibling, None, None]
    widths = [share, share, share * len(far), share * len(far)]

    def share_order(device):
        masks = [0, 1] + list(range(2, row_count, 2)) + list(range(3, row_count, 2))
        return [device ^ mask for mask in masks]

    first_row = s * trail
    source = first_row // local_rows

    def take(value, shares, axis):
        return jnp.concatenate(
            [lax.dynamic_slice_in_dim(value, k * share, share, axis) for k in shares], axis
        )

    aligned = trail <= quarter and all(
        (g * trail) % local_rows // quarter % 2 == g % 2 for g in range(scen_count)
    )
    unit = min(trail, quarter)
    masks = [1 << k for k in reversed(range((row_count - 1).bit_length()))]
    spread = []
    reached = {g: {g * trail // local_rows} for g in range(scen_count)}
    for mask in masks:
        spread.append(
            [
                (g * row_count + k, g * row_count + (k ^ mask))
                for g in range(scen_count)
                for k in sorted(reached[g])
            ]
        )
        for g in range(scen_count):
            reached[g] |= {k ^ mask for k in reached[g]}

    eighth = quarter // 2
    pieces = []
    for pair, sizes in enumerate(PIECES):
        units = [(2 * pair + g, b // 2, b % 2) for g in range(2) for b in range(4)]
        for size in sizes:
            runs = []
            for g, half, part in units[:size]:
                if runs and runs[-1][:2] == (g, half):
                    runs[-1] = (*runs[-1][:3], (part + 1) * eighth)
                else:
                    runs.append((g, half, part * eighth, (part + 1) * eighth))
            pieces.append(runs)
            units = units[size:]
    sizes = [size for pair in PIECES for size in pair]
    count = len(pieces)
    offsets = []
    for runs in pieces:
        places, at_row = [], 0
        for g, h, begin, end in runs:
            places.append((g, h, begin, end, at_row))
            at_row += end - begin
        offsets.append(places)
    last_of = [max(k for k, runs in enumerate(pieces) if any(run[0] == g for run in runs)) for g in range(4)]

    def kept_rows(values, g):
        parts = []
        for k, places in enumerate(offsets):
            parts += [values[k][at : at + end - begin] for h, _, begin, end, at in places if h == g]
        return jnp.concatenate(parts, axis=0)

    def trailing_rows(groups):
        columns = []
        for g in groups:
            kept, parts = kept_rows(mine, g), []
            other = None if aligned else kept_rows(others, g)
            for i in range(trail // unit):
                start = first_row % local_rows + i * unit
                place, inside = start // quarter, start % quarter
                begin = place // 2 * quarter + inside
                value = lax.dynamic_slice_in_dim(kept, begin, unit, 0)
                if not aligned:
                    value = jnp.where(
                        place % 2 == x, value, lax.dynamic_slice_in_dim(other, begin, unit, 0)
                    )
                parts.append(value)
            columns.append(parts[0] if len(parts) == 1 else jnp.concatenate(parts, axis=0))
        rows = columns[0] if len(columns) == 1 else jnp.concatenate(columns, axis=1)
        return jnp.where(source == r, rows, jnp.zeros_like(rows))

    steps, free = [(FAR, 0, "far"), (SLAB, 0, "slab")], {}

    def send_over(link, ready, size):
        begin = max(ready, free.get(link, 0.0))
        free[link] = begin + size * UNIT
        return begin, free[link] + HOP

    clock, finals, arrivals = [], [], []
    for k, size in enumerate(sizes):
        begin, now = send_over("x", 0.0, size)
        steps.append((begin - LEAD if k else -100.0, k, "send"))
        clock.append(now)
    chain = [("in", t) for t in range(hops)] + ["middle"] + [("out", t) for t in range(hops)]
    for k, size in enumerate(sizes):
        steps.append((clock[k], k, "sum"))
        now = clock[k]
        for name in chain:
            _, now = send_over(name, now + STEP, size)
            steps.append((now, k, name))
        finals.append(now)
    for k, size in enumerate(sizes):
        _, now = send_over("x", finals[k] + STEP, size)
        arrivals.append(now)
        steps.append((now, k, "other"))
    batches = BATCHES
    for i, groups in enumerate(batches):
        needed = [k for k, runs in enumerate(pieces) if any(run[0] in groups for run in runs)]
        now = max((finals if aligned else arrivals)[k] for k in needed) + 0.01
        for t in range(len(spread) + 1):
            steps.append((now, i, ("trail", t)))
            now += HOP + STEP + UNIT * len(groups) / (t + 1)
        steps.append((now, i, "factor"))
    steps.sort(key=lambda step: step[0])
    if share % LANES == 0 and row_count == 4:
        ids = jnp.stack([jnp.stack(share_order(r)), jnp.stack(share_order(source))])
        ids, ordered = ids.astype(jnp.int32), inverse
    else:
        ids = None
        ordered = take(take(inverse, share_order(r), 0), share_order(source), 1)
    factors = []

    state, mine, others = [None] * count, [None] * count, [None] * count
    trailing = [None] * len(batches)
    def quarters(positions):
        for position in positions:
            if position not in scaled:
                scaled[position] = scaled_quarter(order, position, border, after(weights))
                done(scaled[position])
        return [scaled[position] for position in positions]

    for _, k, name in steps:
        if name in ("send", "sum"):
            used = sorted({run[1] for run in pieces[k]})
            both = quarters([2 * half + (name == "send") for half in used])
            both = [both[used.index(half)] if half in used else both[0] for half in (0, 1)]
        if name == "send" and k == 0:
            state[k] = over_scen(first_send, swap_x)
        elif name == "send":
            values = list(heads)
            for g in sorted({run[0] for run in pieces[k]}):
                values[g] = after(heads[g])
            (send,) = panel_piece(pieces[k], both, values, [], [bf16])
            done(send)
            state[k] = over_scen(send, swap_x)
        elif name == "far":
            far = list(after(*far)) if len(far) > 1 else [after(far[0])]
            done(*far)
            heads[2:] = joined(far), joined([over_row(value, 1) for value in far])
        elif name == "sum":
            out = panel_piece(pieces[k], both, heads, [after(state[k])], [f32, bf16])
            done(*out)
            state[k] = out[0], over_scen(out[1], (inward + [middle])[0])
        elif name == "middle" or name[0] == "in":
            total, got = after(*state[k])
            total = total + got.astype(f32)
            if name == "middle":
                total = total.astype(bf16)
                done(total)
                if hops:
                    state[k] = total, over_scen(total, outward[0])
                else:
                    mine[k], others[k] = total, over_scen(total, swap_x)
            else:
                done(total)
                state[k] = total, over_scen(total, (inward[1:] + [middle])[name[1]])
        elif name[0] == "out":
            t = name[1]
            final, got = after(*state[k])
            final = jnp.where(spread_to[t], got, final)
            done(final)
            if t < hops - 1:
                state[k] = final, over_scen(final, outward[t + 1])
            else:
                mine[k], others[k] = final, over_scen(final, swap_x)
        elif name == "other":
            others[k] = after(others[k])
            done(others[k])
        elif name == "slab":
            held = held_slab(order, after(slab))
            done(held)
        elif name == "factor":
            rows = after(trailing[k])
            last_one = k == len(batches) - 1
            factors = [
                factor(ids, ordered, tuple(widths), [batches[k]], [rows], factors, bf16 if last_one else f32)
            ]
            done(*factors)
        else:
            t = name[1]
            if t == 0:
                rows = trailing_rows(batches[k])
            else:
                rows, got = after(*trailing[k])
                rows = rows + got
            done(rows)
            trailing[k] = rows
            if t < len(spread):
                trailing[k] = rows, lax.ppermute(rows, ("scen", "row"), spread[t])

    places = []
    for k in range(count):
        for g, h, begin, end, at_row in offsets[k]:
            places.append((g, 0, h, begin, end, k, at_row))
            places.append((g, 1, h, begin, end, count + k, at_row))
    return update(order, held, factors[0], (tuple(widths), places), mine + others)


def solution(mesh):
    return jax.shard_map(
        body,
        mesh=mesh,
        in_specs=(P("scen", "row", None), P("scen", None), P(), P(), P(), P("row", "scen")),
        out_specs=P("row", "scen"),
        check_vma=False,
    )
```

time: 464 us -> 153 us (0.33)
  waiting for transfers between devices: 394 us -> 24 us
  starting transfers between devices: 0.17 us -> 64.5 us
  Pallas kernels: 0 us -> 33.2 us
  matrix products: 20.7 us -> 0 us
  between operations: 13.9 us -> 0.96 us
  local copies, waits for them, and re-layouts: 19.8 us -> 12.1 us
    reduce_scatter x1 -> x0, waiting for transfers between devices: 179 us -> none  [body(): lax.psum_scatter(block_sum, 'scen', scatter_dimension=0, tiled=True)]
    all_gather x3 -> x0, waiting for transfers between devices: 178 us -> none  [the longest x1 71.5 us: body(): lax.all_gather(share_done, 'scen', axis=0, tiled=True)]
    ppermute x0 -> x32, starting transfers between devices: none -> 64.5 us  [the longest x25 49.4 us: body(): lax.ppermute(value.astype(bf16), 'scen', pairs)]
    psum x1 -> x0, waiting for transfers between devices: 36.7 us -> none  [broadcast(): return lax.psum(kept, axis)]
    pallas_call x0 -> x17, Pallas kernels: none -> 33.2 us  [the longest x9 16.8 us: panel_piece(): pl.pallas_call(functools.partial(piece_kernel, runs, len(got)), in_specs=...]
    ppermute x0 -> x32, waiting for transfers between devices: none -> 24 us  [the longest x25 21.7 us: body(): lax.ppermute(value.astype(bf16), 'scen', pairs)]
    dot_general x3 -> x0, matrix products: 20.7 us -> none  [the longest x1 9.96 us: one_group(): jnp.einsum('kib,kjb->ij', left_part, right_part, preferred_element_type=j...]
    unnamed x4 -> x68, local copies, waits for them, and re-layouts: 0.01 us -> 12 us
  transfers between devices with their start and end apart: 5 -> 32, of which waited for: 5 -> 9; matrix products, arithmetic and copies ran while one was open for 1% -> 10% of each run, Pallas kernels for 0% -> 15%
where the time goes in v2:
time: 153 us; the launch traced here: 151 us
  starting transfers between devices  64.5 us (42%)
  Pallas kernels  33.2 us (22%)
  waiting for transfers between devices  24 us (16%)
  other arithmetic  15.8 us (10%)
  local copies, waits for them, and re-layouts  12.1 us (8%)
    ppermute x25, starting transfers between devices, body(): lax.ppermute(value.astype(bf16), 'scen', pairs)  49.4 us
    ppermute x25, waiting for transfers between devices, body(): lax.ppermute(value.astype(bf16), 'scen', pairs)  21.7 us
    pallas_call x9, Pallas kernels, panel_piece(): pl.pallas_call(functools.partial(piece_kernel, runs, len(got)), in_specs=...  16.8 us
    unnamed x68, local copies, waits for them, and re-layouts  12 us
    ppermute x4, starting transfers between devices, body(): trailing[k] = (rows, lax.ppermute(rows, ('scen', 'row'), spread[t]))  11.9 us
    pallas_call x1, Pallas kernels, first_step(): pl.pallas_call(functools.partial(first_kernel, parts), grid=(1,), in_spec...  4.95 us
    pallas_call x1, Pallas kernels, update(): pl.pallas_call(functools.partial(update_kernel, plan), in_specs=[pl.Block...  4.7 us
    add x4, other arithmetic, body(): rows = rows + got  4.54 us
  transfers between devices with their start and end apart: 32, of which 9 were waited for; matrix products, arithmetic and copies ran while one was open for 10% of the time, Pallas kernels for 15%

profile of v2, /device:TPU:0, one launch (start us, length us, event | category | flops | bytes accessed | tf_op | source)
XLA Modules:
  0.0 150.6 jit_solution(16769100382065366313)
XLA Ops:
  0.6 4.9 %first_step.1 = (f32[16,128]{1,0:T(8,128)}, bf16[256,2048]{1,0:T(8,128)(2,1)}, bf16[512,2048]{1,0:T(8,128)(2,1)}, bf16[512,256]{1,0:T(8,128)(2,1)}) custom-call(s32[1]{0:T(128)} %bitcast.4.place_ref, s32[8]{0:T(128)} %counts_ref.1, s32[4]{0:T(128)} %pad_add_fusion.1.order_ref, s32[16,128]{1,0:T(8,128)} %index_ref.1, f32[32,128]{1,0:T(8,128)} %bitcast.20, ...), custom_call_target="tpu_custom_call" | custom-call | tf_op jit(solution)/shard_map/first_step/pallas_call | solution.py:86
  6.1 2.6 %collective-permute-start.6 = (bf16[256,2048]{1,0:T(8,128)(2,1)}, bf16[256,2048]{1,0:T(8,128)(2,1)}, u32[]{:S(2)}, u32[]{:S(2)}) collective-permute-start(bf16[256,2048]{1,0:T(8,128)(2,1)} %get-tuple-element.83.refs_2_), channel_id=1, source_target_pairs={{0,2},{1,3},{2,0},{3,1},{4,6},{5,7},{6,4},{7,5},{8,10},{9,11},{10,... | collective-permute-start | bytes 3145736 | tf_op jit(solution)/shard_map/ppermute | solution.py:301
  10.2 3.4 %copy-done = bf16[16,2048,128]{2,1,0:T(8,128)(2,1)S(1)} copy-done((bf16[16,2048,128]{2,1,0:T(8,128)(2,1)S(1)}, bf16[16,2048,128]{2,1,0:T(8,128)(2,1)}, u32[]{:S(2)}) %copy-start) | copy-done | bytes 8388632
  20.0 3.5 %collective-permute-start.2 = (bf16[512,256]{1,0:T(8,128)(2,1)S(1)}, bf16[512,256]{1,0:T(8,128)(2,1)S(1)}, u32[]{:S(2)}, u32[]{:S(2)}) collective-permute-start(bf16[512,256]{1,0:T(8,128)(2,1)S(1)} %get-tuple-element.89), channel_id=1, source_target_pairs={{0,8},{24,16},{4,12},{28,20},{1,9},{25,17},{5,13},{29,21},{2,10},{... | collective-permute-start | bytes 786440 | tf_op jit(solution)/shard_map/ppermute | solution.py:300
  25.6 2.5 %collective-permute-done.3.refs_4_ = bf16[768,256]{1,0:T(8,128)(2,1)S(1)} collective-permute-done((bf16[768,256]{1,0:T(8,128)(2,1)S(1)}, bf16[768,256]{1,0:T(8,128)(2,1)S(1)}, u32[]{:S(2)}, u32[]{:S(2)}) %collective-permute-start.3) | collective-permute-done | bytes 393248 | tf_op jit(solution)/shard_map/ppermute | solution.py:300
  28.1 1.8 %panel_piece.12 = (f32[768,256]{1,0:T(8,128)S(1)}, bf16[768,256]{1,0:T(8,128)(2,1)}) custom-call(bf16[512,2048]{1,0:T(8,128)(2,1)S(1)} %scaled_quarter.4.refs_0_.refs_1_, bf16[512,2048]{1,0:T(8,128)(2,1)S(1)} %scaled_quarter.5.refs_1_, bf16[256,2048]{1,0:T(8,128)(2,1)S(1)} %copy-done.12, bf16[256,2048]{1,0:T(8,128)(2,1)S(1)} %collective-permute-done.refs_3_.refs_2_, ...), custom_call_target="tpu_custom_call" | custom-call | tf_op jit(solution)/shard_map/panel_piece/pallas_call | solution.py:161
  32.7 1.7 %collective-permute-start.5 = (bf16[768,256]{1,0:T(8,128)(2,1)S(1)}, bf16[768,256]{1,0:T(8,128)(2,1)}, u32[]{:S(2)}, u32[]{:S(2)}) collective-permute-start(bf16[768,256]{1,0:T(8,128)(2,1)S(1)} %panel_piece.11), channel_id=1, source_target_pairs={{0,4},{4,0},{8,12},{12,8},{16,20},{20,16},{24,28},{28,24},{1,5},{5... | collective-permute-start | bytes 1179656 | tf_op jit(solution)/shard_map/ppermute | solution.py:300
  35.8 6.4 %collective-permute-start.9 = (bf16[768,256]{1,0:T(8,128)(2,1)}, bf16[768,256]{1,0:T(8,128)(2,1)}, u32[]{:S(2)}, u32[]{:S(2)}) collective-permute-start(bf16[768,256]{1,0:T(8,128)(2,1)} %get-tuple-element.94), channel_id=1, source_target_pairs={{0,8},{24,16},{4,12},{28,20},{1,9},{25,17},{5,13},{29,21},{2,10},{... | collective-permute-start | bytes 1179656 | tf_op jit(solution)/shard_map/ppermute | solution.py:300
  42.2 1.6 %copy-done.8 = bf16[512,2048]{1,0:T(8,128)(2,1)S(1)} copy-done((bf16[512,2048]{1,0:T(8,128)(2,1)S(1)}, bf16[512,2048]{1,0:T(8,128)(2,1)}, u32[]{:S(2)}) %copy-start.8) | copy-done | bytes 2097176
  43.8 2.7 %panel_piece.13 = bf16[1024,256]{1,0:T(8,128)(2,1)S(1)} custom-call(bf16[512,2048]{1,0:T(8,128)(2,1)S(1)} %copy-done.8, bf16[512,2048]{1,0:T(8,128)(2,1)S(1)} %copy-done.6, bf16[256,2048]{1,0:T(8,128)(2,1)} %collective-permute-done.6.refs_2_), custom_call_target="tpu_custom_call" | custom-call | tf_op jit(solution)/shard_map/panel_piece/pallas_call | solution.py:161
  47.1 2.0 %panel_piece.14 = (f32[768,256]{1,0:T(8,128)S(1)}, bf16[768,256]{1,0:T(8,128)(2,1)S(1)}) custom-call(bf16[512,2048]{1,0:T(8,128)(2,1)S(1)} %copy-done.2, bf16[512,2048]{1,0:T(8,128)(2,1)S(1)} %copy-done.4, bf16[256,2048]{1,0:T(8,128)(2,1)S(1)} %collective-permute-done.refs_3_.refs_2_, bf16[768,256]{1,0:T(8,128)(2,1)} %collective-permute-done.5.refs_3_), custom_call_target="tpu_custom_call" | custom-call | tf_op jit(solution)/shard_map/panel_piece/pallas_call | solution.py:161
  54.7 2.5 %panel_piece.15 = bf16[1024,256]{1,0:T(8,128)(2,1)S(1)} custom-call(bf16[512,2048]{1,0:T(8,128)(2,1)S(1)} %copy-done.9, bf16[512,2048]{1,0:T(8,128)(2,1)S(1)} %copy-done.6, bf16[256,2048]{1,0:T(8,128)(2,1)} %collective-permute-done.8.refs_2_), custom_call_target="tpu_custom_call" | custom-call | tf_op jit(solution)/shard_map/panel_piece/pallas_call | solution.py:161
  58.8 2.3 %collective-permute-done.7 = bf16[512,256]{1,0:T(8,128)(2,1)S(1)} collective-permute-done((bf16[512,256]{1,0:T(8,128)(2,1)S(1)}, bf16[512,256]{1,0:T(8,128)(2,1)S(1)}, u32[]{:S(2)}, u32[]{:S(2)}) %collective-permute-start.7) | collective-permute-done | bytes 262176 | tf_op jit(solution)/shard_map/ppermute | solution.py:300
  61.2 2.6 %panel_piece.16 = (f32[1024,256]{1,0:T(8,128)S(1)}, bf16[1024,256]{1,0:T(8,128)(2,1)S(1)}) custom-call(bf16[512,2048]{1,0:T(8,128)(2,1)S(1)} %copy-done.2, bf16[512,2048]{1,0:T(8,128)(2,1)S(1)} %copy-done.4, bf16[256,2048]{1,0:T(8,128)(2,1)} %collective-permute-done.6.refs_2_, bf16[1024,256]{1,0:T(8,128)(2,1)S(1)} %collective-permute-done.13.refs_3_), custom_call_target="tpu_custom_call" | custom-call | tf_op jit(solution)/shard_map/panel_piece/pallas_call | solution.py:161
  66.1 5.8 %collective-permute-start.15 = (bf16[1024,256]{1,0:T(8,128)(2,1)S(1)}, bf16[1024,256]{1,0:T(8,128)(2,1)S(1)}, u32[]{:S(2)}, u32[]{:S(2)}) collective-permute-start(bf16[1024,256]{1,0:T(8,128)(2,1)S(1)} %get-tuple-element.111), channel_id=1, source_target_pairs={{0,8},{24,16},{4,12},{28,20},{1,9},{25,17},{5,13},{29,21},{2,10},{... | collective-permute-start | bytes 1572872 | tf_op jit(solution)/shard_map/ppermute | solution.py:300
  73.3 2.5 %panel_piece.17 = (f32[1024,256]{1,0:T(8,128)S(1)}, bf16[1024,256]{1,0:T(8,128)(2,1)S(1)}) custom-call(bf16[512,2048]{1,0:T(8,128)(2,1)S(1)} %copy-done.2, bf16[512,2048]{1,0:T(8,128)(2,1)S(1)} %copy-done.4, bf16[256,2048]{1,0:T(8,128)(2,1)} %collective-permute-done.8.refs_2_, bf16[1024,256]{1,0:T(8,128)(2,1)S(1)} %collective-permute-done.17.refs_3_), custom_call_target="tpu_custom_call" | custom-call | tf_op jit(solution)/shard_map/panel_piece/pallas_call | solution.py:161
  75.9 6.1 %collective-permute-start.18 = (bf16[1024,256]{1,0:T(8,128)(2,1)S(1)}, bf16[1024,256]{1,0:T(8,128)(2,1)S(1)}, u32[]{:S(2)}, u32[]{:S(2)}) collective-permute-start(bf16[1024,256]{1,0:T(8,128)(2,1)S(1)} %get-tuple-element.118), channel_id=1, source_target_pairs={{0,8},{24,16},{4,12},{28,20},{1,9},{25,17},{5,13},{29,21},{2,10},{... | collective-permute-start | bytes 1572872 | tf_op jit(solution)/shard_map/ppermute | solution.py:300
  82.1 1.6 %collective-permute-start.19 = (bf16[768,256]{1,0:T(8,128)(2,1)S(1)}, bf16[768,256]{1,0:T(8,128)(2,1)S(1)}, u32[]{:S(2)}, u32[]{:S(2)}) collective-permute-start(bf16[768,256]{1,0:T(8,128)(2,1)S(1)} %add_convert_fusion.2), channel_id=1, source_target_pairs={{8,0},{16,24},{12,4},{20,28},{9,1},{17,25},{13,5},{21,29},{10,2},{... | collective-permute-start | bytes 1179656 | tf_op jit(solution)/shard_map/ppermute | solution.py:300
  87.6 2.0 %copy-done.10 = f32[4,512,512]{2,1,0:T(8,128)} copy-done((f32[4,512,512]{2,1,0:T(8,128)}, f32[4,512,512]{2,1,0:T(8,128)S(1)}, u32[]{:S(2)}) %copy-start.10) | copy-done | bytes 4194328
  89.6 2.4 %collective-permute-done.19 = bf16[768,256]{1,0:T(8,128)(2,1)S(1)} collective-permute-done((bf16[768,256]{1,0:T(8,128)(2,1)S(1)}, bf16[768,256]{1,0:T(8,128)(2,1)S(1)}, u32[]{:S(2)}, u32[]{:S(2)}) %collective-permute-start.19) | collective-permute-done | bytes 393248 | tf_op jit(solution)/shard_map/ppermute | solution.py:300
  92.1 1.9 %collective-permute-start.21 = (bf16[768,256]{1,0:T(8,128)(2,1)S(1)}, bf16[768,256]{1,0:T(8,128)(2,1)S(1)}, u32[]{:S(2)}, u32[]{:S(2)}) collective-permute-start(bf16[768,256]{1,0:T(8,128)(2,1)S(1)} %broadcast_select_fusion.2.rest_2_), channel_id=1, source_target_pairs={{0,4},{4,0},{8,12},{12,8},{16,20},{20,16},{24,28},{28,24},{1,5},{5... | collective-permute-start | bytes 1179656 | tf_op jit(solution)/shard_map/ppermute | solution.py:300
  103.4 6.8 %collective-permute-done.25 = bf16[1024,256]{1,0:T(8,128)(2,1)} collective-permute-done((bf16[1024,256]{1,0:T(8,128)(2,1)S(1)}, bf16[1024,256]{1,0:T(8,128)(2,1)}, u32[]{:S(2)}, u32[]{:S(2)}) %collective-permute-start.25) | collective-permute-done | bytes 524320 | tf_op jit(solution)/shard_map/ppermute | solution.py:300
  111.5 3.5 %collective-permute-start.28 = (bf16[512,768]{1,0:T(8,128)(2,1)S(1)}, bf16[512,768]{1,0:T(8,128)(2,1)S(1)}, u32[]{:S(2)}, u32[]{:S(2)}) collective-permute-start(bf16[512,768]{1,0:T(8,128)(2,1)S(1)} %maximum_select_fusion), channel_id=1, source_target_pairs={{0,2},{4,6},{8,10},{12,14},{17,19},{21,23},{25,27},{29,31}} | collective-permute-start | bytes 2359304 | tf_op jit(solution)/shard_map/ppermute | solution.py:524
  115.0 1.8 %collective-permute-start.27 = (bf16[1024,256]{1,0:T(8,128)(2,1)S(1)}, bf16[1024,256]{1,0:T(8,128)(2,1)S(1)}, u32[]{:S(2)}, u32[]{:S(2)}) collective-permute-start(bf16[1024,256]{1,0:T(8,128)(2,1)S(1)} %broadcast_select_fusion.1.rest_3_), channel_id=1, source_target_pairs={{0,4},{4,0},{8,12},{12,8},{16,20},{20,16},{24,28},{28,24},{1,5},{5... | collective-permute-start | bytes 1572872 | tf_op jit(solution)/shard_map/ppermute | solution.py:300
  116.7 6.0 %collective-permute-done.24 = bf16[1024,256]{1,0:T(8,128)(2,1)S(1)} collective-permute-done((bf16[1024,256]{1,0:T(8,128)(2,1)S(1)}, bf16[1024,256]{1,0:T(8,128)(2,1)S(1)}, u32[]{:S(2)}, u32[]{:S(2)}) %collective-permute-start.24) | collective-permute-done | bytes 524320 | tf_op jit(solution)/shard_map/ppermute | solution.py:300
  125.8 2.3 %collective-permute-start.30 = (bf16[512,768]{1,0:T(8,128)(2,1)}, bf16[512,768]{1,0:T(8,128)(2,1)}, u32[]{:S(2)}, u32[]{:S(2)}) collective-permute-start(bf16[512,768]{1,0:T(8,128)(2,1)} %add.93), channel_id=1, source_target_pairs={{0,1},{2,3},{4,5},{6,7},{8,9},{10,11},{12,13},{14,15},{17,16},{19,... | collective-permute-start | bytes 2359304 | tf_op jit(solution)/shard_map/ppermute | solution.py:524
  128.1 4.1 %collective-permute-start.26 = (bf16[512,256]{1,0:T(8,128)(2,1)S(1)}, bf16[512,256]{1,0:T(8,128)(2,1)S(1)}, u32[]{:S(2)}, u32[]{:S(2)}) collective-permute-start(bf16[512,256]{1,0:T(8,128)(2,1)S(1)} %dynamic-slice_select_fusion), channel_id=1, source_target_pairs={{0,2},{4,6},{8,10},{12,14},{17,19},{21,23},{25,27},{29,31}} | collective-permute-start | bytes 786440 | tf_op jit(solution)/shard_map/ppermute | solution.py:524
  132.3 1.8 %collective-permute-start.31 = (bf16[1024,256]{1,0:T(8,128)(2,1)}, bf16[1024,256]{1,0:T(8,128)(2,1)}, u32[]{:S(2)}, u32[]{:S(2)}) collective-permute-start(bf16[1024,256]{1,0:T(8,128)(2,1)} %broadcast_select_fusion.rest_4_), channel_id=1, source_target_pairs={{0,4},{4,0},{8,12},{12,8},{16,20},{20,16},{24,28},{28,24},{1,5},{5... | collective-permute-start | bytes 1572872 | tf_op jit(solution)/shard_map/ppermute | solution.py:300
  136.9 2.0 %collective-permute-start.29 = (bf16[512,256]{1,0:T(8,128)(2,1)}, bf16[512,256]{1,0:T(8,128)(2,1)}, u32[]{:S(2)}, u32[]{:S(2)}) collective-permute-start(bf16[512,256]{1,0:T(8,128)(2,1)} %add.94), channel_id=1, source_target_pairs={{0,1},{2,3},{4,5},{6,7},{8,9},{10,11},{12,13},{14,15},{17,16},{19,... | collective-permute-start | bytes 786440 | tf_op jit(solution)/shard_map/ppermute | solution.py:524
  139.0 1.6 %add.95.refs_2_ = bf16[512,768]{1,0:T(8,128)(2,1)S(1)} add(bf16[512,768]{1,0:T(8,128)(2,1)} %add.93, bf16[512,768]{1,0:T(8,128)(2,1)} %collective-permute-done.30) | non-fusion elementwise | flops 393216 | bytes 2359296 | tf_op jit(solution)/shard_map/add | solution.py:520
  141.7 1.6 %factor.2.refs_3_ = f32[1024,512]{1,0:T(8,128)S(1)} custom-call(s32[2,4]{1,0:T(2,128)S(1)} %pad_add_fusion.refs_0_, bf16[1024,1024]{1,0:T(8,128)(2,1)S(1)} %copy-done.13, bf16[512,768]{1,0:T(8,128)(2,1)S(1)} %add.95.refs_2_), custom_call_target="tpu_custom_call" | custom-call | tf_op jit(solution)/shard_map/factor/pallas_call | solution.py:224
  145.8 4.7 %update.1 = f32[2048,512]{1,0:T(8,128)} custom-call(s32[4]{0:T(128)S(1)} %copy-done.28, f32[4,512,512]{2,1,0:T(8,128)S(1)} %copy-done.11, bf16[1024,512]{1,0:T(8,128)(2,1)S(1)} %factor.3.factor_ref, bf16[512,256]{1,0:T(8,128)(2,1)S(1)} %copy-done.16, bf16[768,256]{1,0:T(8,128)(2,1)S(1)} %broadcast_select_fusion.3.rest_1_, ...), custom_call_target="tpu_custom_call" | custom-call | tf_op jit(solution)/shard_map/update/pallas_call | solution.py:259
  (147 shorter events, 50.8 us)
Async XLA Ops:
  5.6 9.8 %collective-permute-start = (bf16[256,2048]{1,0:T(8,128)(2,1)}, bf16[256,2048]{1,0:T(8,128)(2,1)S(1)}, u32[]{:S(2)}, u32[]{:S(2)}) collective-permute-start(bf16[256,2048]{1,0:T(8,128)(2,1)} %get-tuple-element.83.refs_2_), channel_id=1, source_target_pairs={{0,1},{1,0},{2,3},{3,2},{4,5},{5,4},{6,7},{7,6},{8,9},{9,8},{10,11... | collective-permute-start | bytes 3145736 | tf_op jit(solution)/shard_map/ppermute | solution.py:301
  6.1 26.7 %collective-permute-start.6 = (bf16[256,2048]{1,0:T(8,128)(2,1)}, bf16[256,2048]{1,0:T(8,128)(2,1)}, u32[]{:S(2)}, u32[]{:S(2)}) collective-permute-start(bf16[256,2048]{1,0:T(8,128)(2,1)} %get-tuple-element.83.refs_2_), channel_id=1, source_target_pairs={{0,2},{1,3},{2,0},{3,1},{4,6},{5,7},{6,4},{7,5},{8,10},{9,11},{10,... | collective-permute-start | bytes 3145736 | tf_op jit(solution)/shard_map/ppermute | solution.py:301
  8.7 10.6 %collective-permute-start.1 = (bf16[512,256]{1,0:T(8,128)(2,1)}, bf16[512,256]{1,0:T(8,128)(2,1)S(1)}, u32[]{:S(2)}, u32[]{:S(2)}) collective-permute-start(bf16[512,256]{1,0:T(8,128)(2,1)} %get-tuple-element.86), channel_id=1, source_target_pairs={{0,4},{4,0},{8,12},{12,8},{16,20},{20,16},{24,28},{28,24},{1,5},{5... | collective-permute-start | bytes 786440 | tf_op jit(solution)/shard_map/ppermute | solution.py:300
  17.1 11.0 %collective-permute-start.3 = (bf16[768,256]{1,0:T(8,128)(2,1)S(1)}, bf16[768,256]{1,0:T(8,128)(2,1)S(1)}, u32[]{:S(2)}, u32[]{:S(2)}) collective-permute-start(bf16[768,256]{1,0:T(8,128)(2,1)S(1)} %panel_piece.9), channel_id=1, source_target_pairs={{0,4},{4,0},{8,12},{12,8},{16,20},{20,16},{24,28},{28,24},{1,5},{5... | collective-permute-start | bytes 1179656 | tf_op jit(solution)/shard_map/ppermute | solution.py:300
  20.0 10.8 %collective-permute-start.2 = (bf16[512,256]{1,0:T(8,128)(2,1)S(1)}, bf16[512,256]{1,0:T(8,128)(2,1)S(1)}, u32[]{:S(2)}, u32[]{:S(2)}) collective-permute-start(bf16[512,256]{1,0:T(8,128)(2,1)S(1)} %get-tuple-element.89), channel_id=1, source_target_pairs={{0,8},{24,16},{4,12},{28,20},{1,9},{25,17},{5,13},{29,21},{2,10},{... | collective-permute-start | bytes 786440 | tf_op jit(solution)/shard_map/ppermute | solution.py:300
  32.7 22.0 %collective-permute-start.8 = (bf16[256,2048]{1,0:T(8,128)(2,1)}, bf16[256,2048]{1,0:T(8,128)(2,1)}, u32[]{:S(2)}, u32[]{:S(2)}) collective-permute-start(bf16[256,2048]{1,0:T(8,128)(2,1)} %collective-permute-done.6.refs_2_), channel_id=1, source_target_pairs={{0,1},{1,0},{2,3},{3,2},{4,5},{5,4},{6,7},{7,6},{8,9},{9,8},{10,11... | collective-permute-start | bytes 3145736 | tf_op jit(solution)/shard_map/ppermute | solution.py:301
  32.7 14.3 %collective-permute-start.5 = (bf16[768,256]{1,0:T(8,128)(2,1)S(1)}, bf16[768,256]{1,0:T(8,128)(2,1)}, u32[]{:S(2)}, u32[]{:S(2)}) collective-permute-start(bf16[768,256]{1,0:T(8,128)(2,1)S(1)} %panel_piece.11), channel_id=1, source_target_pairs={{0,4},{4,0},{8,12},{12,8},{16,20},{20,16},{24,28},{28,24},{1,5},{5... | collective-permute-start | bytes 1179656 | tf_op jit(solution)/shard_map/ppermute | solution.py:300
  34.5 16.1 %collective-permute-start.4 = (bf16[512,256]{1,0:T(8,128)(2,1)}, bf16[512,256]{1,0:T(8,128)(2,1)}, u32[]{:S(2)}, u32[]{:S(2)}) collective-permute-start(bf16[512,256]{1,0:T(8,128)(2,1)} %get-tuple-element.161), channel_id=1, source_target_pairs={{8,16},{16,8},{12,20},{20,12},{9,17},{17,9},{13,21},{21,13},{10,18... | collective-permute-start | bytes 786440 | tf_op jit(solution)/shard_map/ppermute | solution.py:300
  35.8 17.1 %collective-permute-start.9 = (bf16[768,256]{1,0:T(8,128)(2,1)}, bf16[768,256]{1,0:T(8,128)(2,1)}, u32[]{:S(2)}, u32[]{:S(2)}) collective-permute-start(bf16[768,256]{1,0:T(8,128)(2,1)} %get-tuple-element.94), channel_id=1, source_target_pairs={{0,8},{24,16},{4,12},{28,20},{1,9},{25,17},{5,13},{29,21},{2,10},{... | collective-permute-start | bytes 1179656 | tf_op jit(solution)/shard_map/ppermute | solution.py:300
  46.5 14.7 %collective-permute-start.13 = (bf16[1024,256]{1,0:T(8,128)(2,1)S(1)}, bf16[1024,256]{1,0:T(8,128)(2,1)S(1)}, u32[]{:S(2)}, u32[]{:S(2)}) collective-permute-start(bf16[1024,256]{1,0:T(8,128)(2,1)S(1)} %panel_piece.13), channel_id=1, source_target_pairs={{0,4},{4,0},{8,12},{12,8},{16,20},{20,16},{24,28},{28,24},{1,5},{5... | collective-permute-start | bytes 1572872 | tf_op jit(solution)/shard_map/ppermute | solution.py:300
  49.1 14.7 %collective-permute-start.12 = (bf16[768,256]{1,0:T(8,128)(2,1)S(1)}, bf16[768,256]{1,0:T(8,128)(2,1)S(1)}, u32[]{:S(2)}, u32[]{:S(2)}) collective-permute-start(bf16[768,256]{1,0:T(8,128)(2,1)S(1)} %get-tuple-element.101), channel_id=1, source_target_pairs={{0,8},{24,16},{4,12},{28,20},{1,9},{25,17},{5,13},{29,21},{2,10},{... | collective-permute-start | bytes 1179656 | tf_op jit(solution)/shard_map/ppermute | solution.py:300
  51.6 9.5 %collective-permute-start.7 = (bf16[512,256]{1,0:T(8,128)(2,1)S(1)}, bf16[512,256]{1,0:T(8,128)(2,1)S(1)}, u32[]{:S(2)}, u32[]{:S(2)}) collective-permute-start(bf16[512,256]{1,0:T(8,128)(2,1)S(1)} %add_convert_fusion.4), channel_id=1, source_target_pairs={{8,0},{16,24},{12,4},{20,28},{9,1},{17,25},{13,5},{21,29},{10,2},{... | collective-permute-start | bytes 786440 | tf_op jit(solution)/shard_map/ppermute | solution.py:300
  54.0 17.9 %collective-permute-start.11 = (bf16[768,256]{1,0:T(8,128)(2,1)S(1)}, bf16[768,256]{1,0:T(8,128)(2,1)S(1)}, u32[]{:S(2)}, u32[]{:S(2)}) collective-permute-start(bf16[768,256]{1,0:T(8,128)(2,1)S(1)} %get-tuple-element.159), channel_id=1, source_target_pairs={{8,16},{16,8},{12,20},{20,12},{9,17},{17,9},{13,21},{21,13},{10,18... | collective-permute-start | bytes 1179656 | tf_op jit(solution)/shard_map/ppermute | solution.py:300
  57.3 16.1 %collective-permute-start.17 = (bf16[1024,256]{1,0:T(8,128)(2,1)S(1)}, bf16[1024,256]{1,0:T(8,128)(2,1)S(1)}, u32[]{:S(2)}, u32[]{:S(2)}) collective-permute-start(bf16[1024,256]{1,0:T(8,128)(2,1)S(1)} %panel_piece.15), channel_id=1, source_target_pairs={{0,4},{4,0},{8,12},{12,8},{16,20},{20,16},{24,28},{28,24},{1,5},{5... | collective-permute-start | bytes 1572872 | tf_op jit(solution)/shard_map/ppermute | solution.py:300
  63.9 18.1 %collective-permute-start.16 = (bf16[768,256]{1,0:T(8,128)(2,1)S(1)}, bf16[768,256]{1,0:T(8,128)(2,1)S(1)}, u32[]{:S(2)}, u32[]{:S(2)}) collective-permute-start(bf16[768,256]{1,0:T(8,128)(2,1)S(1)} %get-tuple-element.157), channel_id=1, source_target_pairs={{8,16},{16,8},{12,20},{20,12},{9,17},{17,9},{13,21},{21,13},{10,18... | collective-permute-start | bytes 1179656 | tf_op jit(solution)/shard_map/ppermute | solution.py:300
  64.6 21.4 %collective-permute-start.10 = (bf16[512,256]{1,0:T(8,128)(2,1)S(1)}, bf16[512,256]{1,0:T(8,128)(2,1)S(1)}, u32[]{:S(2)}, u32[]{:S(2)}) collective-permute-start(bf16[512,256]{1,0:T(8,128)(2,1)S(1)} %broadcast_select_fusion.4.rest_0_), channel_id=1, source_target_pairs={{0,4},{4,0},{8,12},{12,8},{16,20},{20,16},{24,28},{28,24},{1,5},{5... | collective-permute-start | bytes 786440 | tf_op jit(solution)/shard_map/ppermute | solution.py:300
  66.1 18.1 %collective-permute-start.15 = (bf16[1024,256]{1,0:T(8,128)(2,1)S(1)}, bf16[1024,256]{1,0:T(8,128)(2,1)S(1)}, u32[]{:S(2)}, u32[]{:S(2)}) collective-permute-start(bf16[1024,256]{1,0:T(8,128)(2,1)S(1)} %get-tuple-element.111), channel_id=1, source_target_pairs={{0,8},{24,16},{4,12},{28,20},{1,9},{25,17},{5,13},{29,21},{2,10},{... | collective-permute-start | bytes 1572872 | tf_op jit(solution)/shard_map/ppermute | solution.py:300
  72.0 12.4 %collective-permute-start.14 = (bf16[768,256]{1,0:T(8,128)(2,1)S(1)}, bf16[768,256]{1,0:T(8,128)(2,1)S(1)}, u32[]{:S(2)}, u32[]{:S(2)}) collective-permute-start(bf16[768,256]{1,0:T(8,128)(2,1)S(1)} %add_convert_fusion.3), channel_id=1, source_target_pairs={{8,0},{16,24},{12,4},{20,28},{9,1},{17,25},{13,5},{21,29},{10,2},{... | collective-permute-start | bytes 1179656 | tf_op jit(solution)/shard_map/ppermute | solution.py:300
  75.9 18.2 %collective-permute-start.18 = (bf16[1024,256]{1,0:T(8,128)(2,1)S(1)}, bf16[1024,256]{1,0:T(8,128)(2,1)S(1)}, u32[]{:S(2)}, u32[]{:S(2)}) collective-permute-start(bf16[1024,256]{1,0:T(8,128)(2,1)S(1)} %get-tuple-element.118), channel_id=1, source_target_pairs={{0,8},{24,16},{4,12},{28,20},{1,9},{25,17},{5,13},{29,21},{2,10},{... | collective-permute-start | bytes 1572872 | tf_op jit(solution)/shard_map/ppermute | solution.py:300
  82.1 9.9 %collective-permute-start.19 = (bf16[768,256]{1,0:T(8,128)(2,1)S(1)}, bf16[768,256]{1,0:T(8,128)(2,1)S(1)}, u32[]{:S(2)}, u32[]{:S(2)}) collective-permute-start(bf16[768,256]{1,0:T(8,128)(2,1)S(1)} %add_convert_fusion.2), channel_id=1, source_target_pairs={{8,0},{16,24},{12,4},{20,28},{9,1},{17,25},{13,5},{21,29},{10,2},{... | collective-permute-start | bytes 1179656 | tf_op jit(solution)/shard_map/ppermute | solution.py:300
  84.5 12.4 %collective-permute-start.23 = (bf16[768,256]{1,0:T(8,128)(2,1)S(1)}, bf16[768,256]{1,0:T(8,128)(2,1)S(1)}, u32[]{:S(2)}, u32[]{:S(2)}) collective-permute-start(bf16[768,256]{1,0:T(8,128)(2,1)S(1)} %broadcast_select_fusion.3.rest_1_), channel_id=1, source_target_pairs={{0,4},{4,0},{8,12},{12,8},{16,20},{20,16},{24,28},{28,24},{1,5},{5... | collective-permute-start | bytes 1179656 | tf_op jit(solution)/shard_map/ppermute | solution.py:300
  86.0 10.8 %collective-permute-start.22 = (bf16[1024,256]{1,0:T(8,128)(2,1)S(1)}, bf16[1024,256]{1,0:T(8,128)(2,1)S(1)}, u32[]{:S(2)}, u32[]{:S(2)}) collective-permute-start(bf16[1024,256]{1,0:T(8,128)(2,1)S(1)} %get-tuple-element.153), channel_id=1, source_target_pairs={{8,16},{16,8},{12,20},{20,12},{9,17},{17,9},{13,21},{21,13},{10,18... | collective-permute-start | bytes 1572872 | tf_op jit(solution)/shard_map/ppermute | solution.py:300
  92.1 8.7 %collective-permute-start.21 = (bf16[768,256]{1,0:T(8,128)(2,1)S(1)}, bf16[768,256]{1,0:T(8,128)(2,1)S(1)}, u32[]{:S(2)}, u32[]{:S(2)}) collective-permute-start(bf16[768,256]{1,0:T(8,128)(2,1)S(1)} %broadcast_select_fusion.2.rest_2_), channel_id=1, source_target_pairs={{0,4},{4,0},{8,12},{12,8},{16,20},{20,16},{24,28},{28,24},{1,5},{5... | collective-permute-start | bytes 1179656 | tf_op jit(solution)/shard_map/ppermute | solution.py:300
  95.4 5.4 %collective-permute-start.20 = (bf16[1024,256]{1,0:T(8,128)(2,1)}, bf16[1024,256]{1,0:T(8,128)(2,1)}, u32[]{:S(2)}, u32[]{:S(2)}) collective-permute-start(bf16[1024,256]{1,0:T(8,128)(2,1)} %get-tuple-element.155), channel_id=1, source_target_pairs={{8,16},{16,8},{12,20},{20,12},{9,17},{17,9},{13,21},{21,13},{10,18... | collective-permute-start | bytes 1572872 | tf_op jit(solution)/shard_map/ppermute | solution.py:300
  97.0 13.2 %collective-permute-start.25 = (bf16[1024,256]{1,0:T(8,128)(2,1)S(1)}, bf16[1024,256]{1,0:T(8,128)(2,1)}, u32[]{:S(2)}, u32[]{:S(2)}) collective-permute-start(bf16[1024,256]{1,0:T(8,128)(2,1)S(1)} %add_convert_fusion.1), channel_id=1, source_target_pairs={{8,0},{16,24},{12,4},{20,28},{9,1},{17,25},{13,5},{21,29},{10,2},{... | collective-permute-start | bytes 1572872 | tf_op jit(solution)/shard_map/ppermute | solution.py:300
  102.1 20.7 %collective-permute-start.24 = (bf16[1024,256]{1,0:T(8,128)(2,1)S(1)}, bf16[1024,256]{1,0:T(8,128)(2,1)S(1)}, u32[]{:S(2)}, u32[]{:S(2)}) collective-permute-start(bf16[1024,256]{1,0:T(8,128)(2,1)S(1)} %add_convert_fusion), channel_id=1, source_target_pairs={{8,0},{16,24},{12,4},{20,28},{9,1},{17,25},{13,5},{21,29},{10,2},{... | collective-permute-start | bytes 1572872 | tf_op jit(solution)/shard_map/ppermute | solution.py:300
  111.5 13.2 %collective-permute-start.28 = (bf16[512,768]{1,0:T(8,128)(2,1)S(1)}, bf16[512,768]{1,0:T(8,128)(2,1)S(1)}, u32[]{:S(2)}, u32[]{:S(2)}) collective-permute-start(bf16[512,768]{1,0:T(8,128)(2,1)S(1)} %maximum_select_fusion), channel_id=1, source_target_pairs={{0,2},{4,6},{8,10},{12,14},{17,19},{21,23},{25,27},{29,31}} | collective-permute-start | bytes 2359304 | tf_op jit(solution)/shard_map/ppermute | solution.py:524
  115.0 19.1 %collective-permute-start.27 = (bf16[1024,256]{1,0:T(8,128)(2,1)S(1)}, bf16[1024,256]{1,0:T(8,128)(2,1)S(1)}, u32[]{:S(2)}, u32[]{:S(2)}) collective-permute-start(bf16[1024,256]{1,0:T(8,128)(2,1)S(1)} %broadcast_select_fusion.1.rest_3_), channel_id=1, source_target_pairs={{0,4},{4,0},{8,12},{12,8},{16,20},{20,16},{24,28},{28,24},{1,5},{5... | collective-permute-start | bytes 1572872 | tf_op jit(solution)/shard_map/ppermute | solution.py:300
  125.8 13.2 %collective-permute-start.30 = (bf16[512,768]{1,0:T(8,128)(2,1)}, bf16[512,768]{1,0:T(8,128)(2,1)}, u32[]{:S(2)}, u32[]{:S(2)}) collective-permute-start(bf16[512,768]{1,0:T(8,128)(2,1)} %add.93), channel_id=1, source_target_pairs={{0,1},{2,3},{4,5},{6,7},{8,9},{10,11},{12,13},{14,15},{17,16},{19,... | collective-permute-start | bytes 2359304 | tf_op jit(solution)/shard_map/ppermute | solution.py:524
  128.1 8.0 %collective-permute-start.26 = (bf16[512,256]{1,0:T(8,128)(2,1)S(1)}, bf16[512,256]{1,0:T(8,128)(2,1)S(1)}, u32[]{:S(2)}, u32[]{:S(2)}) collective-permute-start(bf16[512,256]{1,0:T(8,128)(2,1)S(1)} %dynamic-slice_select_fusion), channel_id=1, source_target_pairs={{0,2},{4,6},{8,10},{12,14},{17,19},{21,23},{25,27},{29,31}} | collective-permute-start | bytes 786440 | tf_op jit(solution)/shard_map/ppermute | solution.py:524
  132.3 11.0 %collective-permute-start.31 = (bf16[1024,256]{1,0:T(8,128)(2,1)}, bf16[1024,256]{1,0:T(8,128)(2,1)}, u32[]{:S(2)}, u32[]{:S(2)}) collective-permute-start(bf16[1024,256]{1,0:T(8,128)(2,1)} %broadcast_select_fusion.rest_4_), channel_id=1, source_target_pairs={{0,4},{4,0},{8,12},{12,8},{16,20},{20,16},{24,28},{28,24},{1,5},{5... | collective-permute-start | bytes 1572872 | tf_op jit(solution)/shard_map/ppermute | solution.py:300
  136.9 3.7 %collective-permute-start.29 = (bf16[512,256]{1,0:T(8,128)(2,1)}, bf16[512,256]{1,0:T(8,128)(2,1)}, u32[]{:S(2)}, u32[]{:S(2)}) collective-permute-start(bf16[512,256]{1,0:T(8,128)(2,1)} %add.94), channel_id=1, source_target_pairs={{0,1},{2,3},{4,5},{6,7},{8,9},{10,11},{12,13},{14,15},{17,16},{19,... | collective-permute-start | bytes 786440 | tf_op jit(solution)/shard_map/ppermute | solution.py:524
  (34 other events, 199.4 us)

commit v3 on v2

--- a/solution.py
+++ b/solution.py
@@ -10,12 +10,18 @@
 f32, bf16 = jnp.float32, jnp.bfloat16
 LANES = 128
 MIB = 1 << 20
-LIMIT = 10 * MIB
+LIMIT, LIMIT_FIRST, LIMIT_REST = 10 * MIB, 54 * MIB, 50 * MIB
+SEND_US, SUM_US, JOIN_US, REST_US, TAIL_US = 2.00, 2.00, 1.00, 26.64, 0.92
 IN_VMEM = pl.BlockSpec(memory_space=pltpu.VMEM)
 IN_HBM = pl.BlockSpec(memory_space=pltpu.HBM)
 PIECES = ((2, 3, 3), (4, 4))
-UNIT, HOP, STEP, LEAD, FAR, SLAB = 2.85, 2.0, 1.5, 1.5, 20.0, 60.0
+UNIT, HOP, STEP, FAR, SLAB, AHEAD = 2.85, 2.00, 1.50, 17.72, 88.61, 99.00
+SHIFT = {'send': -1.5, 'sum': 0.0, 'far': 0.0, 'back': 0.0, 'join': 0.0, 'other': 0.0, 'trail': 0.0}
 BATCHES = ((0, 1, 2), (3,))
+
+
+def cost(us):
+    return pl.CostEstimate(flops=int(us * 1e9), bytes_accessed=int(us * 2e6), transcendentals=0)
 
 
 def nt_dot(a, b):
@@ -94,78 +100,133 @@
             pltpu.VMEM((slots, quarter, width), bf16),
             pltpu.SemaphoreType.DMA((parts + 1,)),
         ],
-        compiler_params=pltpu.CompilerParams(vmem_limit_bytes=58 * MIB),
+        cost_estimate=cost(REST_US),
+        compiler_params=pltpu.CompilerParams(vmem_limit_bytes=LIMIT_FIRST),
         name="first_step",
     )(place, counts, order, col_index, table, border)
 
 
-def scale_kernel(position, parts, order_ref, border_ref, weights_ref, out_ref, held, sems):
-    slots, rows, width = held.shape
-    first = pl.multiple_of(order_ref[position] * rows, rows)
+def scale_kernel(positions, parts, order_ref, border_ref, weights_ref, *rest):
+    outs, held, sems = rest[: len(positions)], rest[-2], rest[-1]
+    slots, rows, width = held.shape[1:]
     step = slots // parts
-    copies = [
-        pltpu.make_async_copy(
-            border_ref.at[pl.ds(i * step, step), pl.ds(first, rows), :],
-            held.at[pl.ds(i * step, step)],
-            sems.at[i],
-        )
-        for i in range(parts)
-    ]
+    copies = []
+    for n, position in enumerate(positions):
+        first = pl.multiple_of(order_ref[position] * rows, rows)
+        copies += [
+            pltpu.make_async_copy(
+                border_ref.at[pl.ds(i * step, step), pl.ds(first, rows), :],
+                held.at[n, pl.ds(i * step, step)],
+                sems.at[n * parts + i],
+            )
+            for i in range(parts)
+        ]
     for copy in copies:
         copy.start()
-    for i, copy in enumerate(copies):
-        copy.wait()
-        out_ref[:, i * step * width : (i + 1) * step * width] = scaled_flat(
-            held.at[pl.ds(i * step, step)], weights_ref[i * step : (i + 1) * step, :]
-        )
-
-
-def scaled_quarter(order, position, border, weights):
+    for n, out in enumerate(outs):
+        for i in range(parts):
+            copies[n * parts + i].wait()
+            out[:, i * step * width : (i + 1) * step * width] = scaled_flat(
+                held.at[n, pl.ds(i * step, step)], weights_ref[i * step : (i + 1) * step, :]
+            )
+
+
+def scaled_quarters(order, positions, border, weights):
     slots, rows, width = border.shape
     quarter = rows // 4
     parts = 4 if slots % 4 == 0 else 1
-    return pl.pallas_call(
-        functools.partial(scale_kernel, position, parts),
+    count = len(positions)
+    return pl.pallas_call(
+        functools.partial(scale_kernel, positions, parts),
         in_specs=[pl.BlockSpec(memory_space=pltpu.SMEM), IN_HBM, IN_VMEM],
-        out_specs=IN_VMEM,
-        out_shape=jax.ShapeDtypeStruct((quarter, slots * width), bf16),
+        out_specs=[IN_VMEM] * count,
+        out_shape=[jax.ShapeDtypeStruct((quarter, slots * width), bf16)] * count,
         scratch_shapes=[
-            pltpu.VMEM((slots, quarter, width), bf16),
-            pltpu.SemaphoreType.DMA((parts,)),
+            pltpu.VMEM((count, slots, quarter, width), bf16),
+            pltpu.SemaphoreType.DMA((count * parts,)),
         ],
-        compiler_params=pltpu.CompilerParams(vmem_limit_bytes=LIMIT),
-        name="scaled_quarter",
+        cost_estimate=cost(REST_US),
+        compiler_params=pltpu.CompilerParams(vmem_limit_bytes=LIMIT_REST),
+        name="scaled_quarters",
     )(order, border, weights)
 
 
-def piece_kernel(runs, adds, *refs):
-    rows_refs, heads_refs = refs[:2], refs[2 : 2 + len({g for g, _, _, _ in runs})]
-    rest = refs[2 + len(heads_refs) :]
-    got, outs = rest[:adds], rest[adds:]
+def piece_rows(runs, rows_refs, heads_refs, got, store):
     groups = sorted({g for g, _, _, _ in runs})
     at = 0
     for g, half, begin, end in runs:
         value = nt_dot(rows_refs[half][begin:end, :], heads_refs[groups.index(g)][...])
         place = slice(at, at + end - begin)
-        if adds:
-            value += got[0][place, :].astype(f32)
-        for out in outs:
-            out[place, :] = value.astype(out.dtype)
+        if got is not None:
+            value += got[place, :].astype(f32)
+        store[place, :] = value.astype(store.dtype)
         at += end - begin
 
 
-def panel_piece(runs, scaled, heads, got, kinds):
+def send_kernel(runs, *refs):
+    piece_rows(runs, refs[:2], refs[2:-1], None, refs[-1])
+
+
+def sum_kernel(runs, part_ref, *refs):
+    *heads, got, keep_ref, send_ref, total = refs[2:]
+    piece_rows(runs, refs[:2], heads, got, total)
+    half = keep_ref.shape[0]
+    part = part_ref[0]
+    keep_ref[...] = total[pl.ds(pl.multiple_of(part * half, half), half), :]
+    send_ref[...] = total[pl.ds(pl.multiple_of((1 - part) * half, half), half), :].astype(bf16)
+
+
+def piece_shape(runs, heads):
     groups = sorted({g for g, _, _, _ in runs})
     rows = sum(end - begin for _, _, begin, end in runs)
-    operands = [*scaled, *(heads[g] for g in groups), *got]
-    return pl.pallas_call(
-        functools.partial(piece_kernel, runs, len(got)),
-        in_specs=[IN_VMEM] * len(operands),
-        out_specs=[IN_VMEM] * len(kinds),
-        out_shape=[jax.ShapeDtypeStruct((rows, heads[groups[0]].shape[0]), kind) for kind in kinds],
+    return [heads[g] for g in groups], rows, heads[groups[0]].shape[0]
+
+
+def piece_to_send(runs, scaled, heads):
+    used, rows, columns = piece_shape(runs, heads)
+    return pl.pallas_call(
+        functools.partial(send_kernel, runs),
+        in_specs=[IN_VMEM] * (2 + len(used)),
+        out_specs=IN_VMEM,
+        out_shape=jax.ShapeDtypeStruct((rows, columns), bf16),
+        cost_estimate=cost(SEND_US),
         compiler_params=pltpu.CompilerParams(vmem_limit_bytes=LIMIT),
-        name="panel_piece",
-    )(*operands)
+        name="piece_to_send",
+    )(*scaled, *used)
+
+
+def piece_sum(runs, part, scaled, heads, got):
+    used, rows, columns = piece_shape(runs, heads)
+    return pl.pallas_call(
+        functools.partial(sum_kernel, runs),
+        in_specs=[pl.BlockSpec(memory_space=pltpu.SMEM)] + [IN_VMEM] * (3 + len(used)),
+        out_specs=[IN_VMEM] * 2,
+        out_shape=[jax.ShapeDtypeStruct((rows // 2, columns), kind) for kind in (f32, bf16)],
+        scratch_shapes=[pltpu.VMEM((rows, columns), f32)],
+        cost_estimate=cost(SUM_US),
+        compiler_params=pltpu.CompilerParams(vmem_limit_bytes=LIMIT),
+        name="piece_sum",
+    )(part, *scaled, *used, got)
+
+
+def join_kernel(part_ref, own_ref, got_ref, out_ref):
+    half = own_ref.shape[0]
+    part = part_ref[0]
+    out_ref[pl.ds(pl.multiple_of(part * half, half), half), :] = own_ref[...]
+    out_ref[pl.ds(pl.multiple_of((1 - part) * half, half), half), :] = got_ref[...]
+
+
+def join_halves(part, own, got):
+    rows, columns = own.shape
+    return pl.pallas_call(
+        join_kernel,
+        in_specs=[pl.BlockSpec(memory_space=pltpu.SMEM), IN_VMEM, IN_VMEM],
+        out_specs=IN_VMEM,
+        out_shape=jax.ShapeDtypeStruct((2 * rows, columns), own.dtype),
+        cost_estimate=cost(JOIN_US),
+        compiler_params=pltpu.CompilerParams(vmem_limit_bytes=LIMIT),
+        name="join_halves",
+    )(part, own, got)
 
 
 def hold_kernel(order_ref, slab_ref, out_ref, sems):
@@ -188,6 +249,7 @@
         out_specs=IN_VMEM,
         out_shape=jax.ShapeDtypeStruct((4, rows // 4, columns), slab.dtype),
         scratch_shapes=[pltpu.SemaphoreType.DMA((4,))],
+        cost_estimate=cost(REST_US),
         compiler_params=pltpu.CompilerParams(vmem_limit_bytes=LIMIT),
         name="held_slab",
     )(order, slab)
@@ -226,6 +288,7 @@
         in_specs=([] if ids is None else [smem]) + [IN_VMEM] * (1 + len(trailing) + len(total)),
         out_specs=IN_VMEM,
         out_shape=jax.ShapeDtypeStruct((inverse.shape[0], trailing[0].shape[0]), kind),
+        cost_estimate=cost(TAIL_US),
         compiler_params=pltpu.CompilerParams(vmem_limit_bytes=LIMIT),
         name="factor",
     )(*operands)
@@ -265,6 +328,7 @@
             pltpu.VMEM(held.shape, f32),
             pltpu.SemaphoreType.DMA((4,)),
         ],
+        cost_estimate=cost(TAIL_US),
         compiler_params=pltpu.CompilerParams(vmem_limit_bytes=LIMIT),
         name="update",
     )(order, held, factor_value, *pieces)
@@ -278,26 +342,14 @@
     share = panel_width // row_count
     quarter = local_rows // 4
     trail = slab.shape[1]
-    line = scen_count // 2
-    half = line // 2
     x, z = s % 2, s // 2
     order = jnp.stack([x, 1 - x, 2 + x, 3 - x]).astype(jnp.int32)
 
-    swap_x = [(i, i ^ 1) for i in range(scen_count)]
-    at = lambda place, lane: place * 2 + lane
-
-    def both_ends(a, b):
-        pairs = []
-        for lane in range(2):
-            pairs += [(at(a, lane), at(b, lane)), (at(line - 1 - a, lane), at(line - 1 - b, lane))]
-        return pairs
-
-    inward = [both_ends(t, t + 1) for t in range(half - 1)]
-    outward = [both_ends(t + 1, t) for t in reversed(range(half - 1))]
-    middle = both_ends(half - 1, half)
-    spread_to = [(z == t) | (z == line - 1 - t) for t in reversed(range(half - 1))]
-    hops = len(inward)
-    over_scen = lambda value, pairs: lax.ppermute(value.astype(bf16), "scen", pairs)
+    masks = [1 << bit for bit in range((scen_count - 1).bit_length())]
+    part = (z % 2).astype(jnp.int32).reshape(1)
+    over_scen = lambda value, mask: lax.ppermute(
+        value.astype(bf16), "scen", [(i, i ^ mask) for i in range(scen_count)]
+    )
     over_row = lambda value, mask: lax.ppermute(
         value, "row", [(i, i ^ mask) for i in range(row_count)]
     )
@@ -341,10 +393,10 @@
         (g * trail) % local_rows // quarter % 2 == g % 2 for g in range(scen_count)
     )
     unit = min(trail, quarter)
-    masks = [1 << k for k in reversed(range((row_count - 1).bit_length()))]
+    row_masks = [1 << k for k in reversed(range((row_count - 1).bit_length()))]
     spread = []
     reached = {g: {g * trail // local_rows} for g in range(scen_count)}
-    for mask in masks:
+    for mask in row_masks:
         spread.append(
             [
                 (g * row_count + k, g * row_count + (k ^ mask))
@@ -361,11 +413,11 @@
         units = [(2 * pair + g, b // 2, b % 2) for g in range(2) for b in range(4)]
         for size in sizes:
             runs = []
-            for g, half, part in units[:size]:
+            for g, half, spot in units[:size]:
                 if runs and runs[-1][:2] == (g, half):
-                    runs[-1] = (*runs[-1][:3], (part + 1) * eighth)
+                    runs[-1] = (*runs[-1][:3], (spot + 1) * eighth)
                 else:
-                    runs.append((g, half, part * eighth, (part + 1) * eighth))
+                    runs.append((g, half, spot * eighth, (spot + 1) * eighth))
             pieces.append(runs)
             units = units[size:]
     sizes = [size for pair in PIECES for size in pair]
@@ -404,7 +456,7 @@
         rows = columns[0] if len(columns) == 1 else jnp.concatenate(columns, axis=1)
         return jnp.where(source == r, rows, jnp.zeros_like(rows))
 
-    steps, free = [(FAR, 0, "far"), (SLAB, 0, "slab")], {}
+    steps, free = [(FAR, 0, "heads"), (SLAB, 0, "slab")], {}
 
     def send_over(link, ready, size):
         begin = max(ready, free.get(link, 0.0))
@@ -414,28 +466,36 @@
     clock, finals, arrivals = [], [], []
     for k, size in enumerate(sizes):
         begin, now = send_over("x", 0.0, size)
-        steps.append((begin - LEAD if k else -100.0, k, "send"))
+        late = any(run[0] >= 2 for run in pieces[k])
+        when = max(begin + SHIFT["send"], FAR + 0.01) if late else begin + SHIFT["send"]
+        steps.append((when if k else -100.0, k, "send"))
         clock.append(now)
-    chain = [("in", t) for t in range(hops)] + ["middle"] + [("out", t) for t in range(hops)]
+    hops = len(masks)
     for k, size in enumerate(sizes):
-        steps.append((clock[k], k, "sum"))
-        now = clock[k]
-        for name in chain:
-            _, now = send_over(name, now + STEP, size)
-            steps.append((now, k, name))
+        steps.append((clock[k] + SHIFT["sum"], k, "sum"))
+        _, now = send_over("pair", clock[k] + STEP, size / 2)
+        for t in range(2, hops):
+            steps.append((now + SHIFT["far"], k, ("far", t)))
+            _, now = send_over(("far", t), now + STEP, size)
+        steps.append((now + SHIFT["back"], k, "back"))
+        _, now = send_over("pair back", now + STEP, size / 2)
+        steps.append((now + SHIFT["join"], k, "join"))
         finals.append(now)
     for k, size in enumerate(sizes):
         _, now = send_over("x", finals[k] + STEP, size)
         arrivals.append(now)
-        steps.append((now, k, "other"))
-    batches = BATCHES
+    batches, ends = BATCHES, []
     for i, groups in enumerate(batches):
         needed = [k for k, runs in enumerate(pieces) if any(run[0] in groups for run in runs)]
-        now = max((finals if aligned else arrivals)[k] for k in needed) + 0.01
+        now = max((finals if aligned else arrivals)[k] for k in needed) + 0.01 + SHIFT["trail"]
         for t in range(len(spread) + 1):
             steps.append((now, i, ("trail", t)))
+            ends.append(now)
             now += HOP + STEP + UNIT * len(groups) / (t + 1)
-        steps.append((now, i, "factor"))
+        steps.append((ends[-1] + 0.01, i, "factor"))
+    for k, now in enumerate(arrivals):
+        now = now + SHIFT["other"] if k < count - 1 or not aligned else min(now, ends[-1] + AHEAD)
+        steps.append((now, k, "other"))
     steps.sort(key=lambda step: step[0])
     if share % LANES == 0 and row_count == 4:
         ids = jnp.stack([jnp.stack(share_order(r)), jnp.stack(share_order(source))])
@@ -447,57 +507,41 @@
 
     state, mine, others = [None] * count, [None] * count, [None] * count
     trailing = [None] * len(batches)
-    def quarters(positions):
-        for position in positions:
-            if position not in scaled:
-                scaled[position] = scaled_quarter(order, position, border, after(weights))
-                done(scaled[position])
-        return [scaled[position] for position in positions]
+    rest = (3, 0, 2)
+    scaled.update(zip(rest, scaled_quarters(order, rest, border, after(weights))))
+    done(*(scaled[position] for position in rest))
 
     for _, k, name in steps:
         if name in ("send", "sum"):
-            used = sorted({run[1] for run in pieces[k]})
-            both = quarters([2 * half + (name == "send") for half in used])
-            both = [both[used.index(half)] if half in used else both[0] for half in (0, 1)]
+            both = [scaled[2 * half + (name == "send")] for half in (0, 1)]
         if name == "send" and k == 0:
-            state[k] = over_scen(first_send, swap_x)
+            state[k] = over_scen(first_send, 1)
         elif name == "send":
             values = list(heads)
             for g in sorted({run[0] for run in pieces[k]}):
                 values[g] = after(heads[g])
-            (send,) = panel_piece(pieces[k], both, values, [], [bf16])
+            send = piece_to_send(pieces[k], both, values)
             done(send)
-            state[k] = over_scen(send, swap_x)
-        elif name == "far":
+            state[k] = over_scen(send, 1)
+        elif name == "heads":
             far = list(after(*far)) if len(far) > 1 else [after(far[0])]
             done(*far)
             heads[2:] = joined(far), joined([over_row(value, 1) for value in far])
         elif name == "sum":
-            out = panel_piece(pieces[k], both, heads, [after(state[k])], [f32, bf16])
-            done(*out)
-            state[k] = out[0], over_scen(out[1], (inward + [middle])[0])
-        elif name == "middle" or name[0] == "in":
+            keep, send = piece_sum(pieces[k], part, both, heads, after(state[k]))
+            done(keep, send)
+            state[k] = keep, over_scen(send, 2)
+        elif name[0] == "far" or name == "back":
             total, got = after(*state[k])
             total = total + got.astype(f32)
-            if name == "middle":
+            if name == "back":
                 total = total.astype(bf16)
-                done(total)
-                if hops:
-                    state[k] = total, over_scen(total, outward[0])
-                else:
-                    mine[k], others[k] = total, over_scen(total, swap_x)
-            else:
-                done(total)
-                state[k] = total, over_scen(total, (inward[1:] + [middle])[name[1]])
-        elif name[0] == "out":
-            t = name[1]
-            final, got = after(*state[k])
-            final = jnp.where(spread_to[t], got, final)
-            done(final)
-            if t < hops - 1:
-                state[k] = final, over_scen(final, outward[t + 1])
-            else:
-                mine[k], others[k] = final, over_scen(final, swap_x)
+            done(total)
+            state[k] = total, over_scen(total, 2 if name == "back" else masks[name[1]])
+        elif name == "join":
+            mine[k] = join_halves(part, *after(*state[k]))
+            done(mine[k])
+            others[k] = over_scen(mine[k], 1)
         elif name == "other":
             others[k] = after(others[k])
             done(others[k])

time: 153 us -> 135 us (0.88)
  starting transfers between devices: 64.5 us -> 47.6 us
  waiting for transfers between devices: 24 us -> 40.4 us
  other arithmetic: 15.8 us -> 7.97 us
  Pallas kernels: 33.2 us -> 28 us
  local copies, waits for them, and re-layouts: 12.1 us -> 9.52 us
    ppermute x25, waiting for transfers between devices: 21.7 us -> 40.3 us  [body(): lax.ppermute(value.astype(bf16), 'scen', [(i, i ^ mask) for i in range(sc...]
    ppermute x25, starting transfers between devices: 49.4 us -> 35.4 us  [body(): lax.ppermute(value.astype(bf16), 'scen', [(i, i ^ mask) for i in range(sc...]
    pallas_call x12 -> x15, Pallas kernels: 20.1 us -> 15.9 us  [the longest x5 5.63 us: piece_sum(): pl.pallas_call(functools.partial(sum_kernel, runs), in_specs=[pl.BlockSpe...]
    ppermute x4, starting transfers between devices: 11.9 us -> 9.09 us  [body(): trailing[k] = (rows, lax.ppermute(rows, ('scen', 'row'), spread[t]))]
    unnamed x68 -> x30, local copies, waits for them, and re-layouts: 12 us -> 9.42 us
    convert_element_type x5, other arithmetic: 3.67 us -> 1.17 us  [body(): value.astype(bf16)]
    convert_element_type x5, other arithmetic: 2.61 us -> 0.24 us  [body(): total = total.astype(bf16)]
    select_n x5 -> x0, other arithmetic: 2.09 us -> none  [body(): final = jnp.where(spread_to[t], got, final)]
  transfers between devices with their start and end apart: 32 -> 32, of which waited for: 9 -> 16; matrix products, arithmetic and copies ran while one was open for 10% -> 6% of each run, Pallas kernels for 15% -> 14%
where the time goes in v3:
time: 135 us; the launch traced here: 134 us
  starting transfers between devices  47.6 us (35%)
  waiting for transfers between devices  40.4 us (30%)
  Pallas kernels  28 us (21%)
  local copies, waits for them, and re-layouts  9.52 us (7%)
  other arithmetic  7.97 us (6%)
    ppermute x25, waiting for transfers between devices, body(): lax.ppermute(value.astype(bf16), 'scen', [(i, i ^ mask) for i in range(sc...  40.3 us
    ppermute x25, starting transfers between devices, body(): lax.ppermute(value.astype(bf16), 'scen', [(i, i ^ mask) for i in range(sc...  35.4 us
    unnamed x30, local copies, waits for them, and re-layouts  9.42 us
    ppermute x4, starting transfers between devices, body(): trailing[k] = (rows, lax.ppermute(rows, ('scen', 'row'), spread[t]))  9.09 us
    pallas_call x5, Pallas kernels, piece_sum(): pl.pallas_call(functools.partial(sum_kernel, runs), in_specs=[pl.BlockSpe...  5.63 us
    pallas_call x1, Pallas kernels, scaled_quarters(): pl.pallas_call(functools.partial(scale_kernel, positions, parts), in_spec...  5.47 us
    pallas_call x1, Pallas kernels, first_step(): pl.pallas_call(functools.partial(first_kernel, parts), grid=(1,), in_spec...  4.62 us
    pallas_call x4, Pallas kernels, piece_to_send(): pl.pallas_call(functools.partial(send_kernel, runs), in_specs=[IN_VMEM] *...  4.62 us
  transfers between devices with their start and end apart: 32, of which 16 were waited for; matrix products, arithmetic and copies ran while one was open for 6% of the time, Pallas kernels for 14%

profile of v3, /device:TPU:0, one launch (start us, length us, event | category | flops | bytes accessed | tf_op | source)
XLA Modules:
  0.0 134.0 jit_solution(5407434972023408520)
XLA Ops:
  0.6 4.6 %first_step.1 = (f32[16,128]{1,0:T(8,128)}, bf16[256,2048]{1,0:T(8,128)(2,1)}, bf16[512,2048]{1,0:T(8,128)(2,1)}, bf16[512,256]{1,0:T(8,128)(2,1)}) custom-call(s32[1]{0:T(128)} %bitcast.5.place_ref, s32[8]{0:T(128)} %counts_ref.1, s32[4]{0:T(128)} %pad_add_fusion.1.order_ref, s32[16,128]{1,0:T(8,128)} %index_ref.1, f32[32,128]{1,0:T(8,128)} %bitcast.19, ...), custom_call_target="tpu_custom_call" | custom-call | flops 26639998976 | bytes 53280000 | tf_op jit(solution)/shard_map/first_step/pallas_call | solution.py:92
  5.7 2.6 %collective-permute-start = (bf16[256,2048]{1,0:T(8,128)(2,1)}, bf16[256,2048]{1,0:T(8,128)(2,1)S(1)}, u32[]{:S(2)}, u32[]{:S(2)}) collective-permute-start(bf16[256,2048]{1,0:T(8,128)(2,1)} %get-tuple-element.85.refs_2_), channel_id=1, source_target_pairs={{0,2},{1,3},{2,0},{3,1},{4,6},{5,7},{6,4},{7,5},{8,10},{9,11},{10,... | collective-permute-start | bytes 3145736 | tf_op jit(solution)/shard_map/ppermute | solution.py:353
  10.5 5.5 %scaled_quarters.1 = (bf16[512,2048]{1,0:T(8,128)(2,1)S(1)}, bf16[512,2048]{1,0:T(8,128)(2,1)}, bf16[512,2048]{1,0:T(8,128)(2,1)}) custom-call(s32[4]{0:T(128)S(1)} %copy-done.3, bf16[16,2048,128]{2,1,0:T(8,128)(2,1)} %border_ref.3, f32[16,128]{1,0:T(8,128)S(1)} %copy-done.13), custom_call_target="tpu_custom_call" | custom-call | flops 26639998976 | bytes 53280000 | tf_op jit(solution)/shard_map/scaled_quarters/pallas_call | solution.py:139
  17.3 1.6 %copy-done.8 = bf16[512,2048]{1,0:T(8,128)(2,1)S(1)} copy-done((bf16[512,2048]{1,0:T(8,128)(2,1)S(1)}, bf16[512,2048]{1,0:T(8,128)(2,1)}, u32[]{:S(2)}) %copy-start.8) | copy-done | bytes 2097176
  18.9 1.6 %copy-done.11 = bf16[512,2048]{1,0:T(8,128)(2,1)S(1)} copy-done((bf16[512,2048]{1,0:T(8,128)(2,1)S(1)}, bf16[512,2048]{1,0:T(8,128)(2,1)}, u32[]{:S(2)}) %copy-start.11) | copy-done | bytes 2097176
  23.5 1.6 %collective-permute-start.4 = (bf16[256,256]{1,0:T(8,128)(2,1)S(1)}, bf16[256,256]{1,0:T(8,128)(2,1)S(1)}, u32[]{:S(2)}, u32[]{:S(2)}) collective-permute-start(bf16[256,256]{1,0:T(8,128)(2,1)S(1)} %get-tuple-element.90), channel_id=1, source_target_pairs={{0,8},{4,12},{8,0},{12,4},{16,24},{20,28},{24,16},{28,20},{1,9},{5... | collective-permute-start | bytes 393224 | tf_op jit(solution)/shard_map/ppermute | solution.py:350
  27.2 1.7 %collective-permute-done.4 = bf16[256,256]{1,0:T(8,128)(2,1)S(1)} collective-permute-done((bf16[256,256]{1,0:T(8,128)(2,1)S(1)}, bf16[256,256]{1,0:T(8,128)(2,1)S(1)}, u32[]{:S(2)}, u32[]{:S(2)}) %collective-permute-start.4) | collective-permute-done | bytes 131104 | tf_op jit(solution)/shard_map/ppermute | solution.py:350
  28.9 2.7 %collective-permute-start.8 = (bf16[256,256]{1,0:T(8,128)(2,1)S(1)}, bf16[256,256]{1,0:T(8,128)(2,1)S(1)}, u32[]{:S(2)}, u32[]{:S(2)}) collective-permute-start(bf16[256,256]{1,0:T(8,128)(2,1)S(1)} %get-tuple-element.159), channel_id=1, source_target_pairs={{0,16},{4,20},{8,24},{12,28},{16,0},{20,4},{24,8},{28,12},{1,17},{... | collective-permute-start | bytes 393224 | tf_op jit(solution)/shard_map/ppermute | solution.py:350
  31.6 2.0 %collective-permute-done.2.refs_4_ = bf16[768,256]{1,0:T(8,128)(2,1)S(1)} collective-permute-done((bf16[768,256]{1,0:T(8,128)(2,1)S(1)}, bf16[768,256]{1,0:T(8,128)(2,1)S(1)}, u32[]{:S(2)}, u32[]{:S(2)}) %collective-permute-start.2) | collective-permute-done | bytes 393248 | tf_op jit(solution)/shard_map/ppermute | solution.py:350
  34.7 1.6 %collective-permute-start.7 = (bf16[384,256]{1,0:T(8,128)(2,1)S(1)}, bf16[384,256]{1,0:T(8,128)(2,1)S(1)}, u32[]{:S(2)}, u32[]{:S(2)}) collective-permute-start(bf16[384,256]{1,0:T(8,128)(2,1)S(1)} %get-tuple-element.96), channel_id=1, source_target_pairs={{0,8},{4,12},{8,0},{12,4},{16,24},{20,28},{24,16},{28,20},{1,9},{5... | collective-permute-start | bytes 589832 | tf_op jit(solution)/shard_map/ppermute | solution.py:350
  38.2 2.4 %collective-permute-done.7 = bf16[384,256]{1,0:T(8,128)(2,1)S(1)} collective-permute-done((bf16[384,256]{1,0:T(8,128)(2,1)S(1)}, bf16[384,256]{1,0:T(8,128)(2,1)S(1)}, u32[]{:S(2)}, u32[]{:S(2)}) %collective-permute-start.7) | collective-permute-done | bytes 196640 | tf_op jit(solution)/shard_map/ppermute | solution.py:350
  42.0 1.8 %collective-permute-start.9 = (bf16[384,256]{1,0:T(8,128)(2,1)S(1)}, bf16[384,256]{1,0:T(8,128)(2,1)S(1)}, u32[]{:S(2)}, u32[]{:S(2)}) collective-permute-start(bf16[384,256]{1,0:T(8,128)(2,1)S(1)} %get-tuple-element.105), channel_id=1, source_target_pairs={{0,8},{4,12},{8,0},{12,4},{16,24},{20,28},{24,16},{28,20},{1,9},{5... | collective-permute-start | bytes 589832 | tf_op jit(solution)/shard_map/ppermute | solution.py:350
  44.4 3.8 %collective-permute-start.13 = (bf16[384,256]{1,0:T(8,128)(2,1)S(1)}, bf16[384,256]{1,0:T(8,128)(2,1)S(1)}, u32[]{:S(2)}, u32[]{:S(2)}) collective-permute-start(bf16[384,256]{1,0:T(8,128)(2,1)S(1)} %get-tuple-element.157), channel_id=1, source_target_pairs={{0,16},{4,20},{8,24},{12,28},{16,0},{20,4},{24,8},{28,12},{1,17},{... | collective-permute-start | bytes 589832 | tf_op jit(solution)/shard_map/ppermute | solution.py:350
  50.3 5.0 %collective-permute-done.13 = bf16[384,256]{1,0:T(8,128)(2,1)S(1)} collective-permute-done((bf16[384,256]{1,0:T(8,128)(2,1)S(1)}, bf16[384,256]{1,0:T(8,128)(2,1)S(1)}, u32[]{:S(2)}, u32[]{:S(2)}) %collective-permute-start.13) | collective-permute-done | bytes 196640 | tf_op jit(solution)/shard_map/ppermute | solution.py:350
  56.4 3.2 %collective-permute-start.15 = (bf16[384,256]{1,0:T(8,128)(2,1)S(1)}, bf16[384,256]{1,0:T(8,128)(2,1)S(1)}, u32[]{:S(2)}, u32[]{:S(2)}) collective-permute-start(bf16[384,256]{1,0:T(8,128)(2,1)S(1)} %get-tuple-element.155), channel_id=1, source_target_pairs={{0,16},{4,20},{8,24},{12,28},{16,0},{20,4},{24,8},{28,12},{1,17},{... | collective-permute-start | bytes 589832 | tf_op jit(solution)/shard_map/ppermute | solution.py:350
  62.5 2.1 %collective-permute-done.16.got_ref = bf16[384,256]{1,0:T(8,128)(2,1)S(1)} collective-permute-done((bf16[384,256]{1,0:T(8,128)(2,1)S(1)}, bf16[384,256]{1,0:T(8,128)(2,1)S(1)}, u32[]{:S(2)}, u32[]{:S(2)}) %collective-permute-start.16) | collective-permute-done | bytes 196640 | tf_op jit(solution)/shard_map/ppermute | solution.py:350
  65.1 4.0 %collective-permute-start.19 = (bf16[384,256]{1,0:T(8,128)(2,1)S(1)}, bf16[384,256]{1,0:T(8,128)(2,1)S(1)}, u32[]{:S(2)}, u32[]{:S(2)}) collective-permute-start(bf16[384,256]{1,0:T(8,128)(2,1)S(1)} %add_convert_fusion.2.own_ref), channel_id=1, source_target_pairs={{0,8},{4,12},{8,0},{12,4},{16,24},{20,28},{24,16},{28,20},{1,9},{5... | collective-permute-start | bytes 589832 | tf_op jit(solution)/shard_map/ppermute | solution.py:350
  69.1 2.6 %collective-permute-done.14 = bf16[512,256]{1,0:T(8,128)(2,1)S(1)} collective-permute-done((bf16[512,256]{1,0:T(8,128)(2,1)S(1)}, bf16[512,256]{1,0:T(8,128)(2,1)S(1)}, u32[]{:S(2)}, u32[]{:S(2)}) %collective-permute-start.14) | collective-permute-done | bytes 262176 | tf_op jit(solution)/shard_map/ppermute | solution.py:350
  75.4 1.7 %collective-permute-start.24 = (bf16[768,256]{1,0:T(8,128)(2,1)S(1)}, bf16[768,256]{1,0:T(8,128)(2,1)S(1)}, u32[]{:S(2)}, u32[]{:S(2)}) collective-permute-start(bf16[768,256]{1,0:T(8,128)(2,1)S(1)} %join_halves.6.rest_1_), channel_id=1, source_target_pairs={{0,4},{4,0},{8,12},{12,8},{16,20},{20,16},{24,28},{28,24},{1,5},{5... | collective-permute-start | bytes 1179656 | tf_op jit(solution)/shard_map/ppermute | solution.py:350
  77.1 1.6 %collective-permute-start.22 = (bf16[512,256]{1,0:T(8,128)(2,1)S(1)}, bf16[512,256]{1,0:T(8,128)(2,1)S(1)}, u32[]{:S(2)}, u32[]{:S(2)}) collective-permute-start(bf16[512,256]{1,0:T(8,128)(2,1)S(1)} %get-tuple-element.151), channel_id=1, source_target_pairs={{0,16},{4,20},{8,24},{12,28},{16,0},{20,4},{24,8},{28,12},{1,17},{... | collective-permute-start | bytes 786440 | tf_op jit(solution)/shard_map/ppermute | solution.py:350
  78.8 6.2 %collective-permute-done.17 = bf16[512,256]{1,0:T(8,128)(2,1)S(1)} collective-permute-done((bf16[512,256]{1,0:T(8,128)(2,1)S(1)}, bf16[512,256]{1,0:T(8,128)(2,1)S(1)}, u32[]{:S(2)}, u32[]{:S(2)}) %collective-permute-start.17) | collective-permute-done | bytes 262176 | tf_op jit(solution)/shard_map/ppermute | solution.py:350
  86.0 3.0 %collective-permute-done.22 = bf16[512,256]{1,0:T(8,128)(2,1)S(1)} collective-permute-done((bf16[512,256]{1,0:T(8,128)(2,1)S(1)}, bf16[512,256]{1,0:T(8,128)(2,1)S(1)}, u32[]{:S(2)}, u32[]{:S(2)}) %collective-permute-start.22) | collective-permute-done | bytes 262176 | tf_op jit(solution)/shard_map/ppermute | solution.py:350
  91.7 3.4 %collective-permute-start.20 = (bf16[512,256]{1,0:T(8,128)(2,1)}, bf16[512,256]{1,0:T(8,128)(2,1)S(1)}, u32[]{:S(2)}, u32[]{:S(2)}) collective-permute-start(bf16[512,256]{1,0:T(8,128)(2,1)} %get-tuple-element.153), channel_id=1, source_target_pairs={{0,16},{4,20},{8,24},{12,28},{16,0},{20,4},{24,8},{28,12},{1,17},{... | collective-permute-start | bytes 786440 | tf_op jit(solution)/shard_map/ppermute | solution.py:350
  95.2 2.0 %collective-permute-done.23.got_ref = bf16[512,256]{1,0:T(8,128)(2,1)S(1)} collective-permute-done((bf16[512,256]{1,0:T(8,128)(2,1)S(1)}, bf16[512,256]{1,0:T(8,128)(2,1)S(1)}, u32[]{:S(2)}, u32[]{:S(2)}) %collective-permute-start.23) | collective-permute-done | bytes 262176 | tf_op jit(solution)/shard_map/ppermute | solution.py:350
  98.2 3.3 %collective-permute-start.28 = (bf16[512,768]{1,0:T(8,128)(2,1)}, bf16[512,768]{1,0:T(8,128)(2,1)}, u32[]{:S(2)}, u32[]{:S(2)}) collective-permute-start(bf16[512,768]{1,0:T(8,128)(2,1)} %maximum_select_fusion), channel_id=1, source_target_pairs={{0,2},{4,6},{8,10},{12,14},{17,19},{21,23},{25,27},{29,31}} | collective-permute-start | bytes 2359304 | tf_op jit(solution)/shard_map/ppermute | solution.py:568
  101.6 3.4 %collective-permute-done.20 = bf16[512,256]{1,0:T(8,128)(2,1)S(1)} collective-permute-done((bf16[512,256]{1,0:T(8,128)(2,1)}, bf16[512,256]{1,0:T(8,128)(2,1)S(1)}, u32[]{:S(2)}, u32[]{:S(2)}) %collective-permute-start.20) | collective-permute-done | bytes 262176 | tf_op jit(solution)/shard_map/ppermute | solution.py:350
  105.8 6.0 %collective-permute-done.25.got_ref = bf16[512,256]{1,0:T(8,128)(2,1)S(1)} collective-permute-done((bf16[512,256]{1,0:T(8,128)(2,1)S(1)}, bf16[512,256]{1,0:T(8,128)(2,1)S(1)}, u32[]{:S(2)}, u32[]{:S(2)}) %collective-permute-start.25) | collective-permute-done | bytes 262176 | tf_op jit(solution)/shard_map/ppermute | solution.py:350
  112.6 3.1 %collective-permute-start.26 = (bf16[512,256]{1,0:T(8,128)(2,1)}, bf16[512,256]{1,0:T(8,128)(2,1)}, u32[]{:S(2)}, u32[]{:S(2)}) collective-permute-start(bf16[512,256]{1,0:T(8,128)(2,1)} %dynamic-slice_select_fusion), channel_id=1, source_target_pairs={{0,2},{4,6},{8,10},{12,14},{17,19},{21,23},{25,27},{29,31}} | collective-permute-start | bytes 786440 | tf_op jit(solution)/shard_map/ppermute | solution.py:568
  116.2 1.6 %add.97 = bf16[512,768]{1,0:T(8,128)(2,1)S(1)} add(bf16[512,768]{1,0:T(8,128)(2,1)} %maximum_select_fusion, bf16[512,768]{1,0:T(8,128)(2,1)} %collective-permute-done.28) | non-fusion elementwise | flops 393216 | bytes 2359296 | tf_op jit(solution)/shard_map/add | solution.py:564
  122.4 2.2 %copy-done.4 = f32[2048,512]{1,0:T(8,128)S(1)} copy-done((f32[2048,512]{1,0:T(8,128)S(1)}, f32[2048,512]{1,0:T(8,128)}, u32[]{:S(2)}) %copy-start.4) | copy-done | bytes 4194328
  127.1 1.6 %factor.2.refs_3_ = f32[1024,512]{1,0:T(8,128)S(1)} custom-call(s32[2,4]{1,0:T(2,128)S(1)} %pad_add_fusion.refs_0_, bf16[1024,1024]{1,0:T(8,128)(2,1)S(1)} %copy-done, bf16[512,768]{1,0:T(8,128)(2,1)S(1)} %add.99.refs_2_), custom_call_target="tpu_custom_call" | custom-call | flops 920000000 | bytes 1840000 | tf_op jit(solution)/shard_map/factor/pallas_call | solution.py:286
  129.8 4.0 %update.1 = f32[2048,512]{1,0:T(8,128)} custom-call(s32[4]{0:T(128)S(1)} %copy-done.3, f32[4,512,512]{2,1,0:T(8,128)S(1)} %held_slab.1.slab_ref, bf16[1024,512]{1,0:T(8,128)(2,1)S(1)} %factor.3.factor_ref, bf16[512,256]{1,0:T(8,128)(2,1)S(1)} %join_halves.5.rest_0_, bf16[768,256]{1,0:T(8,128)(2,1)S(1)} %join_halves.6.rest_1_, ...), custom_call_target="tpu_custom_call" | custom-call | flops 920000000 | bytes 1840000 | tf_op jit(solution)/shard_map/update/pallas_call | solution.py:322
  (106 shorter events, 39.9 us)
Async XLA Ops:
  5.2 12.1 %collective-permute-start.1 = (bf16[256,2048]{1,0:T(8,128)(2,1)}, bf16[256,2048]{1,0:T(8,128)(2,1)S(1)}, u32[]{:S(2)}, u32[]{:S(2)}) collective-permute-start(bf16[256,2048]{1,0:T(8,128)(2,1)} %get-tuple-element.85.refs_2_), channel_id=1, source_target_pairs={{0,1},{1,0},{2,3},{3,2},{4,5},{5,4},{6,7},{7,6},{8,9},{9,8},{10,11... | collective-permute-start | bytes 3145736 | tf_op jit(solution)/shard_map/ppermute | solution.py:353
  5.7 30.6 %collective-permute-start = (bf16[256,2048]{1,0:T(8,128)(2,1)}, bf16[256,2048]{1,0:T(8,128)(2,1)S(1)}, u32[]{:S(2)}, u32[]{:S(2)}) collective-permute-start(bf16[256,2048]{1,0:T(8,128)(2,1)} %get-tuple-element.85.refs_2_), channel_id=1, source_target_pairs={{0,2},{1,3},{2,0},{3,1},{4,6},{5,7},{6,4},{7,5},{8,10},{9,11},{10,... | collective-permute-start | bytes 3145736 | tf_op jit(solution)/shard_map/ppermute | solution.py:353
  8.3 13.8 %collective-permute-start.3 = (bf16[512,256]{1,0:T(8,128)(2,1)}, bf16[512,256]{1,0:T(8,128)(2,1)S(1)}, u32[]{:S(2)}, u32[]{:S(2)}) collective-permute-start(bf16[512,256]{1,0:T(8,128)(2,1)} %get-tuple-element.87), channel_id=1, source_target_pairs={{0,4},{4,0},{8,12},{12,8},{16,20},{20,16},{24,28},{28,24},{1,5},{5... | collective-permute-start | bytes 786440 | tf_op jit(solution)/shard_map/ppermute | solution.py:350
  21.5 12.1 %collective-permute-start.2 = (bf16[768,256]{1,0:T(8,128)(2,1)S(1)}, bf16[768,256]{1,0:T(8,128)(2,1)S(1)}, u32[]{:S(2)}, u32[]{:S(2)}) collective-permute-start(bf16[768,256]{1,0:T(8,128)(2,1)S(1)} %piece_to_send.4), channel_id=1, source_target_pairs={{0,4},{4,0},{8,12},{12,8},{16,20},{20,16},{24,28},{28,24},{1,5},{5... | collective-permute-start | bytes 1179656 | tf_op jit(solution)/shard_map/ppermute | solution.py:350
  23.5 5.4 %collective-permute-start.4 = (bf16[256,256]{1,0:T(8,128)(2,1)S(1)}, bf16[256,256]{1,0:T(8,128)(2,1)S(1)}, u32[]{:S(2)}, u32[]{:S(2)}) collective-permute-start(bf16[256,256]{1,0:T(8,128)(2,1)S(1)} %get-tuple-element.90), channel_id=1, source_target_pairs={{0,8},{4,12},{8,0},{12,4},{16,24},{20,28},{24,16},{28,20},{1,9},{5... | collective-permute-start | bytes 393224 | tf_op jit(solution)/shard_map/ppermute | solution.py:350
  26.2 14.7 %collective-permute-start.6 = (bf16[768,256]{1,0:T(8,128)(2,1)S(1)}, bf16[768,256]{1,0:T(8,128)(2,1)S(1)}, u32[]{:S(2)}, u32[]{:S(2)}) collective-permute-start(bf16[768,256]{1,0:T(8,128)(2,1)S(1)} %piece_to_send.5), channel_id=1, source_target_pairs={{0,4},{4,0},{8,12},{12,8},{16,20},{20,16},{24,28},{28,24},{1,5},{5... | collective-permute-start | bytes 1179656 | tf_op jit(solution)/shard_map/ppermute | solution.py:350
  28.9 8.7 %collective-permute-start.8 = (bf16[256,256]{1,0:T(8,128)(2,1)S(1)}, bf16[256,256]{1,0:T(8,128)(2,1)S(1)}, u32[]{:S(2)}, u32[]{:S(2)}) collective-permute-start(bf16[256,256]{1,0:T(8,128)(2,1)S(1)} %get-tuple-element.159), channel_id=1, source_target_pairs={{0,16},{4,20},{8,24},{12,28},{16,0},{20,4},{24,8},{28,12},{1,17},{... | collective-permute-start | bytes 393224 | tf_op jit(solution)/shard_map/ppermute | solution.py:350
  34.7 5.9 %collective-permute-start.7 = (bf16[384,256]{1,0:T(8,128)(2,1)S(1)}, bf16[384,256]{1,0:T(8,128)(2,1)S(1)}, u32[]{:S(2)}, u32[]{:S(2)}) collective-permute-start(bf16[384,256]{1,0:T(8,128)(2,1)S(1)} %get-tuple-element.96), channel_id=1, source_target_pairs={{0,8},{4,12},{8,0},{12,4},{16,24},{20,28},{24,16},{28,20},{1,9},{5... | collective-permute-start | bytes 589832 | tf_op jit(solution)/shard_map/ppermute | solution.py:350
  36.3 12.7 %collective-permute-start.5 = (bf16[256,2048]{1,0:T(8,128)(2,1)S(1)}, bf16[256,2048]{1,0:T(8,128)(2,1)S(1)}, u32[]{:S(2)}, u32[]{:S(2)}) collective-permute-start(bf16[256,2048]{1,0:T(8,128)(2,1)S(1)} %collective-permute-done.refs_2_), channel_id=1, source_target_pairs={{0,1},{1,0},{2,3},{3,2},{4,5},{5,4},{6,7},{7,6},{8,9},{9,8},{10,11... | collective-permute-start | bytes 3145736 | tf_op jit(solution)/shard_map/ppermute | solution.py:353
  37.7 6.7 %collective-permute-start.10 = (bf16[256,256]{1,0:T(8,128)(2,1)S(1)}, bf16[256,256]{1,0:T(8,128)(2,1)S(1)}, u32[]{:S(2)}, u32[]{:S(2)}) collective-permute-start(bf16[256,256]{1,0:T(8,128)(2,1)S(1)} %add_convert_fusion.4.own_ref), channel_id=1, source_target_pairs={{0,8},{4,12},{8,0},{12,4},{16,24},{20,28},{24,16},{28,20},{1,9},{5... | collective-permute-start | bytes 393224 | tf_op jit(solution)/shard_map/ppermute | solution.py:350
  42.0 6.9 %collective-permute-start.9 = (bf16[384,256]{1,0:T(8,128)(2,1)S(1)}, bf16[384,256]{1,0:T(8,128)(2,1)S(1)}, u32[]{:S(2)}, u32[]{:S(2)}) collective-permute-start(bf16[384,256]{1,0:T(8,128)(2,1)S(1)} %get-tuple-element.105), channel_id=1, source_target_pairs={{0,8},{4,12},{8,0},{12,4},{16,24},{20,28},{24,16},{28,20},{1,9},{5... | collective-permute-start | bytes 589832 | tf_op jit(solution)/shard_map/ppermute | solution.py:350
  43.8 17.2 %collective-permute-start.12 = (bf16[1024,256]{1,0:T(8,128)(2,1)S(1)}, bf16[1024,256]{1,0:T(8,128)(2,1)S(1)}, u32[]{:S(2)}, u32[]{:S(2)}) collective-permute-start(bf16[1024,256]{1,0:T(8,128)(2,1)S(1)} %piece_to_send.6), channel_id=1, source_target_pairs={{0,4},{4,0},{8,12},{12,8},{16,20},{20,16},{24,28},{28,24},{1,5},{5... | collective-permute-start | bytes 1572872 | tf_op jit(solution)/shard_map/ppermute | solution.py:350
  44.4 11.0 %collective-permute-start.13 = (bf16[384,256]{1,0:T(8,128)(2,1)S(1)}, bf16[384,256]{1,0:T(8,128)(2,1)S(1)}, u32[]{:S(2)}, u32[]{:S(2)}) collective-permute-start(bf16[384,256]{1,0:T(8,128)(2,1)S(1)} %get-tuple-element.157), channel_id=1, source_target_pairs={{0,16},{4,20},{8,24},{12,28},{16,0},{20,4},{24,8},{28,12},{1,17},{... | collective-permute-start | bytes 589832 | tf_op jit(solution)/shard_map/ppermute | solution.py:350
  55.4 9.2 %collective-permute-start.16 = (bf16[384,256]{1,0:T(8,128)(2,1)S(1)}, bf16[384,256]{1,0:T(8,128)(2,1)S(1)}, u32[]{:S(2)}, u32[]{:S(2)}) collective-permute-start(bf16[384,256]{1,0:T(8,128)(2,1)S(1)} %add_convert_fusion.3.own_ref), channel_id=1, source_target_pairs={{0,8},{4,12},{8,0},{12,4},{16,24},{20,28},{24,16},{28,20},{1,9},{5... | collective-permute-start | bytes 589832 | tf_op jit(solution)/shard_map/ppermute | solution.py:350
  55.6 23.2 %collective-permute-start.18 = (bf16[512,256]{1,0:T(8,128)(2,1)S(1)}, bf16[512,256]{1,0:T(8,128)(2,1)S(1)}, u32[]{:S(2)}, u32[]{:S(2)}) collective-permute-start(bf16[512,256]{1,0:T(8,128)(2,1)S(1)} %join_halves.5.rest_0_), channel_id=1, source_target_pairs={{0,4},{4,0},{8,12},{12,8},{16,20},{20,16},{24,28},{28,24},{1,5},{5... | collective-permute-start | bytes 786440 | tf_op jit(solution)/shard_map/ppermute | solution.py:350
  56.4 8.7 %collective-permute-start.15 = (bf16[384,256]{1,0:T(8,128)(2,1)S(1)}, bf16[384,256]{1,0:T(8,128)(2,1)S(1)}, u32[]{:S(2)}, u32[]{:S(2)}) collective-permute-start(bf16[384,256]{1,0:T(8,128)(2,1)S(1)} %get-tuple-element.155), channel_id=1, source_target_pairs={{0,16},{4,20},{8,24},{12,28},{16,0},{20,4},{24,8},{28,12},{1,17},{... | collective-permute-start | bytes 589832 | tf_op jit(solution)/shard_map/ppermute | solution.py:350
  59.5 13.7 %collective-permute-start.11 = (bf16[1024,256]{1,0:T(8,128)(2,1)S(1)}, bf16[1024,256]{1,0:T(8,128)(2,1)S(1)}, u32[]{:S(2)}, u32[]{:S(2)}) collective-permute-start(bf16[1024,256]{1,0:T(8,128)(2,1)S(1)} %piece_to_send.7), channel_id=1, source_target_pairs={{0,4},{4,0},{8,12},{12,8},{16,20},{20,16},{24,28},{28,24},{1,5},{5... | collective-permute-start | bytes 1572872 | tf_op jit(solution)/shard_map/ppermute | solution.py:350
  62.4 9.3 %collective-permute-start.14 = (bf16[512,256]{1,0:T(8,128)(2,1)S(1)}, bf16[512,256]{1,0:T(8,128)(2,1)S(1)}, u32[]{:S(2)}, u32[]{:S(2)}) collective-permute-start(bf16[512,256]{1,0:T(8,128)(2,1)S(1)} %get-tuple-element.115), channel_id=1, source_target_pairs={{0,8},{4,12},{8,0},{12,4},{16,24},{20,28},{24,16},{28,20},{1,9},{5... | collective-permute-start | bytes 786440 | tf_op jit(solution)/shard_map/ppermute | solution.py:350
  65.1 13.6 %collective-permute-start.19 = (bf16[384,256]{1,0:T(8,128)(2,1)S(1)}, bf16[384,256]{1,0:T(8,128)(2,1)S(1)}, u32[]{:S(2)}, u32[]{:S(2)}) collective-permute-start(bf16[384,256]{1,0:T(8,128)(2,1)S(1)} %add_convert_fusion.2.own_ref), channel_id=1, source_target_pairs={{0,8},{4,12},{8,0},{12,4},{16,24},{20,28},{24,16},{28,20},{1,9},{5... | collective-permute-start | bytes 589832 | tf_op jit(solution)/shard_map/ppermute | solution.py:350
  74.6 10.4 %collective-permute-start.17 = (bf16[512,256]{1,0:T(8,128)(2,1)S(1)}, bf16[512,256]{1,0:T(8,128)(2,1)S(1)}, u32[]{:S(2)}, u32[]{:S(2)}) collective-permute-start(bf16[512,256]{1,0:T(8,128)(2,1)S(1)} %get-tuple-element.124), channel_id=1, source_target_pairs={{0,8},{4,12},{8,0},{12,4},{16,24},{20,28},{24,16},{28,20},{1,9},{5... | collective-permute-start | bytes 786440 | tf_op jit(solution)/shard_map/ppermute | solution.py:350
  75.4 16.3 %collective-permute-start.24 = (bf16[768,256]{1,0:T(8,128)(2,1)S(1)}, bf16[768,256]{1,0:T(8,128)(2,1)S(1)}, u32[]{:S(2)}, u32[]{:S(2)}) collective-permute-start(bf16[768,256]{1,0:T(8,128)(2,1)S(1)} %join_halves.6.rest_1_), channel_id=1, source_target_pairs={{0,4},{4,0},{8,12},{12,8},{16,20},{20,16},{24,28},{28,24},{1,5},{5... | collective-permute-start | bytes 1179656 | tf_op jit(solution)/shard_map/ppermute | solution.py:350
  77.1 11.9 %collective-permute-start.22 = (bf16[512,256]{1,0:T(8,128)(2,1)S(1)}, bf16[512,256]{1,0:T(8,128)(2,1)S(1)}, u32[]{:S(2)}, u32[]{:S(2)}) collective-permute-start(bf16[512,256]{1,0:T(8,128)(2,1)S(1)} %get-tuple-element.151), channel_id=1, source_target_pairs={{0,16},{4,20},{8,24},{12,28},{16,0},{20,4},{24,8},{28,12},{1,17},{... | collective-permute-start | bytes 786440 | tf_op jit(solution)/shard_map/ppermute | solution.py:350
  89.0 8.1 %collective-permute-start.23 = (bf16[512,256]{1,0:T(8,128)(2,1)S(1)}, bf16[512,256]{1,0:T(8,128)(2,1)S(1)}, u32[]{:S(2)}, u32[]{:S(2)}) collective-permute-start(bf16[512,256]{1,0:T(8,128)(2,1)S(1)} %add_convert_fusion.1.own_ref), channel_id=1, source_target_pairs={{0,8},{4,12},{8,0},{12,4},{16,24},{20,28},{24,16},{28,20},{1,9},{5... | collective-permute-start | bytes 786440 | tf_op jit(solution)/shard_map/ppermute | solution.py:350
  90.4 11.2 %collective-permute-start.21 = (bf16[768,256]{1,0:T(8,128)(2,1)S(1)}, bf16[768,256]{1,0:T(8,128)(2,1)S(1)}, u32[]{:S(2)}, u32[]{:S(2)}) collective-permute-start(bf16[768,256]{1,0:T(8,128)(2,1)S(1)} %join_halves.7.rest_2_), channel_id=1, source_target_pairs={{0,4},{4,0},{8,12},{12,8},{16,20},{20,16},{24,28},{28,24},{1,5},{5... | collective-permute-start | bytes 1179656 | tf_op jit(solution)/shard_map/ppermute | solution.py:350
  91.7 13.2 %collective-permute-start.20 = (bf16[512,256]{1,0:T(8,128)(2,1)}, bf16[512,256]{1,0:T(8,128)(2,1)S(1)}, u32[]{:S(2)}, u32[]{:S(2)}) collective-permute-start(bf16[512,256]{1,0:T(8,128)(2,1)} %get-tuple-element.153), channel_id=1, source_target_pairs={{0,16},{4,20},{8,24},{12,28},{16,0},{20,4},{24,8},{28,12},{1,17},{... | collective-permute-start | bytes 786440 | tf_op jit(solution)/shard_map/ppermute | solution.py:350
  98.2 17.9 %collective-permute-start.28 = (bf16[512,768]{1,0:T(8,128)(2,1)}, bf16[512,768]{1,0:T(8,128)(2,1)}, u32[]{:S(2)}, u32[]{:S(2)}) collective-permute-start(bf16[512,768]{1,0:T(8,128)(2,1)} %maximum_select_fusion), channel_id=1, source_target_pairs={{0,2},{4,6},{8,10},{12,14},{17,19},{21,23},{25,27},{29,31}} | collective-permute-start | bytes 2359304 | tf_op jit(solution)/shard_map/ppermute | solution.py:568
  105.0 6.8 %collective-permute-start.25 = (bf16[512,256]{1,0:T(8,128)(2,1)S(1)}, bf16[512,256]{1,0:T(8,128)(2,1)S(1)}, u32[]{:S(2)}, u32[]{:S(2)}) collective-permute-start(bf16[512,256]{1,0:T(8,128)(2,1)S(1)} %add_convert_fusion.own_ref), channel_id=1, source_target_pairs={{0,8},{4,12},{8,0},{12,4},{16,24},{20,28},{24,16},{28,20},{1,9},{5... | collective-permute-start | bytes 786440 | tf_op jit(solution)/shard_map/ppermute | solution.py:350
  105.1 14.9 %collective-permute-start.27 = (bf16[1024,256]{1,0:T(8,128)(2,1)S(1)}, bf16[1024,256]{1,0:T(8,128)(2,1)S(1)}, u32[]{:S(2)}, u32[]{:S(2)}) collective-permute-start(bf16[1024,256]{1,0:T(8,128)(2,1)S(1)} %join_halves.8.rest_3_), channel_id=1, source_target_pairs={{0,4},{4,0},{8,12},{12,8},{16,20},{20,16},{24,28},{28,24},{1,5},{5... | collective-permute-start | bytes 1572872 | tf_op jit(solution)/shard_map/ppermute | solution.py:350
  112.6 7.4 %collective-permute-start.26 = (bf16[512,256]{1,0:T(8,128)(2,1)}, bf16[512,256]{1,0:T(8,128)(2,1)}, u32[]{:S(2)}, u32[]{:S(2)}) collective-permute-start(bf16[512,256]{1,0:T(8,128)(2,1)} %dynamic-slice_select_fusion), channel_id=1, source_target_pairs={{0,2},{4,6},{8,10},{12,14},{17,19},{21,23},{25,27},{29,31}} | collective-permute-start | bytes 786440 | tf_op jit(solution)/shard_map/ppermute | solution.py:568
  115.8 14.0 %collective-permute-start.31 = (bf16[1024,256]{1,0:T(8,128)(2,1)S(1)}, bf16[1024,256]{1,0:T(8,128)(2,1)S(1)}, u32[]{:S(2)}, u32[]{:S(2)}) collective-permute-start(bf16[1024,256]{1,0:T(8,128)(2,1)S(1)} %join_halves.9.rest_4_), channel_id=1, source_target_pairs={{0,4},{4,0},{8,12},{12,8},{16,20},{20,16},{24,28},{28,24},{1,5},{5... | collective-permute-start | bytes 1572872 | tf_op jit(solution)/shard_map/ppermute | solution.py:350
  117.7 7.8 %collective-permute-start.30 = (bf16[512,768]{1,0:T(8,128)(2,1)S(1)}, bf16[512,768]{1,0:T(8,128)(2,1)S(1)}, u32[]{:S(2)}, u32[]{:S(2)}) collective-permute-start(bf16[512,768]{1,0:T(8,128)(2,1)S(1)} %add.97), channel_id=1, source_target_pairs={{0,1},{2,3},{4,5},{6,7},{8,9},{10,11},{12,13},{14,15},{17,16},{19,... | collective-permute-start | bytes 2359304 | tf_op jit(solution)/shard_map/ppermute | solution.py:568
  121.1 7.6 %collective-permute-start.29 = (bf16[512,256]{1,0:T(8,128)(2,1)S(1)}, bf16[512,256]{1,0:T(8,128)(2,1)S(1)}, u32[]{:S(2)}, u32[]{:S(2)}) collective-permute-start(bf16[512,256]{1,0:T(8,128)(2,1)S(1)} %add.98), channel_id=1, source_target_pairs={{0,1},{2,3},{4,5},{6,7},{8,9},{10,11},{12,13},{14,15},{17,16},{19,... | collective-permute-start | bytes 786440 | tf_op jit(solution)/shard_map/ppermute | solution.py:568
  (15 other events, 60.1 us)

commit v4 on v3

--- a/solution.py
+++ b/solution.py
@@ -11,12 +11,13 @@
 LANES = 128
 MIB = 1 << 20
 LIMIT, LIMIT_FIRST, LIMIT_REST = 10 * MIB, 54 * MIB, 50 * MIB
-SEND_US, SUM_US, JOIN_US, REST_US, TAIL_US = 2.00, 2.00, 1.00, 26.64, 0.92
+SEND_US, SUM_US, JOIN_US, REST_US, TAIL_US = 2.00, 0.54, 1.00, 26.64, 0.92
 IN_VMEM = pl.BlockSpec(memory_space=pltpu.VMEM)
 IN_HBM = pl.BlockSpec(memory_space=pltpu.HBM)
 PIECES = ((2, 3, 3), (4, 4))
-UNIT, HOP, STEP, FAR, SLAB, AHEAD = 2.85, 2.00, 1.50, 17.72, 88.61, 99.00
-SHIFT = {'send': -1.5, 'sum': 0.0, 'far': 0.0, 'back': 0.0, 'join': 0.0, 'other': 0.0, 'trail': 0.0}
+UNIT, HOP, STEP, FAR, SLAB, AHEAD = 2.85, 2.00, 1.50, 17.72, 83.09, 99.00
+KEPT = 6.00
+SHIFT = {'send': -1.5, 'sum': 1.32, 'far': 0.0, 'back': 0.0, 'join': 0.0, 'other': 0.0, 'trail': 0.0}
 BATCHES = ((0, 1, 2), (3,))
 
 
@@ -456,7 +457,7 @@
         rows = columns[0] if len(columns) == 1 else jnp.concatenate(columns, axis=1)
         return jnp.where(source == r, rows, jnp.zeros_like(rows))
 
-    steps, free = [(FAR, 0, "heads"), (SLAB, 0, "slab")], {}
+    steps, free = [(FAR, 0, "heads"), (SLAB, 0, "slab"), (KEPT, 0, "kept")], {}
 
     def send_over(link, ready, size):
         begin = max(ready, free.get(link, 0.0))
@@ -507,13 +508,18 @@
 
     state, mine, others = [None] * count, [None] * count, [None] * count
     trailing = [None] * len(batches)
-    rest = (3, 0, 2)
-    scaled.update(zip(rest, scaled_quarters(order, rest, border, after(weights))))
-    done(*(scaled[position] for position in rest))
+    def scale(*positions):
+        scaled.update(zip(positions, scaled_quarters(order, positions, border, after(weights))))
+        done(*(scaled[position] for position in positions))
+
+    scale(3)
 
     for _, k, name in steps:
         if name in ("send", "sum"):
             both = [scaled[2 * half + (name == "send")] for half in (0, 1)]
+        if name == "kept":
+            scale(0, 2)
+            continue
         if name == "send" and k == 0:
             state[k] = over_scen(first_send, 1)
         elif name == "send":

time: 135 us -> 126 us (0.933)
  starting transfers between devices: 47.6 us -> 42.1 us
  local copies, waits for them, and re-layouts: 9.52 us -> 6.94 us
  other arithmetic: 7.97 us -> 6.29 us
    ppermute x25, starting transfers between devices: 35.4 us -> 31.2 us  [body(): lax.ppermute(value.astype(bf16), 'scen', [(i, i ^ mask) for i in range(sc...]
    unnamed x30 -> x28, local copies, waits for them, and re-layouts: 9.42 us -> 6.83 us
    pallas_call x1 -> x2, Pallas kernels: 5.47 us -> 6.39 us  [scaled_quarters(): pl.pallas_call(functools.partial(scale_kernel, positions, parts), in_spec...]
  transfers between devices with their start and end apart: 32 -> 32, of which waited for: 16 -> 15; matrix products, arithmetic and copies ran while one was open for 6% -> 5% of each run, Pallas kernels for 14% -> 16%
where the time goes in v4:
time: 126 us
  starting transfers between devices  42.1 us (33%)
  waiting for transfers between devices  41.1 us (33%)
  Pallas kernels  28.8 us (23%)
  local copies, waits for them, and re-layouts  6.94 us (6%)
  other arithmetic  6.29 us (5%)
    ppermute x25, waiting for transfers between devices, body(): lax.ppermute(value.astype(bf16), 'scen', [(i, i ^ mask) for i in range(sc...  41.1 us
    ppermute x25, starting transfers between devices, body(): lax.ppermute(value.astype(bf16), 'scen', [(i, i ^ mask) for i in range(sc...  31.2 us
    ppermute x4, starting transfers between devices, body(): trailing[k] = (rows, lax.ppermute(rows, ('scen', 'row'), spread[t]))  7.9 us
    unnamed x28, local copies, waits for them, and re-layouts  6.83 us
    pallas_call x2, Pallas kernels, scaled_quarters(): pl.pallas_call(functools.partial(scale_kernel, positions, parts), in_spec...  6.39 us
    pallas_call x5, Pallas kernels, piece_sum(): pl.pallas_call(functools.partial(sum_kernel, runs), in_specs=[pl.BlockSpe...  5.61 us
    pallas_call x4, Pallas kernels, piece_to_send(): pl.pallas_call(functools.partial(send_kernel, runs), in_specs=[IN_VMEM] *...  4.59 us
    pallas_call x1, Pallas kernels, first_step(): pl.pallas_call(functools.partial(first_kernel, parts), grid=(1,), in_spec...  4.57 us
  transfers between devices with their start and end apart: 32, of which 15 were waited for; matrix products, arithmetic and copies ran while one was open for 5% of the time, Pallas kernels for 16%

profile of v4, /device:TPU:0, one launch (start us, length us, event | category | flops | bytes accessed | tf_op | source)
XLA Modules:
  0.0 125.9 jit_solution(15226052987558187461)
XLA Ops:
  0.6 4.6 %first_step.1 = (f32[16,128]{1,0:T(8,128)}, bf16[256,2048]{1,0:T(8,128)(2,1)}, bf16[512,2048]{1,0:T(8,128)(2,1)}, bf16[512,256]{1,0:T(8,128)(2,1)}) custom-call(s32[1]{0:T(128)} %bitcast.5.place_ref, s32[8]{0:T(128)} %counts_ref.1, s32[4]{0:T(128)} %pad_add_fusion.1.order_ref, s32[16,128]{1,0:T(8,128)} %index_ref.1, f32[32,128]{1,0:T(8,128)} %bitcast.19, ...), custom_call_target="tpu_custom_call" | custom-call | flops 26639998976 | bytes 53280000 | tf_op jit(solution)/shard_map/first_step/pallas_call | solution.py:93
  5.2 3.0 %collective-permute-start.4 = (bf16[256,2048]{1,0:T(8,128)(2,1)}, bf16[256,2048]{1,0:T(8,128)(2,1)S(1)}, u32[]{:S(2)}, u32[]{:S(2)}) collective-permute-start(bf16[256,2048]{1,0:T(8,128)(2,1)} %get-tuple-element.82.refs_2_), channel_id=1, source_target_pairs={{0,2},{1,3},{2,0},{3,1},{4,6},{5,7},{6,4},{7,5},{8,10},{9,11},{10,... | collective-permute-start | bytes 3145736 | tf_op jit(solution)/shard_map/ppermute | solution.py:354
  8.2 1.5 %collective-permute-start.1 = (bf16[512,256]{1,0:T(8,128)(2,1)}, bf16[512,256]{1,0:T(8,128)(2,1)S(1)}, u32[]{:S(2)}, u32[]{:S(2)}) collective-permute-start(bf16[512,256]{1,0:T(8,128)(2,1)} %get-tuple-element.87), channel_id=1, source_target_pairs={{0,4},{4,0},{8,12},{12,8},{16,20},{20,16},{24,28},{28,24},{1,5},{5... | collective-permute-start | bytes 786440 | tf_op jit(solution)/shard_map/ppermute | solution.py:351
  10.4 2.2 %scaled_quarters.2.refs_1_ = bf16[512,2048]{1,0:T(8,128)(2,1)S(1)} custom-call(s32[4]{0:T(128)S(1)} %copy-done.4, bf16[16,2048,128]{2,1,0:T(8,128)(2,1)} %border_ref.5, f32[16,128]{1,0:T(8,128)S(1)} %copy-done.11), custom_call_target="tpu_custom_call" | custom-call | flops 26639998976 | bytes 53280000 | tf_op jit(solution)/shard_map/scaled_quarters/pallas_call | solution.py:140
  13.9 1.6 %copy-done.6 = bf16[512,2048]{1,0:T(8,128)(2,1)S(1)} copy-done((bf16[512,2048]{1,0:T(8,128)(2,1)S(1)}, bf16[512,2048]{1,0:T(8,128)(2,1)}, u32[]{:S(2)}) %copy-start.6) | copy-done | bytes 2097176
  15.5 1.6 %copy-done.9 = bf16[512,2048]{1,0:T(8,128)(2,1)S(1)} copy-done((bf16[512,2048]{1,0:T(8,128)(2,1)S(1)}, bf16[512,2048]{1,0:T(8,128)(2,1)}, u32[]{:S(2)}) %copy-start.9) | copy-done | bytes 2097176
  18.8 4.2 %scaled_quarters.3 = (bf16[512,2048]{1,0:T(8,128)(2,1)S(1)}, bf16[512,2048]{1,0:T(8,128)(2,1)}) custom-call(s32[4]{0:T(128)S(1)} %copy-done.4, bf16[16,2048,128]{2,1,0:T(8,128)(2,1)} %border_ref.5, f32[16,128]{1,0:T(8,128)S(1)} %copy-done.12), custom_call_target="tpu_custom_call" | custom-call | flops 26639998976 | bytes 53280000 | tf_op jit(solution)/shard_map/scaled_quarters/pallas_call | solution.py:140
  23.0 1.6 %copy-done = bf16[512,2048]{1,0:T(8,128)(2,1)S(1)} copy-done((bf16[512,2048]{1,0:T(8,128)(2,1)S(1)}, bf16[512,2048]{1,0:T(8,128)(2,1)}, u32[]{:S(2)}) %copy-start) | copy-done | bytes 2097176
  25.4 1.6 %collective-permute-start.2 = (bf16[256,256]{1,0:T(8,128)(2,1)S(1)}, bf16[256,256]{1,0:T(8,128)(2,1)S(1)}, u32[]{:S(2)}, u32[]{:S(2)}) collective-permute-start(bf16[256,256]{1,0:T(8,128)(2,1)S(1)} %get-tuple-element.90), channel_id=1, source_target_pairs={{0,8},{4,12},{8,0},{12,4},{16,24},{20,28},{24,16},{28,20},{1,9},{5... | collective-permute-start | bytes 393224 | tf_op jit(solution)/shard_map/ppermute | solution.py:351
  28.0 1.6 %collective-permute-start.7 = (bf16[768,256]{1,0:T(8,128)(2,1)S(1)}, bf16[768,256]{1,0:T(8,128)(2,1)S(1)}, u32[]{:S(2)}, u32[]{:S(2)}) collective-permute-start(bf16[768,256]{1,0:T(8,128)(2,1)S(1)} %piece_to_send.5), channel_id=1, source_target_pairs={{0,4},{4,0},{8,12},{12,8},{16,20},{20,16},{24,28},{28,24},{1,5},{5... | collective-permute-start | bytes 1179656 | tf_op jit(solution)/shard_map/ppermute | solution.py:351
  30.8 2.6 %collective-permute-start.3 = (bf16[256,256]{1,0:T(8,128)(2,1)S(1)}, bf16[256,256]{1,0:T(8,128)(2,1)S(1)}, u32[]{:S(2)}, u32[]{:S(2)}) collective-permute-start(bf16[256,256]{1,0:T(8,128)(2,1)S(1)} %get-tuple-element.159), channel_id=1, source_target_pairs={{0,16},{4,20},{8,24},{12,28},{16,0},{20,4},{24,8},{28,12},{1,17},{... | collective-permute-start | bytes 393224 | tf_op jit(solution)/shard_map/ppermute | solution.py:351
  34.5 1.6 %collective-permute-start.8 = (bf16[384,256]{1,0:T(8,128)(2,1)S(1)}, bf16[384,256]{1,0:T(8,128)(2,1)S(1)}, u32[]{:S(2)}, u32[]{:S(2)}) collective-permute-start(bf16[384,256]{1,0:T(8,128)(2,1)S(1)} %get-tuple-element.96), channel_id=1, source_target_pairs={{0,8},{4,12},{8,0},{12,4},{16,24},{20,28},{24,16},{28,20},{1,9},{5... | collective-permute-start | bytes 589832 | tf_op jit(solution)/shard_map/ppermute | solution.py:351
  39.9 3.0 %collective-permute-done.8 = bf16[384,256]{1,0:T(8,128)(2,1)S(1)} collective-permute-done((bf16[384,256]{1,0:T(8,128)(2,1)S(1)}, bf16[384,256]{1,0:T(8,128)(2,1)S(1)}, u32[]{:S(2)}, u32[]{:S(2)}) %collective-permute-start.8) | collective-permute-done | bytes 196640 | tf_op jit(solution)/shard_map/ppermute | solution.py:351
  44.4 1.5 %collective-permute-start.13 = (bf16[1024,256]{1,0:T(8,128)(2,1)S(1)}, bf16[1024,256]{1,0:T(8,128)(2,1)S(1)}, u32[]{:S(2)}, u32[]{:S(2)}) collective-permute-start(bf16[1024,256]{1,0:T(8,128)(2,1)S(1)} %piece_to_send.6), channel_id=1, source_target_pairs={{0,4},{4,0},{8,12},{12,8},{16,20},{20,16},{24,28},{28,24},{1,5},{5... | collective-permute-start | bytes 1572872 | tf_op jit(solution)/shard_map/ppermute | solution.py:351
  45.9 1.7 %collective-permute-start.9 = (bf16[384,256]{1,0:T(8,128)(2,1)S(1)}, bf16[384,256]{1,0:T(8,128)(2,1)S(1)}, u32[]{:S(2)}, u32[]{:S(2)}) collective-permute-start(bf16[384,256]{1,0:T(8,128)(2,1)S(1)} %get-tuple-element.157), channel_id=1, source_target_pairs={{0,16},{4,20},{8,24},{12,28},{16,0},{20,4},{24,8},{28,12},{1,17},{... | collective-permute-start | bytes 589832 | tf_op jit(solution)/shard_map/ppermute | solution.py:351
  47.6 4.7 %collective-permute-done.11 = bf16[384,256]{1,0:T(8,128)(2,1)S(1)} collective-permute-done((bf16[384,256]{1,0:T(8,128)(2,1)S(1)}, bf16[384,256]{1,0:T(8,128)(2,1)S(1)}, u32[]{:S(2)}, u32[]{:S(2)}) %collective-permute-start.11) | collective-permute-done | bytes 196640 | tf_op jit(solution)/shard_map/ppermute | solution.py:351
  53.7 2.2 %collective-permute-done.9 = bf16[384,256]{1,0:T(8,128)(2,1)S(1)} collective-permute-done((bf16[384,256]{1,0:T(8,128)(2,1)S(1)}, bf16[384,256]{1,0:T(8,128)(2,1)S(1)}, u32[]{:S(2)}, u32[]{:S(2)}) %collective-permute-start.9) | collective-permute-done | bytes 196640 | tf_op jit(solution)/shard_map/ppermute | solution.py:351
  56.0 2.8 %collective-permute-start.14 = (bf16[384,256]{1,0:T(8,128)(2,1)S(1)}, bf16[384,256]{1,0:T(8,128)(2,1)S(1)}, u32[]{:S(2)}, u32[]{:S(2)}) collective-permute-start(bf16[384,256]{1,0:T(8,128)(2,1)S(1)} %get-tuple-element.155), channel_id=1, source_target_pairs={{0,16},{4,20},{8,24},{12,28},{16,0},{20,4},{24,8},{28,12},{1,17},{... | collective-permute-start | bytes 589832 | tf_op jit(solution)/shard_map/ppermute | solution.py:351
  62.4 4.5 %collective-permute-done.12.got_ref = bf16[384,256]{1,0:T(8,128)(2,1)S(1)} collective-permute-done((bf16[384,256]{1,0:T(8,128)(2,1)S(1)}, bf16[384,256]{1,0:T(8,128)(2,1)S(1)}, u32[]{:S(2)}, u32[]{:S(2)}) %collective-permute-start.12) | collective-permute-done | bytes 196640 | tf_op jit(solution)/shard_map/ppermute | solution.py:351
  68.0 4.2 %collective-permute-done.17 = bf16[512,256]{1,0:T(8,128)(2,1)S(1)} collective-permute-done((bf16[512,256]{1,0:T(8,128)(2,1)S(1)}, bf16[512,256]{1,0:T(8,128)(2,1)S(1)}, u32[]{:S(2)}, u32[]{:S(2)}) %collective-permute-start.17) | collective-permute-done | bytes 262176 | tf_op jit(solution)/shard_map/ppermute | solution.py:351
  74.4 2.1 %collective-permute-start.19 = (bf16[512,256]{1,0:T(8,128)(2,1)S(1)}, bf16[512,256]{1,0:T(8,128)(2,1)S(1)}, u32[]{:S(2)}, u32[]{:S(2)}) collective-permute-start(bf16[512,256]{1,0:T(8,128)(2,1)S(1)} %get-tuple-element.124), channel_id=1, source_target_pairs={{0,8},{4,12},{8,0},{12,4},{16,24},{20,28},{24,16},{28,20},{1,9},{5... | collective-permute-start | bytes 786440 | tf_op jit(solution)/shard_map/ppermute | solution.py:351
  79.1 4.4 %collective-permute-done.19 = bf16[512,256]{1,0:T(8,128)(2,1)S(1)} collective-permute-done((bf16[512,256]{1,0:T(8,128)(2,1)S(1)}, bf16[512,256]{1,0:T(8,128)(2,1)S(1)}, u32[]{:S(2)}, u32[]{:S(2)}) %collective-permute-start.19) | collective-permute-done | bytes 262176 | tf_op jit(solution)/shard_map/ppermute | solution.py:351
  84.4 3.7 %collective-permute-done.18 = bf16[512,256]{1,0:T(8,128)(2,1)S(1)} collective-permute-done((bf16[512,256]{1,0:T(8,128)(2,1)S(1)}, bf16[512,256]{1,0:T(8,128)(2,1)S(1)}, u32[]{:S(2)}, u32[]{:S(2)}) %collective-permute-start.18) | collective-permute-done | bytes 262176 | tf_op jit(solution)/shard_map/ppermute | solution.py:351
  89.3 1.6 %collective-permute-start.25 = (bf16[768,256]{1,0:T(8,128)(2,1)S(1)}, bf16[768,256]{1,0:T(8,128)(2,1)S(1)}, u32[]{:S(2)}, u32[]{:S(2)}) collective-permute-start(bf16[768,256]{1,0:T(8,128)(2,1)S(1)} %join_halves.7.rest_2_), channel_id=1, source_target_pairs={{0,4},{4,0},{8,12},{12,8},{16,20},{20,16},{24,28},{28,24},{1,5},{5... | collective-permute-start | bytes 1179656 | tf_op jit(solution)/shard_map/ppermute | solution.py:351
  92.5 3.7 %collective-permute-done.21.got_ref = bf16[512,256]{1,0:T(8,128)(2,1)S(1)} collective-permute-done((bf16[512,256]{1,0:T(8,128)(2,1)S(1)}, bf16[512,256]{1,0:T(8,128)(2,1)S(1)}, u32[]{:S(2)}, u32[]{:S(2)}) %collective-permute-start.21) | collective-permute-done | bytes 262176 | tf_op jit(solution)/shard_map/ppermute | solution.py:351
  97.3 3.3 %collective-permute-start.23 = (bf16[512,768]{1,0:T(8,128)(2,1)}, bf16[512,768]{1,0:T(8,128)(2,1)}, u32[]{:S(2)}, u32[]{:S(2)}) collective-permute-start(bf16[512,768]{1,0:T(8,128)(2,1)} %maximum_select_fusion), channel_id=1, source_target_pairs={{0,2},{4,6},{8,10},{12,14},{17,19},{21,23},{25,27},{29,31}} | collective-permute-start | bytes 2359304 | tf_op jit(solution)/shard_map/ppermute | solution.py:574
  101.7 2.4 %collective-permute-start.28 = (bf16[1024,256]{1,0:T(8,128)(2,1)S(1)}, bf16[1024,256]{1,0:T(8,128)(2,1)S(1)}, u32[]{:S(2)}, u32[]{:S(2)}) collective-permute-start(bf16[1024,256]{1,0:T(8,128)(2,1)S(1)} %join_halves.8.rest_3_), channel_id=1, source_target_pairs={{0,4},{4,0},{8,12},{12,8},{16,20},{20,16},{24,28},{28,24},{1,5},{5... | collective-permute-start | bytes 1572872 | tf_op jit(solution)/shard_map/ppermute | solution.py:351
  104.1 4.0 %collective-permute-done.26.got_ref = bf16[512,256]{1,0:T(8,128)(2,1)S(1)} collective-permute-done((bf16[512,256]{1,0:T(8,128)(2,1)S(1)}, bf16[512,256]{1,0:T(8,128)(2,1)S(1)}, u32[]{:S(2)}, u32[]{:S(2)}) %collective-permute-start.26) | collective-permute-done | bytes 262176 | tf_op jit(solution)/shard_map/ppermute | solution.py:351
  109.2 2.0 %collective-permute-start.27 = (bf16[512,256]{1,0:T(8,128)(2,1)S(1)}, bf16[512,256]{1,0:T(8,128)(2,1)S(1)}, u32[]{:S(2)}, u32[]{:S(2)}) collective-permute-start(bf16[512,256]{1,0:T(8,128)(2,1)S(1)} %dynamic-slice_select_fusion), channel_id=1, source_target_pairs={{0,2},{4,6},{8,10},{12,14},{17,19},{21,23},{25,27},{29,31}} | collective-permute-start | bytes 786440 | tf_op jit(solution)/shard_map/ppermute | solution.py:574
  111.1 1.6 %add.97 = bf16[512,768]{1,0:T(8,128)(2,1)S(1)} add(bf16[512,768]{1,0:T(8,128)(2,1)} %maximum_select_fusion, bf16[512,768]{1,0:T(8,128)(2,1)} %collective-permute-done.23) | non-fusion elementwise | flops 393216 | bytes 2359296 | tf_op jit(solution)/shard_map/add | solution.py:570
  117.8 1.6 %factor.2.refs_3_ = f32[1024,512]{1,0:T(8,128)S(1)} custom-call(s32[2,4]{1,0:T(2,128)S(1)} %pad_add_fusion.refs_0_, bf16[1024,1024]{1,0:T(8,128)(2,1)S(1)} %copy-done.2, bf16[512,768]{1,0:T(8,128)(2,1)S(1)} %add.99.refs_2_), custom_call_target="tpu_custom_call" | custom-call | flops 920000000 | bytes 1840000 | tf_op jit(solution)/shard_map/factor/pallas_call | solution.py:287
  121.7 4.0 %update.1 = f32[2048,512]{1,0:T(8,128)} custom-call(s32[4]{0:T(128)S(1)} %copy-done.4, f32[4,512,512]{2,1,0:T(8,128)S(1)} %held_slab.1.slab_ref, bf16[1024,512]{1,0:T(8,128)(2,1)S(1)} %factor.3.factor_ref, bf16[512,256]{1,0:T(8,128)(2,1)S(1)} %join_halves.5.rest_0_, bf16[768,256]{1,0:T(8,128)(2,1)S(1)} %join_halves.6.rest_1_, ...), custom_call_target="tpu_custom_call" | custom-call | flops 920000000 | bytes 1840000 | tf_op jit(solution)/shard_map/update/pallas_call | solution.py:323
  (105 shorter events, 38.7 us)
Async XLA Ops:
  5.2 31.0 %collective-permute-start.4 = (bf16[256,2048]{1,0:T(8,128)(2,1)}, bf16[256,2048]{1,0:T(8,128)(2,1)S(1)}, u32[]{:S(2)}, u32[]{:S(2)}) collective-permute-start(bf16[256,2048]{1,0:T(8,128)(2,1)} %get-tuple-element.82.refs_2_), channel_id=1, source_target_pairs={{0,2},{1,3},{2,0},{3,1},{4,6},{5,7},{6,4},{7,5},{8,10},{9,11},{10,... | collective-permute-start | bytes 3145736 | tf_op jit(solution)/shard_map/ppermute | solution.py:354
  8.2 5.7 %collective-permute-start = (bf16[256,2048]{1,0:T(8,128)(2,1)}, bf16[256,2048]{1,0:T(8,128)(2,1)S(1)}, u32[]{:S(2)}, u32[]{:S(2)}) collective-permute-start(bf16[256,2048]{1,0:T(8,128)(2,1)} %get-tuple-element.82.refs_2_), channel_id=1, source_target_pairs={{0,1},{1,0},{2,3},{3,2},{4,5},{5,4},{6,7},{7,6},{8,9},{9,8},{10,11... | collective-permute-start | bytes 3145736 | tf_op jit(solution)/shard_map/ppermute | solution.py:354
  8.2 14.8 %collective-permute-start.1 = (bf16[512,256]{1,0:T(8,128)(2,1)}, bf16[512,256]{1,0:T(8,128)(2,1)S(1)}, u32[]{:S(2)}, u32[]{:S(2)}) collective-permute-start(bf16[512,256]{1,0:T(8,128)(2,1)} %get-tuple-element.87), channel_id=1, source_target_pairs={{0,4},{4,0},{8,12},{12,8},{16,20},{20,16},{24,28},{28,24},{1,5},{5... | collective-permute-start | bytes 786440 | tf_op jit(solution)/shard_map/ppermute | solution.py:351
  18.1 15.3 %collective-permute-start.5 = (bf16[768,256]{1,0:T(8,128)(2,1)S(1)}, bf16[768,256]{1,0:T(8,128)(2,1)S(1)}, u32[]{:S(2)}, u32[]{:S(2)}) collective-permute-start(bf16[768,256]{1,0:T(8,128)(2,1)S(1)} %piece_to_send.4), channel_id=1, source_target_pairs={{0,4},{4,0},{8,12},{12,8},{16,20},{20,16},{24,28},{28,24},{1,5},{5... | collective-permute-start | bytes 1179656 | tf_op jit(solution)/shard_map/ppermute | solution.py:351
  25.4 5.4 %collective-permute-start.2 = (bf16[256,256]{1,0:T(8,128)(2,1)S(1)}, bf16[256,256]{1,0:T(8,128)(2,1)S(1)}, u32[]{:S(2)}, u32[]{:S(2)}) collective-permute-start(bf16[256,256]{1,0:T(8,128)(2,1)S(1)} %get-tuple-element.90), channel_id=1, source_target_pairs={{0,8},{4,12},{8,0},{12,4},{16,24},{20,28},{24,16},{28,20},{1,9},{5... | collective-permute-start | bytes 393224 | tf_op jit(solution)/shard_map/ppermute | solution.py:351
  28.0 14.9 %collective-permute-start.7 = (bf16[768,256]{1,0:T(8,128)(2,1)S(1)}, bf16[768,256]{1,0:T(8,128)(2,1)S(1)}, u32[]{:S(2)}, u32[]{:S(2)}) collective-permute-start(bf16[768,256]{1,0:T(8,128)(2,1)S(1)} %piece_to_send.5), channel_id=1, source_target_pairs={{0,4},{4,0},{8,12},{12,8},{16,20},{20,16},{24,28},{28,24},{1,5},{5... | collective-permute-start | bytes 1179656 | tf_op jit(solution)/shard_map/ppermute | solution.py:351
  30.8 8.1 %collective-permute-start.3 = (bf16[256,256]{1,0:T(8,128)(2,1)S(1)}, bf16[256,256]{1,0:T(8,128)(2,1)S(1)}, u32[]{:S(2)}, u32[]{:S(2)}) collective-permute-start(bf16[256,256]{1,0:T(8,128)(2,1)S(1)} %get-tuple-element.159), channel_id=1, source_target_pairs={{0,16},{4,20},{8,24},{12,28},{16,0},{20,4},{24,8},{28,12},{1,17},{... | collective-permute-start | bytes 393224 | tf_op jit(solution)/shard_map/ppermute | solution.py:351
  34.5 8.3 %collective-permute-start.8 = (bf16[384,256]{1,0:T(8,128)(2,1)S(1)}, bf16[384,256]{1,0:T(8,128)(2,1)S(1)}, u32[]{:S(2)}, u32[]{:S(2)}) collective-permute-start(bf16[384,256]{1,0:T(8,128)(2,1)S(1)} %get-tuple-element.96), channel_id=1, source_target_pairs={{0,8},{4,12},{8,0},{12,4},{16,24},{20,28},{24,16},{28,20},{1,9},{5... | collective-permute-start | bytes 589832 | tf_op jit(solution)/shard_map/ppermute | solution.py:351
  36.2 16.2 %collective-permute-start.10 = (bf16[256,2048]{1,0:T(8,128)(2,1)S(1)}, bf16[256,2048]{1,0:T(8,128)(2,1)S(1)}, u32[]{:S(2)}, u32[]{:S(2)}) collective-permute-start(bf16[256,2048]{1,0:T(8,128)(2,1)S(1)} %collective-permute-done.4.refs_2_), channel_id=1, source_target_pairs={{0,1},{1,0},{2,3},{3,2},{4,5},{5,4},{6,7},{7,6},{8,9},{9,8},{10,11... | collective-permute-start | bytes 3145736 | tf_op jit(solution)/shard_map/ppermute | solution.py:354
  39.0 6.9 %collective-permute-start.6 = (bf16[256,256]{1,0:T(8,128)(2,1)S(1)}, bf16[256,256]{1,0:T(8,128)(2,1)S(1)}, u32[]{:S(2)}, u32[]{:S(2)}) collective-permute-start(bf16[256,256]{1,0:T(8,128)(2,1)S(1)} %add_convert_fusion.4.own_ref), channel_id=1, source_target_pairs={{0,8},{4,12},{8,0},{12,4},{16,24},{20,28},{24,16},{28,20},{1,9},{5... | collective-permute-start | bytes 393224 | tf_op jit(solution)/shard_map/ppermute | solution.py:351
  44.0 8.3 %collective-permute-start.11 = (bf16[384,256]{1,0:T(8,128)(2,1)S(1)}, bf16[384,256]{1,0:T(8,128)(2,1)S(1)}, u32[]{:S(2)}, u32[]{:S(2)}) collective-permute-start(bf16[384,256]{1,0:T(8,128)(2,1)S(1)} %get-tuple-element.105), channel_id=1, source_target_pairs={{0,8},{4,12},{8,0},{12,4},{16,24},{20,28},{24,16},{28,20},{1,9},{5... | collective-permute-start | bytes 589832 | tf_op jit(solution)/shard_map/ppermute | solution.py:351
  44.4 16.5 %collective-permute-start.13 = (bf16[1024,256]{1,0:T(8,128)(2,1)S(1)}, bf16[1024,256]{1,0:T(8,128)(2,1)S(1)}, u32[]{:S(2)}, u32[]{:S(2)}) collective-permute-start(bf16[1024,256]{1,0:T(8,128)(2,1)S(1)} %piece_to_send.6), channel_id=1, source_target_pairs={{0,4},{4,0},{8,12},{12,8},{16,20},{20,16},{24,28},{28,24},{1,5},{5... | collective-permute-start | bytes 1572872 | tf_op jit(solution)/shard_map/ppermute | solution.py:351
  45.9 10.0 %collective-permute-start.9 = (bf16[384,256]{1,0:T(8,128)(2,1)S(1)}, bf16[384,256]{1,0:T(8,128)(2,1)S(1)}, u32[]{:S(2)}, u32[]{:S(2)}) collective-permute-start(bf16[384,256]{1,0:T(8,128)(2,1)S(1)} %get-tuple-element.157), channel_id=1, source_target_pairs={{0,16},{4,20},{8,24},{12,28},{16,0},{20,4},{24,8},{28,12},{1,17},{... | collective-permute-start | bytes 589832 | tf_op jit(solution)/shard_map/ppermute | solution.py:351
  55.9 10.9 %collective-permute-start.12 = (bf16[384,256]{1,0:T(8,128)(2,1)S(1)}, bf16[384,256]{1,0:T(8,128)(2,1)S(1)}, u32[]{:S(2)}, u32[]{:S(2)}) collective-permute-start(bf16[384,256]{1,0:T(8,128)(2,1)S(1)} %add_convert_fusion.3.own_ref), channel_id=1, source_target_pairs={{0,8},{4,12},{8,0},{12,4},{16,24},{20,28},{24,16},{28,20},{1,9},{5... | collective-permute-start | bytes 589832 | tf_op jit(solution)/shard_map/ppermute | solution.py:351
  56.0 10.9 %collective-permute-start.14 = (bf16[384,256]{1,0:T(8,128)(2,1)S(1)}, bf16[384,256]{1,0:T(8,128)(2,1)S(1)}, u32[]{:S(2)}, u32[]{:S(2)}) collective-permute-start(bf16[384,256]{1,0:T(8,128)(2,1)S(1)} %get-tuple-element.155), channel_id=1, source_target_pairs={{0,16},{4,20},{8,24},{12,28},{16,0},{20,4},{24,8},{28,12},{1,17},{... | collective-permute-start | bytes 589832 | tf_op jit(solution)/shard_map/ppermute | solution.py:351
  58.8 20.3 %collective-permute-start.20 = (bf16[512,256]{1,0:T(8,128)(2,1)S(1)}, bf16[512,256]{1,0:T(8,128)(2,1)S(1)}, u32[]{:S(2)}, u32[]{:S(2)}) collective-permute-start(bf16[512,256]{1,0:T(8,128)(2,1)S(1)} %join_halves.5.rest_0_), channel_id=1, source_target_pairs={{0,4},{4,0},{8,12},{12,8},{16,20},{20,16},{24,28},{28,24},{1,5},{5... | collective-permute-start | bytes 786440 | tf_op jit(solution)/shard_map/ppermute | solution.py:351
  60.2 12.9 %collective-permute-start.16 = (bf16[1024,256]{1,0:T(8,128)(2,1)S(1)}, bf16[1024,256]{1,0:T(8,128)(2,1)S(1)}, u32[]{:S(2)}, u32[]{:S(2)}) collective-permute-start(bf16[1024,256]{1,0:T(8,128)(2,1)S(1)} %piece_to_send.7), channel_id=1, source_target_pairs={{0,4},{4,0},{8,12},{12,8},{16,20},{20,16},{24,28},{28,24},{1,5},{5... | collective-permute-start | bytes 1572872 | tf_op jit(solution)/shard_map/ppermute | solution.py:351
  62.2 10.0 %collective-permute-start.17 = (bf16[512,256]{1,0:T(8,128)(2,1)S(1)}, bf16[512,256]{1,0:T(8,128)(2,1)S(1)}, u32[]{:S(2)}, u32[]{:S(2)}) collective-permute-start(bf16[512,256]{1,0:T(8,128)(2,1)S(1)} %get-tuple-element.115), channel_id=1, source_target_pairs={{0,8},{4,12},{8,0},{12,4},{16,24},{20,28},{24,16},{28,20},{1,9},{5... | collective-permute-start | bytes 786440 | tf_op jit(solution)/shard_map/ppermute | solution.py:351
  67.0 12.1 %collective-permute-start.15 = (bf16[384,256]{1,0:T(8,128)(2,1)S(1)}, bf16[384,256]{1,0:T(8,128)(2,1)S(1)}, u32[]{:S(2)}, u32[]{:S(2)}) collective-permute-start(bf16[384,256]{1,0:T(8,128)(2,1)S(1)} %add_convert_fusion.2.own_ref), channel_id=1, source_target_pairs={{0,8},{4,12},{8,0},{12,4},{16,24},{20,28},{24,16},{28,20},{1,9},{5... | collective-permute-start | bytes 589832 | tf_op jit(solution)/shard_map/ppermute | solution.py:351
  74.4 9.0 %collective-permute-start.19 = (bf16[512,256]{1,0:T(8,128)(2,1)S(1)}, bf16[512,256]{1,0:T(8,128)(2,1)S(1)}, u32[]{:S(2)}, u32[]{:S(2)}) collective-permute-start(bf16[512,256]{1,0:T(8,128)(2,1)S(1)} %get-tuple-element.124), channel_id=1, source_target_pairs={{0,8},{4,12},{8,0},{12,4},{16,24},{20,28},{24,16},{28,20},{1,9},{5... | collective-permute-start | bytes 786440 | tf_op jit(solution)/shard_map/ppermute | solution.py:351
  76.6 14.7 %collective-permute-start.22 = (bf16[768,256]{1,0:T(8,128)(2,1)S(1)}, bf16[768,256]{1,0:T(8,128)(2,1)S(1)}, u32[]{:S(2)}, u32[]{:S(2)}) collective-permute-start(bf16[768,256]{1,0:T(8,128)(2,1)S(1)} %join_halves.6.rest_1_), channel_id=1, source_target_pairs={{0,4},{4,0},{8,12},{12,8},{16,20},{20,16},{24,28},{28,24},{1,5},{5... | collective-permute-start | bytes 1179656 | tf_op jit(solution)/shard_map/ppermute | solution.py:351
  77.9 10.2 %collective-permute-start.18 = (bf16[512,256]{1,0:T(8,128)(2,1)S(1)}, bf16[512,256]{1,0:T(8,128)(2,1)S(1)}, u32[]{:S(2)}, u32[]{:S(2)}) collective-permute-start(bf16[512,256]{1,0:T(8,128)(2,1)S(1)} %get-tuple-element.153), channel_id=1, source_target_pairs={{0,16},{4,20},{8,24},{12,28},{16,0},{20,4},{24,8},{28,12},{1,17},{... | collective-permute-start | bytes 786440 | tf_op jit(solution)/shard_map/ppermute | solution.py:351
  88.2 8.0 %collective-permute-start.21 = (bf16[512,256]{1,0:T(8,128)(2,1)S(1)}, bf16[512,256]{1,0:T(8,128)(2,1)S(1)}, u32[]{:S(2)}, u32[]{:S(2)}) collective-permute-start(bf16[512,256]{1,0:T(8,128)(2,1)S(1)} %add_convert_fusion.1.own_ref), channel_id=1, source_target_pairs={{0,8},{4,12},{8,0},{12,4},{16,24},{20,28},{24,16},{28,20},{1,9},{5... | collective-permute-start | bytes 786440 | tf_op jit(solution)/shard_map/ppermute | solution.py:351
  89.3 11.3 %collective-permute-start.25 = (bf16[768,256]{1,0:T(8,128)(2,1)S(1)}, bf16[768,256]{1,0:T(8,128)(2,1)S(1)}, u32[]{:S(2)}, u32[]{:S(2)}) collective-permute-start(bf16[768,256]{1,0:T(8,128)(2,1)S(1)} %join_halves.7.rest_2_), channel_id=1, source_target_pairs={{0,4},{4,0},{8,12},{12,8},{16,20},{20,16},{24,28},{28,24},{1,5},{5... | collective-permute-start | bytes 1179656 | tf_op jit(solution)/shard_map/ppermute | solution.py:351
  91.3 10.3 %collective-permute-start.24 = (bf16[512,256]{1,0:T(8,128)(2,1)}, bf16[512,256]{1,0:T(8,128)(2,1)S(1)}, u32[]{:S(2)}, u32[]{:S(2)}) collective-permute-start(bf16[512,256]{1,0:T(8,128)(2,1)} %get-tuple-element.151), channel_id=1, source_target_pairs={{0,16},{4,20},{8,24},{12,28},{16,0},{20,4},{24,8},{28,12},{1,17},{... | collective-permute-start | bytes 786440 | tf_op jit(solution)/shard_map/ppermute | solution.py:351
  97.3 13.8 %collective-permute-start.23 = (bf16[512,768]{1,0:T(8,128)(2,1)}, bf16[512,768]{1,0:T(8,128)(2,1)}, u32[]{:S(2)}, u32[]{:S(2)}) collective-permute-start(bf16[512,768]{1,0:T(8,128)(2,1)} %maximum_select_fusion), channel_id=1, source_target_pairs={{0,2},{4,6},{8,10},{12,14},{17,19},{21,23},{25,27},{29,31}} | collective-permute-start | bytes 2359304 | tf_op jit(solution)/shard_map/ppermute | solution.py:574
  101.7 6.4 %collective-permute-start.26 = (bf16[512,256]{1,0:T(8,128)(2,1)S(1)}, bf16[512,256]{1,0:T(8,128)(2,1)S(1)}, u32[]{:S(2)}, u32[]{:S(2)}) collective-permute-start(bf16[512,256]{1,0:T(8,128)(2,1)S(1)} %add_convert_fusion.own_ref), channel_id=1, source_target_pairs={{0,8},{4,12},{8,0},{12,4},{16,24},{20,28},{24,16},{28,20},{1,9},{5... | collective-permute-start | bytes 786440 | tf_op jit(solution)/shard_map/ppermute | solution.py:351
  101.7 14.4 %collective-permute-start.28 = (bf16[1024,256]{1,0:T(8,128)(2,1)S(1)}, bf16[1024,256]{1,0:T(8,128)(2,1)S(1)}, u32[]{:S(2)}, u32[]{:S(2)}) collective-permute-start(bf16[1024,256]{1,0:T(8,128)(2,1)S(1)} %join_halves.8.rest_3_), channel_id=1, source_target_pairs={{0,4},{4,0},{8,12},{12,8},{16,20},{20,16},{24,28},{28,24},{1,5},{5... | collective-permute-start | bytes 1572872 | tf_op jit(solution)/shard_map/ppermute | solution.py:351
  108.1 13.6 %collective-permute-start.31 = (bf16[1024,256]{1,0:T(8,128)(2,1)S(1)}, bf16[1024,256]{1,0:T(8,128)(2,1)S(1)}, u32[]{:S(2)}, u32[]{:S(2)}) collective-permute-start(bf16[1024,256]{1,0:T(8,128)(2,1)S(1)} %join_halves.9.rest_4_), channel_id=1, source_target_pairs={{0,4},{4,0},{8,12},{12,8},{16,20},{20,16},{24,28},{28,24},{1,5},{5... | collective-permute-start | bytes 1572872 | tf_op jit(solution)/shard_map/ppermute | solution.py:351
  109.2 7.0 %collective-permute-start.27 = (bf16[512,256]{1,0:T(8,128)(2,1)S(1)}, bf16[512,256]{1,0:T(8,128)(2,1)S(1)}, u32[]{:S(2)}, u32[]{:S(2)}) collective-permute-start(bf16[512,256]{1,0:T(8,128)(2,1)S(1)} %dynamic-slice_select_fusion), channel_id=1, source_target_pairs={{0,2},{4,6},{8,10},{12,14},{17,19},{21,23},{25,27},{29,31}} | collective-permute-start | bytes 786440 | tf_op jit(solution)/shard_map/ppermute | solution.py:574
  112.7 4.9 %collective-permute-start.30 = (bf16[512,768]{1,0:T(8,128)(2,1)S(1)}, bf16[512,768]{1,0:T(8,128)(2,1)S(1)}, u32[]{:S(2)}, u32[]{:S(2)}) collective-permute-start(bf16[512,768]{1,0:T(8,128)(2,1)S(1)} %add.97), channel_id=1, source_target_pairs={{0,1},{2,3},{4,5},{6,7},{8,9},{10,11},{12,13},{14,15},{17,16},{19,... | collective-permute-start | bytes 2359304 | tf_op jit(solution)/shard_map/ppermute | solution.py:574
  116.2 3.2 %collective-permute-start.29 = (bf16[512,256]{1,0:T(8,128)(2,1)S(1)}, bf16[512,256]{1,0:T(8,128)(2,1)S(1)}, u32[]{:S(2)}, u32[]{:S(2)}) collective-permute-start(bf16[512,256]{1,0:T(8,128)(2,1)S(1)} %add.98), channel_id=1, source_target_pairs={{0,1},{2,3},{4,5},{6,7},{8,9},{10,11},{12,13},{14,15},{17,16},{19,... | collective-permute-start | bytes 786440 | tf_op jit(solution)/shard_map/ppermute | solution.py:574
  (14 other events, 51.6 us)

commit v5 on v4

--- a/solution.py
+++ b/solution.py
@@ -304,15 +304,26 @@
     for p in range(4):
         rows = pl.ds(pl.multiple_of(order_ref[p] * quarter, quarter), quarter)
         stores.append(pltpu.make_async_copy(held.at[p], out_ref.at[rows], sems.at[p]))
+    eighth = quarter // 2
     for p in range(4):
-        held[p] = slab_ref[p]
-        for g, side, half, begin, end, piece, at in places:
-            if 2 * half + side == p:
-                held[p, begin:end, :] -= jnp.dot(
-                    pieces[piece][at : at + end - begin, :],
-                    factor_ref[ends[g] : ends[g + 1], :],
-                    preferred_element_type=f32,
+        for first in (0, eighth):
+            parts = []
+            for g in range(len(widths)):
+                for group, side, half, begin, end, piece, at in places:
+                    if group == g and 2 * half + side == p and begin <= first < end:
+                        start = at + first - begin
+                        parts.append(pieces[piece][start : start + eighth, :])
+            rows = slice(first, first + eighth)
+            if all(width % LANES == 0 for width in widths):
+                held[p, rows, :] = slab_ref[p, rows, :] - jnp.dot(
+                    jnp.concatenate(parts, axis=1), factor_ref[...], preferred_element_type=f32
                 )
+            else:
+                held[p, rows, :] = slab_ref[p, rows, :]
+                for g, part in enumerate(parts):
+                    held[p, rows, :] -= jnp.dot(
+                        part, factor_ref[ends[g] : ends[g + 1], :], preferred_element_type=f32
+                    )
         stores[p].start()
     for store in stores:
         store.wait()

time: 126 us -> 126 us (level)
  no operation moved by 1% of the time
where the time goes in v5:
time: 126 us
  starting transfers between devices  42.1 us (33%)
  waiting for transfers between devices  41.1 us (33%)
  Pallas kernels  28.7 us (23%)
  local copies, waits for them, and re-layouts  6.94 us (6%)
  other arithmetic  6.29 us (5%)
    ppermute x25, waiting for transfers between devices, body(): lax.ppermute(value.astype(bf16), 'scen', [(i, i ^ mask) for i in range(sc...  41.1 us
    ppermute x25, starting transfers between devices, body(): lax.ppermute(value.astype(bf16), 'scen', [(i, i ^ mask) for i in range(sc...  31.2 us
    ppermute x4, starting transfers between devices, body(): trailing[k] = (rows, lax.ppermute(rows, ('scen', 'row'), spread[t]))  7.9 us
    unnamed x28, local copies, waits for them, and re-layouts  6.83 us
    pallas_call x2, Pallas kernels, scaled_quarters(): pl.pallas_call(functools.partial(scale_kernel, positions, parts), in_spec...  6.39 us
    pallas_call x5, Pallas kernels, piece_sum(): pl.pallas_call(functools.partial(sum_kernel, runs), in_specs=[pl.BlockSpe...  5.61 us
    pallas_call x4, Pallas kernels, piece_to_send(): pl.pallas_call(functools.partial(send_kernel, runs), in_specs=[IN_VMEM] *...  4.59 us
    pallas_call x1, Pallas kernels, first_step(): pl.pallas_call(functools.partial(first_kernel, parts), grid=(1,), in_spec...  4.57 us
  transfers between devices with their start and end apart: 32, of which 15 were waited for; matrix products, arithmetic and copies ran while one was open for 5% of the time, Pallas kernels for 16%

profile of v5, /device:TPU:0, one launch (start us, length us, event | category | flops | bytes accessed | tf_op | source)
XLA Modules:
  0.0 125.8 jit_solution(17433913278141659183)
XLA Ops:
  0.6 4.6 %first_step.1 = (f32[16,128]{1,0:T(8,128)}, bf16[256,2048]{1,0:T(8,128)(2,1)}, bf16[512,2048]{1,0:T(8,128)(2,1)}, bf16[512,256]{1,0:T(8,128)(2,1)}) custom-call(s32[1]{0:T(128)} %bitcast.5.place_ref, s32[8]{0:T(128)} %counts_ref.1, s32[4]{0:T(128)} %pad_add_fusion.1.order_ref, s32[16,128]{1,0:T(8,128)} %index_ref.1, f32[32,128]{1,0:T(8,128)} %bitcast.19, ...), custom_call_target="tpu_custom_call" | custom-call | flops 26639998976 | bytes 53280000 | tf_op jit(solution)/shard_map/first_step/pallas_call | solution.py:93
  5.2 3.0 %collective-permute-start.4 = (bf16[256,2048]{1,0:T(8,128)(2,1)}, bf16[256,2048]{1,0:T(8,128)(2,1)S(1)}, u32[]{:S(2)}, u32[]{:S(2)}) collective-permute-start(bf16[256,2048]{1,0:T(8,128)(2,1)} %get-tuple-element.82.refs_2_), channel_id=1, source_target_pairs={{0,2},{1,3},{2,0},{3,1},{4,6},{5,7},{6,4},{7,5},{8,10},{9,11},{10,... | collective-permute-start | bytes 3145736 | tf_op jit(solution)/shard_map/ppermute | solution.py:365
  8.2 1.5 %collective-permute-start.1 = (bf16[512,256]{1,0:T(8,128)(2,1)}, bf16[512,256]{1,0:T(8,128)(2,1)S(1)}, u32[]{:S(2)}, u32[]{:S(2)}) collective-permute-start(bf16[512,256]{1,0:T(8,128)(2,1)} %get-tuple-element.87), channel_id=1, source_target_pairs={{0,4},{4,0},{8,12},{12,8},{16,20},{20,16},{24,28},{28,24},{1,5},{5... | collective-permute-start | bytes 786440 | tf_op jit(solution)/shard_map/ppermute | solution.py:362
  10.4 2.2 %scaled_quarters.2.refs_1_ = bf16[512,2048]{1,0:T(8,128)(2,1)S(1)} custom-call(s32[4]{0:T(128)S(1)} %copy-done.4, bf16[16,2048,128]{2,1,0:T(8,128)(2,1)} %border_ref.5, f32[16,128]{1,0:T(8,128)S(1)} %copy-done.11), custom_call_target="tpu_custom_call" | custom-call | flops 26639998976 | bytes 53280000 | tf_op jit(solution)/shard_map/scaled_quarters/pallas_call | solution.py:140
  13.9 1.6 %copy-done.6 = bf16[512,2048]{1,0:T(8,128)(2,1)S(1)} copy-done((bf16[512,2048]{1,0:T(8,128)(2,1)S(1)}, bf16[512,2048]{1,0:T(8,128)(2,1)}, u32[]{:S(2)}) %copy-start.6) | copy-done | bytes 2097176
  15.5 1.6 %copy-done.9 = bf16[512,2048]{1,0:T(8,128)(2,1)S(1)} copy-done((bf16[512,2048]{1,0:T(8,128)(2,1)S(1)}, bf16[512,2048]{1,0:T(8,128)(2,1)}, u32[]{:S(2)}) %copy-start.9) | copy-done | bytes 2097176
  18.8 4.2 %scaled_quarters.3 = (bf16[512,2048]{1,0:T(8,128)(2,1)S(1)}, bf16[512,2048]{1,0:T(8,128)(2,1)}) custom-call(s32[4]{0:T(128)S(1)} %copy-done.4, bf16[16,2048,128]{2,1,0:T(8,128)(2,1)} %border_ref.5, f32[16,128]{1,0:T(8,128)S(1)} %copy-done.12), custom_call_target="tpu_custom_call" | custom-call | flops 26639998976 | bytes 53280000 | tf_op jit(solution)/shard_map/scaled_quarters/pallas_call | solution.py:140
  23.0 1.6 %copy-done = bf16[512,2048]{1,0:T(8,128)(2,1)S(1)} copy-done((bf16[512,2048]{1,0:T(8,128)(2,1)S(1)}, bf16[512,2048]{1,0:T(8,128)(2,1)}, u32[]{:S(2)}) %copy-start) | copy-done | bytes 2097176
  25.4 1.6 %collective-permute-start.2 = (bf16[256,256]{1,0:T(8,128)(2,1)S(1)}, bf16[256,256]{1,0:T(8,128)(2,1)S(1)}, u32[]{:S(2)}, u32[]{:S(2)}) collective-permute-start(bf16[256,256]{1,0:T(8,128)(2,1)S(1)} %get-tuple-element.90), channel_id=1, source_target_pairs={{0,8},{4,12},{8,0},{12,4},{16,24},{20,28},{24,16},{28,20},{1,9},{5... | collective-permute-start | bytes 393224 | tf_op jit(solution)/shard_map/ppermute | solution.py:362
  28.0 1.6 %collective-permute-start.7 = (bf16[768,256]{1,0:T(8,128)(2,1)S(1)}, bf16[768,256]{1,0:T(8,128)(2,1)S(1)}, u32[]{:S(2)}, u32[]{:S(2)}) collective-permute-start(bf16[768,256]{1,0:T(8,128)(2,1)S(1)} %piece_to_send.5), channel_id=1, source_target_pairs={{0,4},{4,0},{8,12},{12,8},{16,20},{20,16},{24,28},{28,24},{1,5},{5... | collective-permute-start | bytes 1179656 | tf_op jit(solution)/shard_map/ppermute | solution.py:362
  30.8 2.6 %collective-permute-start.3 = (bf16[256,256]{1,0:T(8,128)(2,1)S(1)}, bf16[256,256]{1,0:T(8,128)(2,1)S(1)}, u32[]{:S(2)}, u32[]{:S(2)}) collective-permute-start(bf16[256,256]{1,0:T(8,128)(2,1)S(1)} %get-tuple-element.159), channel_id=1, source_target_pairs={{0,16},{4,20},{8,24},{12,28},{16,0},{20,4},{24,8},{28,12},{1,17},{... | collective-permute-start | bytes 393224 | tf_op jit(solution)/shard_map/ppermute | solution.py:362
  34.5 1.6 %collective-permute-start.8 = (bf16[384,256]{1,0:T(8,128)(2,1)S(1)}, bf16[384,256]{1,0:T(8,128)(2,1)S(1)}, u32[]{:S(2)}, u32[]{:S(2)}) collective-permute-start(bf16[384,256]{1,0:T(8,128)(2,1)S(1)} %get-tuple-element.96), channel_id=1, source_target_pairs={{0,8},{4,12},{8,0},{12,4},{16,24},{20,28},{24,16},{28,20},{1,9},{5... | collective-permute-start | bytes 589832 | tf_op jit(solution)/shard_map/ppermute | solution.py:362
  39.9 3.0 %collective-permute-done.8 = bf16[384,256]{1,0:T(8,128)(2,1)S(1)} collective-permute-done((bf16[384,256]{1,0:T(8,128)(2,1)S(1)}, bf16[384,256]{1,0:T(8,128)(2,1)S(1)}, u32[]{:S(2)}, u32[]{:S(2)}) %collective-permute-start.8) | collective-permute-done | bytes 196640 | tf_op jit(solution)/shard_map/ppermute | solution.py:362
  44.4 1.5 %collective-permute-start.13 = (bf16[1024,256]{1,0:T(8,128)(2,1)S(1)}, bf16[1024,256]{1,0:T(8,128)(2,1)S(1)}, u32[]{:S(2)}, u32[]{:S(2)}) collective-permute-start(bf16[1024,256]{1,0:T(8,128)(2,1)S(1)} %piece_to_send.6), channel_id=1, source_target_pairs={{0,4},{4,0},{8,12},{12,8},{16,20},{20,16},{24,28},{28,24},{1,5},{5... | collective-permute-start | bytes 1572872 | tf_op jit(solution)/shard_map/ppermute | solution.py:362
  45.9 1.7 %collective-permute-start.9 = (bf16[384,256]{1,0:T(8,128)(2,1)S(1)}, bf16[384,256]{1,0:T(8,128)(2,1)S(1)}, u32[]{:S(2)}, u32[]{:S(2)}) collective-permute-start(bf16[384,256]{1,0:T(8,128)(2,1)S(1)} %get-tuple-element.157), channel_id=1, source_target_pairs={{0,16},{4,20},{8,24},{12,28},{16,0},{20,4},{24,8},{28,12},{1,17},{... | collective-permute-start | bytes 589832 | tf_op jit(solution)/shard_map/ppermute | solution.py:362
  47.6 4.7 %collective-permute-done.11 = bf16[384,256]{1,0:T(8,128)(2,1)S(1)} collective-permute-done((bf16[384,256]{1,0:T(8,128)(2,1)S(1)}, bf16[384,256]{1,0:T(8,128)(2,1)S(1)}, u32[]{:S(2)}, u32[]{:S(2)}) %collective-permute-start.11) | collective-permute-done | bytes 196640 | tf_op jit(solution)/shard_map/ppermute | solution.py:362
  53.7 2.2 %collective-permute-done.9 = bf16[384,256]{1,0:T(8,128)(2,1)S(1)} collective-permute-done((bf16[384,256]{1,0:T(8,128)(2,1)S(1)}, bf16[384,256]{1,0:T(8,128)(2,1)S(1)}, u32[]{:S(2)}, u32[]{:S(2)}) %collective-permute-start.9) | collective-permute-done | bytes 196640 | tf_op jit(solution)/shard_map/ppermute | solution.py:362
  56.0 2.8 %collective-permute-start.14 = (bf16[384,256]{1,0:T(8,128)(2,1)S(1)}, bf16[384,256]{1,0:T(8,128)(2,1)S(1)}, u32[]{:S(2)}, u32[]{:S(2)}) collective-permute-start(bf16[384,256]{1,0:T(8,128)(2,1)S(1)} %get-tuple-element.155), channel_id=1, source_target_pairs={{0,16},{4,20},{8,24},{12,28},{16,0},{20,4},{24,8},{28,12},{1,17},{... | collective-permute-start | bytes 589832 | tf_op jit(solution)/shard_map/ppermute | solution.py:362
  62.4 4.5 %collective-permute-done.12.got_ref = bf16[384,256]{1,0:T(8,128)(2,1)S(1)} collective-permute-done((bf16[384,256]{1,0:T(8,128)(2,1)S(1)}, bf16[384,256]{1,0:T(8,128)(2,1)S(1)}, u32[]{:S(2)}, u32[]{:S(2)}) %collective-permute-start.12) | collective-permute-done | bytes 196640 | tf_op jit(solution)/shard_map/ppermute | solution.py:362
  68.0 4.2 %collective-permute-done.17 = bf16[512,256]{1,0:T(8,128)(2,1)S(1)} collective-permute-done((bf16[512,256]{1,0:T(8,128)(2,1)S(1)}, bf16[512,256]{1,0:T(8,128)(2,1)S(1)}, u32[]{:S(2)}, u32[]{:S(2)}) %collective-permute-start.17) | collective-permute-done | bytes 262176 | tf_op jit(solution)/shard_map/ppermute | solution.py:362
  74.4 2.1 %collective-permute-start.19 = (bf16[512,256]{1,0:T(8,128)(2,1)S(1)}, bf16[512,256]{1,0:T(8,128)(2,1)S(1)}, u32[]{:S(2)}, u32[]{:S(2)}) collective-permute-start(bf16[512,256]{1,0:T(8,128)(2,1)S(1)} %get-tuple-element.124), channel_id=1, source_target_pairs={{0,8},{4,12},{8,0},{12,4},{16,24},{20,28},{24,16},{28,20},{1,9},{5... | collective-permute-start | bytes 786440 | tf_op jit(solution)/shard_map/ppermute | solution.py:362
  79.1 4.4 %collective-permute-done.19 = bf16[512,256]{1,0:T(8,128)(2,1)S(1)} collective-permute-done((bf16[512,256]{1,0:T(8,128)(2,1)S(1)}, bf16[512,256]{1,0:T(8,128)(2,1)S(1)}, u32[]{:S(2)}, u32[]{:S(2)}) %collective-permute-start.19) | collective-permute-done | bytes 262176 | tf_op jit(solution)/shard_map/ppermute | solution.py:362
  84.4 3.7 %collective-permute-done.18 = bf16[512,256]{1,0:T(8,128)(2,1)S(1)} collective-permute-done((bf16[512,256]{1,0:T(8,128)(2,1)S(1)}, bf16[512,256]{1,0:T(8,128)(2,1)S(1)}, u32[]{:S(2)}, u32[]{:S(2)}) %collective-permute-start.18) | collective-permute-done | bytes 262176 | tf_op jit(solution)/shard_map/ppermute | solution.py:362
  89.3 1.6 %collective-permute-start.25 = (bf16[768,256]{1,0:T(8,128)(2,1)S(1)}, bf16[768,256]{1,0:T(8,128)(2,1)S(1)}, u32[]{:S(2)}, u32[]{:S(2)}) collective-permute-start(bf16[768,256]{1,0:T(8,128)(2,1)S(1)} %join_halves.7.rest_2_), channel_id=1, source_target_pairs={{0,4},{4,0},{8,12},{12,8},{16,20},{20,16},{24,28},{28,24},{1,5},{5... | collective-permute-start | bytes 1179656 | tf_op jit(solution)/shard_map/ppermute | solution.py:362
  92.5 3.7 %collective-permute-done.21.got_ref = bf16[512,256]{1,0:T(8,128)(2,1)S(1)} collective-permute-done((bf16[512,256]{1,0:T(8,128)(2,1)S(1)}, bf16[512,256]{1,0:T(8,128)(2,1)S(1)}, u32[]{:S(2)}, u32[]{:S(2)}) %collective-permute-start.21) | collective-permute-done | bytes 262176 | tf_op jit(solution)/shard_map/ppermute | solution.py:362
  97.3 3.3 %collective-permute-start.23 = (bf16[512,768]{1,0:T(8,128)(2,1)}, bf16[512,768]{1,0:T(8,128)(2,1)}, u32[]{:S(2)}, u32[]{:S(2)}) collective-permute-start(bf16[512,768]{1,0:T(8,128)(2,1)} %maximum_select_fusion), channel_id=1, source_target_pairs={{0,2},{4,6},{8,10},{12,14},{17,19},{21,23},{25,27},{29,31}} | collective-permute-start | bytes 2359304 | tf_op jit(solution)/shard_map/ppermute | solution.py:585
  101.7 2.4 %collective-permute-start.28 = (bf16[1024,256]{1,0:T(8,128)(2,1)S(1)}, bf16[1024,256]{1,0:T(8,128)(2,1)S(1)}, u32[]{:S(2)}, u32[]{:S(2)}) collective-permute-start(bf16[1024,256]{1,0:T(8,128)(2,1)S(1)} %join_halves.8.rest_3_), channel_id=1, source_target_pairs={{0,4},{4,0},{8,12},{12,8},{16,20},{20,16},{24,28},{28,24},{1,5},{5... | collective-permute-start | bytes 1572872 | tf_op jit(solution)/shard_map/ppermute | solution.py:362
  104.1 4.0 %collective-permute-done.26.got_ref = bf16[512,256]{1,0:T(8,128)(2,1)S(1)} collective-permute-done((bf16[512,256]{1,0:T(8,128)(2,1)S(1)}, bf16[512,256]{1,0:T(8,128)(2,1)S(1)}, u32[]{:S(2)}, u32[]{:S(2)}) %collective-permute-start.26) | collective-permute-done | bytes 262176 | tf_op jit(solution)/shard_map/ppermute | solution.py:362
  109.2 2.0 %collective-permute-start.27 = (bf16[512,256]{1,0:T(8,128)(2,1)S(1)}, bf16[512,256]{1,0:T(8,128)(2,1)S(1)}, u32[]{:S(2)}, u32[]{:S(2)}) collective-permute-start(bf16[512,256]{1,0:T(8,128)(2,1)S(1)} %dynamic-slice_select_fusion), channel_id=1, source_target_pairs={{0,2},{4,6},{8,10},{12,14},{17,19},{21,23},{25,27},{29,31}} | collective-permute-start | bytes 786440 | tf_op jit(solution)/shard_map/ppermute | solution.py:585
  111.1 1.6 %add.97 = bf16[512,768]{1,0:T(8,128)(2,1)S(1)} add(bf16[512,768]{1,0:T(8,128)(2,1)} %maximum_select_fusion, bf16[512,768]{1,0:T(8,128)(2,1)} %collective-permute-done.23) | non-fusion elementwise | flops 393216 | bytes 2359296 | tf_op jit(solution)/shard_map/add | solution.py:581
  117.8 1.6 %factor.2.refs_3_ = f32[1024,512]{1,0:T(8,128)S(1)} custom-call(s32[2,4]{1,0:T(2,128)S(1)} %pad_add_fusion.refs_0_, bf16[1024,1024]{1,0:T(8,128)(2,1)S(1)} %copy-done.2, bf16[512,768]{1,0:T(8,128)(2,1)S(1)} %add.99.refs_2_), custom_call_target="tpu_custom_call" | custom-call | flops 920000000 | bytes 1840000 | tf_op jit(solution)/shard_map/factor/pallas_call | solution.py:287
  121.7 3.9 %update.1 = f32[2048,512]{1,0:T(8,128)} custom-call(s32[4]{0:T(128)S(1)} %copy-done.4, f32[4,512,512]{2,1,0:T(8,128)S(1)} %held_slab.1.slab_ref, bf16[1024,512]{1,0:T(8,128)(2,1)S(1)} %factor.3.factor_ref, bf16[512,256]{1,0:T(8,128)(2,1)S(1)} %join_halves.5.rest_0_, bf16[768,256]{1,0:T(8,128)(2,1)S(1)} %join_halves.6.rest_1_, ...), custom_call_target="tpu_custom_call" | custom-call | flops 920000000 | bytes 1840000 | tf_op jit(solution)/shard_map/update/pallas_call | solution.py:334
  (105 shorter events, 38.7 us)
Async XLA Ops:
  5.2 31.0 %collective-permute-start.4 = (bf16[256,2048]{1,0:T(8,128)(2,1)}, bf16[256,2048]{1,0:T(8,128)(2,1)S(1)}, u32[]{:S(2)}, u32[]{:S(2)}) collective-permute-start(bf16[256,2048]{1,0:T(8,128)(2,1)} %get-tuple-element.82.refs_2_), channel_id=1, source_target_pairs={{0,2},{1,3},{2,0},{3,1},{4,6},{5,7},{6,4},{7,5},{8,10},{9,11},{10,... | collective-permute-start | bytes 3145736 | tf_op jit(solution)/shard_map/ppermute | solution.py:365
  8.2 5.7 %collective-permute-start = (bf16[256,2048]{1,0:T(8,128)(2,1)}, bf16[256,2048]{1,0:T(8,128)(2,1)S(1)}, u32[]{:S(2)}, u32[]{:S(2)}) collective-permute-start(bf16[256,2048]{1,0:T(8,128)(2,1)} %get-tuple-element.82.refs_2_), channel_id=1, source_target_pairs={{0,1},{1,0},{2,3},{3,2},{4,5},{5,4},{6,7},{7,6},{8,9},{9,8},{10,11... | collective-permute-start | bytes 3145736 | tf_op jit(solution)/shard_map/ppermute | solution.py:365
  8.2 14.8 %collective-permute-start.1 = (bf16[512,256]{1,0:T(8,128)(2,1)}, bf16[512,256]{1,0:T(8,128)(2,1)S(1)}, u32[]{:S(2)}, u32[]{:S(2)}) collective-permute-start(bf16[512,256]{1,0:T(8,128)(2,1)} %get-tuple-element.87), channel_id=1, source_target_pairs={{0,4},{4,0},{8,12},{12,8},{16,20},{20,16},{24,28},{28,24},{1,5},{5... | collective-permute-start | bytes 786440 | tf_op jit(solution)/shard_map/ppermute | solution.py:362
  18.1 15.3 %collective-permute-start.5 = (bf16[768,256]{1,0:T(8,128)(2,1)S(1)}, bf16[768,256]{1,0:T(8,128)(2,1)S(1)}, u32[]{:S(2)}, u32[]{:S(2)}) collective-permute-start(bf16[768,256]{1,0:T(8,128)(2,1)S(1)} %piece_to_send.4), channel_id=1, source_target_pairs={{0,4},{4,0},{8,12},{12,8},{16,20},{20,16},{24,28},{28,24},{1,5},{5... | collective-permute-start | bytes 1179656 | tf_op jit(solution)/shard_map/ppermute | solution.py:362
  25.4 5.4 %collective-permute-start.2 = (bf16[256,256]{1,0:T(8,128)(2,1)S(1)}, bf16[256,256]{1,0:T(8,128)(2,1)S(1)}, u32[]{:S(2)}, u32[]{:S(2)}) collective-permute-start(bf16[256,256]{1,0:T(8,128)(2,1)S(1)} %get-tuple-element.90), channel_id=1, source_target_pairs={{0,8},{4,12},{8,0},{12,4},{16,24},{20,28},{24,16},{28,20},{1,9},{5... | collective-permute-start | bytes 393224 | tf_op jit(solution)/shard_map/ppermute | solution.py:362
  28.0 14.9 %collective-permute-start.7 = (bf16[768,256]{1,0:T(8,128)(2,1)S(1)}, bf16[768,256]{1,0:T(8,128)(2,1)S(1)}, u32[]{:S(2)}, u32[]{:S(2)}) collective-permute-start(bf16[768,256]{1,0:T(8,128)(2,1)S(1)} %piece_to_send.5), channel_id=1, source_target_pairs={{0,4},{4,0},{8,12},{12,8},{16,20},{20,16},{24,28},{28,24},{1,5},{5... | collective-permute-start | bytes 1179656 | tf_op jit(solution)/shard_map/ppermute | solution.py:362
  30.8 8.1 %collective-permute-start.3 = (bf16[256,256]{1,0:T(8,128)(2,1)S(1)}, bf16[256,256]{1,0:T(8,128)(2,1)S(1)}, u32[]{:S(2)}, u32[]{:S(2)}) collective-permute-start(bf16[256,256]{1,0:T(8,128)(2,1)S(1)} %get-tuple-element.159), channel_id=1, source_target_pairs={{0,16},{4,20},{8,24},{12,28},{16,0},{20,4},{24,8},{28,12},{1,17},{... | collective-permute-start | bytes 393224 | tf_op jit(solution)/shard_map/ppermute | solution.py:362
  34.5 8.3 %collective-permute-start.8 = (bf16[384,256]{1,0:T(8,128)(2,1)S(1)}, bf16[384,256]{1,0:T(8,128)(2,1)S(1)}, u32[]{:S(2)}, u32[]{:S(2)}) collective-permute-start(bf16[384,256]{1,0:T(8,128)(2,1)S(1)} %get-tuple-element.96), channel_id=1, source_target_pairs={{0,8},{4,12},{8,0},{12,4},{16,24},{20,28},{24,16},{28,20},{1,9},{5... | collective-permute-start | bytes 589832 | tf_op jit(solution)/shard_map/ppermute | solution.py:362
  36.2 16.2 %collective-permute-start.10 = (bf16[256,2048]{1,0:T(8,128)(2,1)S(1)}, bf16[256,2048]{1,0:T(8,128)(2,1)S(1)}, u32[]{:S(2)}, u32[]{:S(2)}) collective-permute-start(bf16[256,2048]{1,0:T(8,128)(2,1)S(1)} %collective-permute-done.4.refs_2_), channel_id=1, source_target_pairs={{0,1},{1,0},{2,3},{3,2},{4,5},{5,4},{6,7},{7,6},{8,9},{9,8},{10,11... | collective-permute-start | bytes 3145736 | tf_op jit(solution)/shard_map/ppermute | solution.py:365
  39.0 6.9 %collective-permute-start.6 = (bf16[256,256]{1,0:T(8,128)(2,1)S(1)}, bf16[256,256]{1,0:T(8,128)(2,1)S(1)}, u32[]{:S(2)}, u32[]{:S(2)}) collective-permute-start(bf16[256,256]{1,0:T(8,128)(2,1)S(1)} %add_convert_fusion.4.own_ref), channel_id=1, source_target_pairs={{0,8},{4,12},{8,0},{12,4},{16,24},{20,28},{24,16},{28,20},{1,9},{5... | collective-permute-start | bytes 393224 | tf_op jit(solution)/shard_map/ppermute | solution.py:362
  44.0 8.3 %collective-permute-start.11 = (bf16[384,256]{1,0:T(8,128)(2,1)S(1)}, bf16[384,256]{1,0:T(8,128)(2,1)S(1)}, u32[]{:S(2)}, u32[]{:S(2)}) collective-permute-start(bf16[384,256]{1,0:T(8,128)(2,1)S(1)} %get-tuple-element.105), channel_id=1, source_target_pairs={{0,8},{4,12},{8,0},{12,4},{16,24},{20,28},{24,16},{28,20},{1,9},{5... | collective-permute-start | bytes 589832 | tf_op jit(solution)/shard_map/ppermute | solution.py:362
  44.4 16.5 %collective-permute-start.13 = (bf16[1024,256]{1,0:T(8,128)(2,1)S(1)}, bf16[1024,256]{1,0:T(8,128)(2,1)S(1)}, u32[]{:S(2)}, u32[]{:S(2)}) collective-permute-start(bf16[1024,256]{1,0:T(8,128)(2,1)S(1)} %piece_to_send.6), channel_id=1, source_target_pairs={{0,4},{4,0},{8,12},{12,8},{16,20},{20,16},{24,28},{28,24},{1,5},{5... | collective-permute-start | bytes 1572872 | tf_op jit(solution)/shard_map/ppermute | solution.py:362
  45.9 10.0 %collective-permute-start.9 = (bf16[384,256]{1,0:T(8,128)(2,1)S(1)}, bf16[384,256]{1,0:T(8,128)(2,1)S(1)}, u32[]{:S(2)}, u32[]{:S(2)}) collective-permute-start(bf16[384,256]{1,0:T(8,128)(2,1)S(1)} %get-tuple-element.157), channel_id=1, source_target_pairs={{0,16},{4,20},{8,24},{12,28},{16,0},{20,4},{24,8},{28,12},{1,17},{... | collective-permute-start | bytes 589832 | tf_op jit(solution)/shard_map/ppermute | solution.py:362
  55.9 10.9 %collective-permute-start.12 = (bf16[384,256]{1,0:T(8,128)(2,1)S(1)}, bf16[384,256]{1,0:T(8,128)(2,1)S(1)}, u32[]{:S(2)}, u32[]{:S(2)}) collective-permute-start(bf16[384,256]{1,0:T(8,128)(2,1)S(1)} %add_convert_fusion.3.own_ref), channel_id=1, source_target_pairs={{0,8},{4,12},{8,0},{12,4},{16,24},{20,28},{24,16},{28,20},{1,9},{5... | collective-permute-start | bytes 589832 | tf_op jit(solution)/shard_map/ppermute | solution.py:362
  56.0 10.9 %collective-permute-start.14 = (bf16[384,256]{1,0:T(8,128)(2,1)S(1)}, bf16[384,256]{1,0:T(8,128)(2,1)S(1)}, u32[]{:S(2)}, u32[]{:S(2)}) collective-permute-start(bf16[384,256]{1,0:T(8,128)(2,1)S(1)} %get-tuple-element.155), channel_id=1, source_target_pairs={{0,16},{4,20},{8,24},{12,28},{16,0},{20,4},{24,8},{28,12},{1,17},{... | collective-permute-start | bytes 589832 | tf_op jit(solution)/shard_map/ppermute | solution.py:362
  58.8 20.3 %collective-permute-start.20 = (bf16[512,256]{1,0:T(8,128)(2,1)S(1)}, bf16[512,256]{1,0:T(8,128)(2,1)S(1)}, u32[]{:S(2)}, u32[]{:S(2)}) collective-permute-start(bf16[512,256]{1,0:T(8,128)(2,1)S(1)} %join_halves.5.rest_0_), channel_id=1, source_target_pairs={{0,4},{4,0},{8,12},{12,8},{16,20},{20,16},{24,28},{28,24},{1,5},{5... | collective-permute-start | bytes 786440 | tf_op jit(solution)/shard_map/ppermute | solution.py:362
  60.2 12.9 %collective-permute-start.16 = (bf16[1024,256]{1,0:T(8,128)(2,1)S(1)}, bf16[1024,256]{1,0:T(8,128)(2,1)S(1)}, u32[]{:S(2)}, u32[]{:S(2)}) collective-permute-start(bf16[1024,256]{1,0:T(8,128)(2,1)S(1)} %piece_to_send.7), channel_id=1, source_target_pairs={{0,4},{4,0},{8,12},{12,8},{16,20},{20,16},{24,28},{28,24},{1,5},{5... | collective-permute-start | bytes 1572872 | tf_op jit(solution)/shard_map/ppermute | solution.py:362
  62.2 10.0 %collective-permute-start.17 = (bf16[512,256]{1,0:T(8,128)(2,1)S(1)}, bf16[512,256]{1,0:T(8,128)(2,1)S(1)}, u32[]{:S(2)}, u32[]{:S(2)}) collective-permute-start(bf16[512,256]{1,0:T(8,128)(2,1)S(1)} %get-tuple-element.115), channel_id=1, source_target_pairs={{0,8},{4,12},{8,0},{12,4},{16,24},{20,28},{24,16},{28,20},{1,9},{5... | collective-permute-start | bytes 786440 | tf_op jit(solution)/shard_map/ppermute | solution.py:362
  67.0 12.1 %collective-permute-start.15 = (bf16[384,256]{1,0:T(8,128)(2,1)S(1)}, bf16[384,256]{1,0:T(8,128)(2,1)S(1)}, u32[]{:S(2)}, u32[]{:S(2)}) collective-permute-start(bf16[384,256]{1,0:T(8,128)(2,1)S(1)} %add_convert_fusion.2.own_ref), channel_id=1, source_target_pairs={{0,8},{4,12},{8,0},{12,4},{16,24},{20,28},{24,16},{28,20},{1,9},{5... | collective-permute-start | bytes 589832 | tf_op jit(solution)/shard_map/ppermute | solution.py:362
  74.4 9.0 %collective-permute-start.19 = (bf16[512,256]{1,0:T(8,128)(2,1)S(1)}, bf16[512,256]{1,0:T(8,128)(2,1)S(1)}, u32[]{:S(2)}, u32[]{:S(2)}) collective-permute-start(bf16[512,256]{1,0:T(8,128)(2,1)S(1)} %get-tuple-element.124), channel_id=1, source_target_pairs={{0,8},{4,12},{8,0},{12,4},{16,24},{20,28},{24,16},{28,20},{1,9},{5... | collective-permute-start | bytes 786440 | tf_op jit(solution)/shard_map/ppermute | solution.py:362
  76.6 14.7 %collective-permute-start.22 = (bf16[768,256]{1,0:T(8,128)(2,1)S(1)}, bf16[768,256]{1,0:T(8,128)(2,1)S(1)}, u32[]{:S(2)}, u32[]{:S(2)}) collective-permute-start(bf16[768,256]{1,0:T(8,128)(2,1)S(1)} %join_halves.6.rest_1_), channel_id=1, source_target_pairs={{0,4},{4,0},{8,12},{12,8},{16,20},{20,16},{24,28},{28,24},{1,5},{5... | collective-permute-start | bytes 1179656 | tf_op jit(solution)/shard_map/ppermute | solution.py:362
  77.9 10.2 %collective-permute-start.18 = (bf16[512,256]{1,0:T(8,128)(2,1)S(1)}, bf16[512,256]{1,0:T(8,128)(2,1)S(1)}, u32[]{:S(2)}, u32[]{:S(2)}) collective-permute-start(bf16[512,256]{1,0:T(8,128)(2,1)S(1)} %get-tuple-element.153), channel_id=1, source_target_pairs={{0,16},{4,20},{8,24},{12,28},{16,0},{20,4},{24,8},{28,12},{1,17},{... | collective-permute-start | bytes 786440 | tf_op jit(solution)/shard_map/ppermute | solution.py:362
  88.2 8.0 %collective-permute-start.21 = (bf16[512,256]{1,0:T(8,128)(2,1)S(1)}, bf16[512,256]{1,0:T(8,128)(2,1)S(1)}, u32[]{:S(2)}, u32[]{:S(2)}) collective-permute-start(bf16[512,256]{1,0:T(8,128)(2,1)S(1)} %add_convert_fusion.1.own_ref), channel_id=1, source_target_pairs={{0,8},{4,12},{8,0},{12,4},{16,24},{20,28},{24,16},{28,20},{1,9},{5... | collective-permute-start | bytes 786440 | tf_op jit(solution)/shard_map/ppermute | solution.py:362
  89.3 11.3 %collective-permute-start.25 = (bf16[768,256]{1,0:T(8,128)(2,1)S(1)}, bf16[768,256]{1,0:T(8,128)(2,1)S(1)}, u32[]{:S(2)}, u32[]{:S(2)}) collective-permute-start(bf16[768,256]{1,0:T(8,128)(2,1)S(1)} %join_halves.7.rest_2_), channel_id=1, source_target_pairs={{0,4},{4,0},{8,12},{12,8},{16,20},{20,16},{24,28},{28,24},{1,5},{5... | collective-permute-start | bytes 1179656 | tf_op jit(solution)/shard_map/ppermute | solution.py:362
  91.3 10.3 %collective-permute-start.24 = (bf16[512,256]{1,0:T(8,128)(2,1)}, bf16[512,256]{1,0:T(8,128)(2,1)S(1)}, u32[]{:S(2)}, u32[]{:S(2)}) collective-permute-start(bf16[512,256]{1,0:T(8,128)(2,1)} %get-tuple-element.151), channel_id=1, source_target_pairs={{0,16},{4,20},{8,24},{12,28},{16,0},{20,4},{24,8},{28,12},{1,17},{... | collective-permute-start | bytes 786440 | tf_op jit(solution)/shard_map/ppermute | solution.py:362
  97.3 13.8 %collective-permute-start.23 = (bf16[512,768]{1,0:T(8,128)(2,1)}, bf16[512,768]{1,0:T(8,128)(2,1)}, u32[]{:S(2)}, u32[]{:S(2)}) collective-permute-start(bf16[512,768]{1,0:T(8,128)(2,1)} %maximum_select_fusion), channel_id=1, source_target_pairs={{0,2},{4,6},{8,10},{12,14},{17,19},{21,23},{25,27},{29,31}} | collective-permute-start | bytes 2359304 | tf_op jit(solution)/shard_map/ppermute | solution.py:585
  101.7 6.4 %collective-permute-start.26 = (bf16[512,256]{1,0:T(8,128)(2,1)S(1)}, bf16[512,256]{1,0:T(8,128)(2,1)S(1)}, u32[]{:S(2)}, u32[]{:S(2)}) collective-permute-start(bf16[512,256]{1,0:T(8,128)(2,1)S(1)} %add_convert_fusion.own_ref), channel_id=1, source_target_pairs={{0,8},{4,12},{8,0},{12,4},{16,24},{20,28},{24,16},{28,20},{1,9},{5... | collective-permute-start | bytes 786440 | tf_op jit(solution)/shard_map/ppermute | solution.py:362
  101.7 14.4 %collective-permute-start.28 = (bf16[1024,256]{1,0:T(8,128)(2,1)S(1)}, bf16[1024,256]{1,0:T(8,128)(2,1)S(1)}, u32[]{:S(2)}, u32[]{:S(2)}) collective-permute-start(bf16[1024,256]{1,0:T(8,128)(2,1)S(1)} %join_halves.8.rest_3_), channel_id=1, source_target_pairs={{0,4},{4,0},{8,12},{12,8},{16,20},{20,16},{24,28},{28,24},{1,5},{5... | collective-permute-start | bytes 1572872 | tf_op jit(solution)/shard_map/ppermute | solution.py:362
  108.1 13.6 %collective-permute-start.31 = (bf16[1024,256]{1,0:T(8,128)(2,1)S(1)}, bf16[1024,256]{1,0:T(8,128)(2,1)S(1)}, u32[]{:S(2)}, u32[]{:S(2)}) collective-permute-start(bf16[1024,256]{1,0:T(8,128)(2,1)S(1)} %join_halves.9.rest_4_), channel_id=1, source_target_pairs={{0,4},{4,0},{8,12},{12,8},{16,20},{20,16},{24,28},{28,24},{1,5},{5... | collective-permute-start | bytes 1572872 | tf_op jit(solution)/shard_map/ppermute | solution.py:362
  109.2 7.0 %collective-permute-start.27 = (bf16[512,256]{1,0:T(8,128)(2,1)S(1)}, bf16[512,256]{1,0:T(8,128)(2,1)S(1)}, u32[]{:S(2)}, u32[]{:S(2)}) collective-permute-start(bf16[512,256]{1,0:T(8,128)(2,1)S(1)} %dynamic-slice_select_fusion), channel_id=1, source_target_pairs={{0,2},{4,6},{8,10},{12,14},{17,19},{21,23},{25,27},{29,31}} | collective-permute-start | bytes 786440 | tf_op jit(solution)/shard_map/ppermute | solution.py:585
  112.7 4.9 %collective-permute-start.30 = (bf16[512,768]{1,0:T(8,128)(2,1)S(1)}, bf16[512,768]{1,0:T(8,128)(2,1)S(1)}, u32[]{:S(2)}, u32[]{:S(2)}) collective-permute-start(bf16[512,768]{1,0:T(8,128)(2,1)S(1)} %add.97), channel_id=1, source_target_pairs={{0,1},{2,3},{4,5},{6,7},{8,9},{10,11},{12,13},{14,15},{17,16},{19,... | collective-permute-start | bytes 2359304 | tf_op jit(solution)/shard_map/ppermute | solution.py:585
  116.2 3.2 %collective-permute-start.29 = (bf16[512,256]{1,0:T(8,128)(2,1)S(1)}, bf16[512,256]{1,0:T(8,128)(2,1)S(1)}, u32[]{:S(2)}, u32[]{:S(2)}) collective-permute-start(bf16[512,256]{1,0:T(8,128)(2,1)S(1)} %add.98), channel_id=1, source_target_pairs={{0,1},{2,3},{4,5},{6,7},{8,9},{10,11},{12,13},{14,15},{17,16},{19,... | collective-permute-start | bytes 786440 | tf_op jit(solution)/shard_map/ppermute | solution.py:585
  (14 other events, 51.6 us)
